TPU v7x, 32 devices: a whole 2x2x4 slice. The times are simulated.
32 devices in a mesh: req: 4 (over y, x), blk: 8 (over z, core).
Axes of the slice: x: 2, y: 2, z: 4, core: 2. Of those that a mesh axis runs over, the one named last changes fastest.
Arguments:
- new_states: bfloat16 [2048, 1024], P('req'), may hold values from -50 to 50
- encoder_out: bfloat16 [2048, 1024], P('req'), may hold values from -90 to 90
- cache_in: bfloat16 [4, 4096, 2048], P(None, 'blk', 'req'), may hold values from -90 to 90
- slot_order: int32 [4], replicated, may hold values from 0 to 3, each once
- new_lengths: int32 [4], replicated, may hold values from 1 to 512, 1280 in all
- cache_lengths: int32 [4], replicated, may hold values from 1 to 4096, 8192 in all
- enc_lengths: int32 [4], replicated, may hold values from 1 to 512, 1536 in all
- bucket_of: int32 [4608], replicated, may hold values from 0 to 31, as said below
- rel_bias: float32 [32, 16], replicated, may hold values from -4 to 4
- norm_gain: float32 [3, 1024], replicated, may hold values from 0.25 to 1.75
- self_q: bfloat16 [1024, 1024], P('req', 'blk'), may hold values from -0.09375 to 0.09375
- self_kv: bfloat16 [1024, 2, 1024], P('req', None, 'blk'), may hold values from -0.1875 to 0.1875
- self_out: bfloat16 [1024, 1024], P('blk', 'req'), may hold values from -0.1875 to 0.1875
- cross_q: bfloat16 [1024, 1024], P('req', 'blk'), may hold values from -0.09375 to 0.09375
- cross_kv: bfloat16 [1024, 2, 1024], P('req', None, 'blk'), may hold values from -0.1875 to 0.1875
- cross_out: bfloat16 [1024, 1024], P('blk', 'req'), may hold values from -0.1875 to 0.1875
- ff_in: bfloat16 [1024, 2, 2816], P('req', None, 'blk'), may hold values from -0.1875 to 0.1875
- ff_out: bfloat16 [2816, 1024], P('blk', 'req'), may hold values from -0.109375 to 0.109375
Outputs:
- layer_out: bfloat16 [2048, 1024], P('req')
- cache_out: bfloat16 [4, 4096, 2048], P('req', None, 'blk')
Inputs may be any that keep to these rules, and one draw needn't show every extreme that they name: Slot s holds request slot_order[s]; every request is held once. `new_lengths`: they sum to 1280 and the most is 512. `cache_lengths`: they sum to 8192 and the most is 4096. `enc_lengths`: they sum to 1536 and the most is 512. `bucket_of`: non-decreasing in the distance, 0 at distance 0 and 31 at distance 4608 - 1.
All inputs are finite; a program needn't handle non-finite values.
Results may differ from a plain program's by a relative error of at most 0.035.
Values may be sent and summed in bfloat16 or wider, within the bound.
No kernel may reach another device: no remote copies, remote signals or barrier semaphores. Data moves between devices by JAX's collectives and lax.ppermute only.
A program may use at most 128 MiB of HBM per device.

v0:
```python
import jax
import jax.numpy as jnp
from jax import lax
from jax.sharding import PartitionSpec as P

H = 16
HD = 64


EPSILON = 1e-06
NEG_FILL = -1e30


def rms_rows(row_block, gain):
    mean_square = jnp.mean(row_block * row_block, axis=-1, keepdims=True)
    return (row_block * lax.rsqrt(mean_square + EPSILON) * gain).astype(jnp.bfloat16)


def softmax_rows(scores):
    row_top = jnp.max(scores, axis=-1, keepdims=True)
    weights = jnp.exp(scores - row_top)
    return (weights / jnp.sum(weights, axis=-1, keepdims=True)).astype(jnp.bfloat16)


def pick_lengths(table, own_slots):
    matches = own_slots[:, None] == jnp.arange(table.shape[0], dtype=jnp.int32)[None, :]
    return jnp.sum(jnp.where(matches, table[None, :], 0), axis=1)


def shifted_bias(bias_dist, base, row_count, col_count):
    heads_here, span_len = bias_dist.shape
    line_len = row_count + col_count - 1
    steps = jnp.arange(line_len + 1, dtype=jnp.int32)
    line = bias_dist[:, jnp.clip(base + row_count - 1 - steps, 0, span_len - 1)]
    tiled = jnp.broadcast_to(line[:, None, :], (heads_here, row_count, line_len + 1))
    flat = tiled.reshape(heads_here, row_count * (line_len + 1))[:, : row_count * line_len]
    skewed = flat.reshape(heads_here, row_count, line_len)
    return skewed[:, :, row_count - 1 : row_count - 1 + col_count]


def row_total(left, weight):
    term = jnp.dot(left, weight, preferred_element_type=jnp.float32)
    return lax.psum(term.astype(jnp.bfloat16), "blk").astype(jnp.float32)


def cached_scores(queries, key_rows, first_col, old_len, bias_dist):
    col_ids = first_col + jnp.arange(key_rows.shape[0], dtype=jnp.int32)[None, :]
    scores = jnp.einsum("qhe,khe->hqk", queries, key_rows, preferred_element_type=jnp.float32)
    scores = scores + shifted_bias(
        bias_dist, old_len - first_col, queries.shape[0], key_rows.shape[0]
    )
    return jnp.where((col_ids < old_len)[None], scores, NEG_FILL)


def fresh_scores(queries, fresh_keys, fresh_len, bias_dist):
    row_ids = jnp.arange(queries.shape[0], dtype=jnp.int32)[:, None]
    col_ids = jnp.arange(fresh_keys.shape[0], dtype=jnp.int32)[None, :]
    scores = jnp.einsum("qhe,khe->hqk", queries, fresh_keys, preferred_element_type=jnp.float32)
    scores = scores + shifted_bias(bias_dist, 0, queries.shape[0], fresh_keys.shape[0])
    admitted = (col_ids <= row_ids) & (col_ids < fresh_len)
    return jnp.where(admitted[None], scores, NEG_FILL)


def self_padded(
    queries, key_rows, value_rows, fresh_keys, fresh_values, old_len, fresh_len, bias_dist
):
    scores = jnp.concatenate(
        [
            cached_scores(queries, key_rows, 0, old_len, bias_dist),
            fresh_scores(queries, fresh_keys, fresh_len, bias_dist),
        ],
        axis=2,
    )
    weights = softmax_rows(scores)
    value_all = jnp.concatenate([value_rows, fresh_values], axis=0)
    return jnp.einsum(
        "hqk,khe->qhe", weights, value_all, preferred_element_type=jnp.float32
    ).astype(jnp.bfloat16)


def self_attend(queries, key_value, cache_dec, slot_old, slot_new, bias_dist, heads_dev):
    req_dev, cache_len = (cache_dec.shape[0], cache_dec.shape[1])
    cache_split = cache_dec.reshape(req_dev, cache_len, heads_dev, 2, -1)

    def one_request(request):
        queries_one, pair_one, cache_one, old_len, fresh_len = request
        return self_padded(
            queries_one,
            cache_one[:, :, 0],
            cache_one[:, :, 1],
            pair_one[:, 0],
            pair_one[:, 1],
            old_len,
            fresh_len,
            bias_dist,
        )

    return lax.map(one_request, (queries, key_value, cache_split, slot_old, slot_new))


def cross_attend(queries, key_value, slot_enc):
    scores = jnp.einsum(
        "rqhe,rkhe->rhqk", queries, key_value[:, :, 0], preferred_element_type=jnp.float32
    )
    col_ids = jnp.arange(key_value.shape[1], dtype=jnp.int32)
    scores = jnp.where(
        col_ids[None, None, None, :] < slot_enc[:, None, None, None], scores, NEG_FILL
    )
    weights = softmax_rows(scores)
    return jnp.einsum(
        "rhqk,rkhe->rqhe", weights, key_value[:, :, 1], preferred_element_type=jnp.float32
    ).astype(jnp.bfloat16)


def add_branch(residual, left, weight, gain):
    residual = residual + row_total(left, weight)
    normed = rms_rows(residual, gain)
    return (residual, normed)


def per_device(
    new_states,
    encoder_out,
    cache_in,
    slot_order,
    new_lengths,
    cache_lengths,
    enc_lengths,
    bucket_of,
    rel_bias,
    norm_gain,
    self_q,
    self_kv,
    self_out,
    cross_q,
    cross_kv,
    cross_out,
    ff_in,
    ff_out,
):
    blk_count = lax.axis_size("blk")
    heads_dev = H // blk_count
    width_dev = heads_dev * HD
    req_dev = cache_in.shape[0] // lax.axis_size("req")
    own_slots = lax.dynamic_slice_in_dim(slot_order, lax.axis_index("req") * req_dev, req_dev, 0)
    slot_new = pick_lengths(new_lengths, own_slots)
    slot_old = pick_lengths(cache_lengths, own_slots)
    slot_enc = pick_lengths(enc_lengths, own_slots)
    ordered = jnp.take(cache_in, slot_order, axis=0)
    cache_dec = lax.all_to_all(
        lax.all_to_all(ordered, "req", split_axis=0, concat_axis=2, tiled=True),
        "blk",
        split_axis=2,
        concat_axis=1,
        tiled=True,
    )
    onehot = (bucket_of[:, None] == jnp.arange(rel_bias.shape[0], dtype=jnp.int32)[None, :]).astype(
        jnp.float32
    )
    own_bias = lax.dynamic_slice_in_dim(rel_bias, lax.axis_index("blk") * heads_dev, heads_dev, 1)
    bias_dist = jnp.dot(onehot, own_bias, precision=lax.Precision.HIGHEST).T
    gathered = (
        lax.all_gather(self_q, "req", axis=0, tiled=True),
        lax.all_gather(self_kv, "req", axis=0, tiled=True),
        lax.all_gather(self_out, "req", axis=1, tiled=True),
        lax.all_gather(cross_q, "req", axis=0, tiled=True),
        lax.all_gather(cross_kv, "req", axis=0, tiled=True),
        lax.all_gather(cross_out, "req", axis=1, tiled=True),
        lax.all_gather(ff_in, "req", axis=0, tiled=True),
        lax.all_gather(ff_out, "req", axis=1, tiled=True),
    )
    wq_self, wkv_self, wo_self, wq_cross, wkv_cross, wo_cross, w_in, w_out = gathered
    states_full = new_states.astype(jnp.float32)
    normed = rms_rows(states_full, norm_gain[0])
    residual = states_full
    self_cat = jnp.concatenate([wq_self, wkv_self.reshape(wkv_self.shape[0], -1)], axis=1)
    projected = (
        jnp.dot(normed, self_cat, preferred_element_type=jnp.float32)
        .astype(jnp.bfloat16)
        .reshape(req_dev, -1, 3, heads_dev, HD)
    )
    context = self_attend(
        projected[:, :, 0], projected[:, :, 1:], cache_dec, slot_old, slot_new, bias_dist, heads_dev
    )
    residual, normed = add_branch(residual, context.reshape(-1, width_dev), wo_self, norm_gain[1])
    queries = (
        jnp.dot(normed, wq_cross, preferred_element_type=jnp.float32)
        .astype(jnp.bfloat16)
        .reshape(req_dev, -1, heads_dev, HD)
    )
    cross_pair = wkv_cross.reshape(wkv_cross.shape[0], -1)
    key_value = (
        jnp.dot(encoder_out, cross_pair, preferred_element_type=jnp.float32)
        .astype(jnp.bfloat16)
        .reshape(req_dev, -1, 2, heads_dev, HD)
    )
    context = cross_attend(queries, key_value, slot_enc)
    residual, normed = add_branch(residual, context.reshape(-1, width_dev), wo_cross, norm_gain[2])
    ff_dev = w_in.shape[2]
    gate_up = jnp.dot(normed, w_in.reshape(w_in.shape[0], -1), preferred_element_type=jnp.float32)
    hidden = (jax.nn.gelu(gate_up[:, :ff_dev], approximate=True) * gate_up[:, ff_dev:]).astype(
        jnp.bfloat16
    )
    layer_out = (residual + row_total(hidden, w_out)).astype(jnp.bfloat16)
    return (layer_out, cache_dec)


def solution(mesh):
    in_specs = (
        P("req", None),
        P("req", None),
        P(None, "blk", "req"),
        P(),
        P(),
        P(),
        P(),
        P(),
        P(),
        P(),
        P("req", "blk"),
        P("req", None, "blk"),
        P("blk", "req"),
        P("req", "blk"),
        P("req", None, "blk"),
        P("blk", "req"),
        P("req", None, "blk"),
        P("blk", "req"),
    )
    out_specs = (P("req", None), P("req", None, "blk"))
    return jax.shard_map(
        per_device, mesh=mesh, in_specs=in_specs, out_specs=out_specs, check_vma=False
    )
```

profile of v0, /device:TPU:0, one launch (start us, length us, event | category | flops | bytes accessed | tf_op | source)
XLA Modules:
  0.0 527.7 jit_solution(10853733468998918538)
XLA Ops:
  14.8 5.3 %all-to-all-start = ((bf16[4,512,512]{2,1,0:T(8,128)(2,1)}), bf16[4,512,512]{2,1,0:T(8,128)(2,1)S(1)}, u32[]{:S(2)}, u32[]{:S(2)}) async-start(bf16[4,512,512]{2,1,0:T(8,128)(2,1)} %broadcast_select_fusion), calls=%async_computation | async-start | bytes 4194304 | tf_op jit(solution)/shard_map/all_to_all | solution.py:151
  27.0 10.9 %gather_fusion.1 = f32[4608,2]{1,0:T(8,128)} fusion(f32[2,4608]{0,1:T(8,128)} %fusion.39, s32[5120]{0:T(1024)S(1)} %pad_clamp_fusion), kind=kCustom, calls=%fused_computation.1 | custom fusion | bytes 92160 | tf_op jit(solution)/shard_map/while/body/eval_jaxpr/gather | solution.py:34
  49.1 18.5 %copy.87 = bf16[1,512,2048]{1,0,2:T(2,128)(2,1)} copy(bf16[1,512,2048]{1,2,0:T(8,128)(2,1)S(1)} %bitcast.109) | data formatting | bytes 4194304 | tf_op jit(solution)/shard_map/all_to_all | solution.py:151
  68.1 14.1 %reduce.14 = bf16[2048,512]{1,0:T(8,128)(2,1)S(1)} reduce(bf16[2048,1,512]{2,1,0:T(2,128)(2,1)} %bitcast.106, bf16[]{:T(256)} %broadcast.215), dimensions={1}, to_apply=%bitcast.102.reduce_sub_computation | reduce | bytes 4194306
  91.1 8.8 %broadcast_bitcast_fusion = f32[1,2,512,4608]{3,2,1,0:T(8,128)} fusion(f32[2,4608]{1,0:T(2,128)S(1)} %copy.64), kind=kLoop, calls=%fused_computation.10 | loop fusion | bytes 18911232
  99.9 31.0 %copy.77 = f32[1,2,512,4608]{3,1,2,0:T(2,128)S(1)} copy(f32[1,2,512,4608]{3,2,1,0:T(8,128)} %broadcast_bitcast_fusion) | data formatting | bytes 37748736
  130.9 6.8 %slice.87 = f32[2,2358784]{1,0:T(2,128)} slice(f32[2,2359296]{1,0:T(2,128)S(1)} %bitcast.103), slice={[0:2], [0:2358784]} | slice | bytes 37740544 | tf_op jit(solution)/shard_map/while/body/eval_jaxpr/slice | solution.py:36
  137.8 41.7 %reshape.257 = f32[4717568]{0:T(1024)} reshape(f32[2,2358784]{1,0:T(2,128)} %slice.87) | data formatting | bytes 37740544
  179.5 24.9 %reshape.220 = f32[2,512,4607]{2,1,0:T(8,128)} reshape(f32[4717568]{0:T(1024)} %reshape.257) | data formatting | bytes 37740544 | tf_op jit(solution)/shard_map/while/body/eval_jaxpr/reshape | solution.py:37
  204.4 10.6 %all_gather.25 = bf16[1024,2,128]{2,1,0:T(2,128)(2,1)S(1)} all-gather(bf16[256,2,128]{2,1,0:T(2,128)(2,1)S(1)} %copy-done.16), channel_id=1, replica_groups=mesh['req'=4,'blk'=8] {'req'}, dimensions={0}, use_global_device_ids=true | all-gather | bytes 655360 | tf_op jit(solution)/shard_map/all_gather | solution.py:164
  226.1 9.5 %reshape.222 = f32[2,512,1023]{2,1,0:T(8,128)} reshape(f32[2,523776]{1,0:T(2,128)} %slice.90) | data formatting | bytes 8380416 | tf_op jit(solution)/shard_map/while/body/eval_jaxpr/reshape | solution.py:37
  235.7 8.2 %all_gather.24 = bf16[1024,128]{1,0:T(8,128)(2,1)S(1)} all-gather(bf16[256,128]{1,0:T(8,128)(2,1)S(1)} %copy-done.18), channel_id=1, replica_groups=mesh['req'=4,'blk'=8] {'req'}, dimensions={0}, use_global_device_ids=true | all-gather | bytes 327680 | tf_op jit(solution)/shard_map/all_gather | solution.py:163
  243.9 10.7 %all_gather.26 = bf16[128,1024]{1,0:T(8,128)(2,1)S(1)} all-gather(bf16[128,256]{1,0:T(8,128)(2,1)S(1)} %copy-done.19), channel_id=1, replica_groups=mesh['req'=4,'blk'=8] {'req'}, dimensions={1}, use_global_device_ids=true | all-gather | bytes 327680 | tf_op jit(solution)/shard_map/all_gather | solution.py:165
  254.6 8.7 %all_gather.28 = bf16[1024,128]{1,0:T(8,128)(2,1)} all-gather(bf16[256,128]{1,0:T(8,128)(2,1)S(1)} %copy-done.20), channel_id=1, replica_groups=mesh['req'=4,'blk'=8] {'req'}, dimensions={0}, use_global_device_ids=true | all-gather | bytes 327680 | tf_op jit(solution)/shard_map/all_gather | solution.py:166
  263.3 10.7 %all_gather.27 = bf16[1024,2,128]{2,1,0:T(2,128)(2,1)} all-gather(bf16[256,2,128]{2,1,0:T(2,128)(2,1)S(1)} %copy-done.17), channel_id=1, replica_groups=mesh['req'=4,'blk'=8] {'req'}, dimensions={0}, use_global_device_ids=true | all-gather | bytes 655360 | tf_op jit(solution)/shard_map/all_gather | solution.py:167
  281.4 7.0 %reshape.260 = bf16[2048,1,512]{2,1,0:T(2,128)(2,1)} reshape(bf16[8,2,65536]{2,1,0:T(2,128)(2,1)} %all-to-all-done.1) | data formatting | bytes 4194304
  300.2 11.3 %fusion.70 = (f32[2,512]{1,0:T(2,128)S(1)}, f32[2,512,4096]{2,1,0:T(8,128)S(1)}) fusion(f32[2,512,4607]{2,1,0:T(8,128)} %reshape.220, bf16[4096,2,2,64]{0,3,2,1:T(8,128)(2,1)} %squeeze.39, bf16[1,512,3,2,64]{1,4,3,2,0:T(8,128)(2,1)} %bitcast.116, pred[4096]{0:T(1024)(128)(4,1)S(1)} %iota_compare_fusion.3), kind=kOutput, calls=%fused_computation.118 | convolution fusion | flops 549452800 | bytes 34742272 | tf_op jit(solution)/shard_map/while/body/eval_jaxpr/qhe,khe->hqk/dot_general | solution.py:48
  311.5 5.7 %copy-done.2 = f32[2,512,4096]{2,1,0:T(8,128)} copy-done((f32[2,512,4096]{2,1,0:T(8,128)}, f32[2,512,4096]{2,1,0:T(8,128)S(1)}, u32[]{:S(2)}) %copy-start.2) | copy-done | bytes 16777240
  320.4 7.9 %fusion.13 = bf16[2,64,512]{2,1,0:T(8,128)(2,1)S(1)} fusion(f32[2,512,512]{2,1,0:T(8,128)S(1)} %copy-done.8, f32[2,512,4096]{2,1,0:T(8,128)} %copy-done.2, f32[2,512]{1,0:T(2,128)S(1)} %fusion.3, f32[2,512]{1,0:T(2,128)S(1)} %reduce_max.32, bf16[512,2,64]{0,2,1:T(8,128)(2,1)S(1)} %slice_bitcast_fusion.10, bf16[4096,2,64]{0,2,1:T(8,128)(2,1)} %slice_bitcast_fusion.2), kind=kOutput, calls=%fused_computation.42 | convolution fusion | flops 625278976 | bytes 20193280 | tf_op jit(solution)/shard_map/while/body/eval_jaxpr/hqk,khe->qhe/dot_general | solution.py:76
  329.9 9.4 %all_gather.29 = bf16[128,1024]{1,0:T(8,128)(2,1)S(1)} all-gather(bf16[128,256]{1,0:T(8,128)(2,1)S(1)} %copy-done.21), channel_id=1, replica_groups=mesh['req'=4,'blk'=8] {'req'}, dimensions={1}, use_global_device_ids=true | all-gather | bytes 327680 | tf_op jit(solution)/shard_map/all_gather | solution.py:168
  341.8 46.7 %all-reduce.4.cloned.1.call-done = bf16[512,1024]{1,0:T(8,128)(2,1)} async-done(((bf16[512,1024]{1,0:T(8,128)(2,1)}), bf16[512,1024]{1,0:T(8,128)(2,1)}) %all-reduce.4.cloned.1.call-update) | async-done | bytes 1048592 | tf_op jit(solution)/shard_map/psum | solution.py:43
  394.9 18.6 %all_gather.31 = bf16[352,1024]{1,0:T(8,128)(2,1)} all-gather(bf16[352,256]{1,0:T(8,128)(2,1)S(1)} %copy-done.15), channel_id=1, replica_groups=mesh['req'=4,'blk'=8] {'req'}, dimensions={1}, use_global_device_ids=true | all-gather | bytes 901120 | tf_op jit(solution)/shard_map/all_gather | solution.py:170
  413.4 38.7 %all-reduce.6.cloned.1.call-done = bf16[512,1024]{1,0:T(8,128)(2,1)} async-done(((bf16[512,1024]{1,0:T(8,128)(2,1)}), bf16[512,1024]{1,0:T(8,128)(2,1)}) %all-reduce.6.cloned.1.call-update) | async-done | bytes 1048592 | tf_op jit(solution)/shard_map/psum | solution.py:43
  462.4 53.9 %all-reduce.8.cloned.1.call-done = bf16[512,1024]{1,0:T(8,128)(2,1)} async-done(((bf16[512,1024]{1,0:T(8,128)(2,1)}), bf16[512,1024]{1,0:T(8,128)(2,1)}) %all-reduce.8.cloned.1.call-update) | async-done | bytes 1048592 | tf_op jit(solution)/shard_map/psum | solution.py:43
  (124 shorter events, 91.2 us)
Async XLA Ops:
  14.8 6.0 %copy-start.26 = (s32[4]{0:T(128)S(1)}, s32[4]{0:T(128)}, u32[]{:S(2)}) copy-start(s32[4]{0:T(128)} %param.23) | copy-start | bytes 52
  14.8 8.1 %copy-start.22 = (s32[4608]{0:T(1024)S(1)}, s32[4608]{0:T(1024)}, u32[]{:S(2)}) copy-start(s32[4608]{0:T(1024)} %param.25) | copy-start | bytes 55300
  14.8 30.2 %all-to-all-start = ((bf16[4,512,512]{2,1,0:T(8,128)(2,1)}), bf16[4,512,512]{2,1,0:T(8,128)(2,1)S(1)}, u32[]{:S(2)}, u32[]{:S(2)}) async-start(bf16[4,512,512]{2,1,0:T(8,128)(2,1)} %broadcast_select_fusion), calls=%async_computation | async-start | bytes 4194304 | tf_op jit(solution)/shard_map/all_to_all | solution.py:151
  86.0 195.4 %all-to-all-start.1 = ((bf16[8,2,65536]{2,1,0:T(2,128)(2,1)}), bf16[8,2,65536]{2,1,0:T(2,128)(2,1)}, u32[]{:S(2)}, u32[]{:S(2)}) async-start(bf16[8,2,65536]{2,1,0:T(2,128)(2,1)} %reshape.259), calls=%async_computation.1 | async-start | bytes 4194304 | tf_op jit(solution)/shard_map/all_to_all | solution.py:150
  91.0 297.5 %all-reduce.4.cloned.1.call-start = ((), (), s32[]{:S(2)}) async-start(), calls=%async_computation.2 | async-start | bytes 2097152 | tf_op jit(solution)/shard_map/psum | solution.py:43
  179.5 25.0 %copy-start.16 = (bf16[256,2,128]{2,1,0:T(2,128)(2,1)S(1)}, bf16[256,2,128]{2,1,0:T(2,128)(2,1)}, u32[]{:S(2)}) copy-start(bf16[256,2,128]{2,1,0:T(2,128)(2,1)} %param.29) | copy-start | bytes 393220
  226.1 9.6 %copy-start.18 = (bf16[256,128]{1,0:T(8,128)(2,1)S(1)}, bf16[256,128]{1,0:T(8,128)(2,1)}, u32[]{:S(2)}) copy-start(bf16[256,128]{1,0:T(8,128)(2,1)} %param.28) | copy-start | bytes 196612
  226.1 17.7 %copy-start.19 = (bf16[128,256]{1,0:T(8,128)(2,1)S(1)}, bf16[128,256]{1,0:T(8,128)(2,1)}, u32[]{:S(2)}) copy-start(bf16[128,256]{1,0:T(8,128)(2,1)} %param.30) | copy-start | bytes 196612
  226.1 28.4 %copy-start.20 = (bf16[256,128]{1,0:T(8,128)(2,1)S(1)}, bf16[256,128]{1,0:T(8,128)(2,1)}, u32[]{:S(2)}) copy-start(bf16[256,128]{1,0:T(8,128)(2,1)} %param.31) | copy-start | bytes 196612
  226.1 37.1 %copy-start.17 = (bf16[256,2,128]{2,1,0:T(2,128)(2,1)S(1)}, bf16[256,2,128]{2,1,0:T(2,128)(2,1)}, u32[]{:S(2)}) copy-start(bf16[256,2,128]{2,1,0:T(2,128)(2,1)} %param.32) | copy-start | bytes 393220
  226.1 47.8 %copy-start.27 = (s32[4]{0:T(128)S(1)}, s32[4]{0:T(128)}, u32[]{:S(2)}) copy-start(s32[4]{0:T(128)} %param.22) | copy-start | bytes 52
  235.7 40.9 %copy-start.4 = (bf16[512,1024]{1,0:T(8,128)(2,1)S(1)}, bf16[512,1024]{1,0:T(8,128)(2,1)}, u32[]{:S(2)}) copy-start(bf16[512,1024]{1,0:T(8,128)(2,1)} %param.18) | copy-start | bytes 3145732
  235.7 41.2 %copy-start.23 = (f32[3,1024]{1,0:T(4,128)S(1)}, f32[3,1024]{1,0:T(4,128)}, u32[]{:S(2)}) copy-start(f32[3,1024]{1,0:T(4,128)} %param.27) | copy-start | bytes 36868
  300.2 17.1 %copy-start.8 = (f32[2,512,512]{2,1,0:T(8,128)S(1)}, f32[2,512,512]{2,1,0:T(8,128)}, u32[]{:S(2)}) copy-start(f32[2,512,512]{2,1,0:T(8,128)} %get-tuple-element.32) | copy-start | bytes 6291460
  311.5 5.7 %copy-start.2 = (f32[2,512,4096]{2,1,0:T(8,128)}, f32[2,512,4096]{2,1,0:T(8,128)S(1)}, u32[]{:S(2)}) copy-start(f32[2,512,4096]{2,1,0:T(8,128)S(1)} %get-tuple-element.22) | copy-start | bytes 50331652
  328.3 11.0 %copy-start.28 = (s32[4]{0:T(128)S(1)}, s32[4]{0:T(128)}, u32[]{:S(2)}) copy-start(s32[4]{0:T(128)} %param.24) | copy-start | bytes 52
  328.3 13.0 %copy-start.13 = (bf16[1024,2,128]{2,1,0:T(2,128)(2,1)S(1)}, bf16[1024,2,128]{2,1,0:T(2,128)(2,1)}, u32[]{:S(2)}) copy-start(bf16[1024,2,128]{2,1,0:T(2,128)(2,1)} %all_gather.27) | copy-start | bytes 1572868
  328.3 13.0 %copy-start.24 = (bf16[512,1024]{1,0:T(8,128)(2,1)S(1)}, bf16[512,1024]{1,0:T(8,128)(2,1)}, u32[]{:S(2)}) copy-start(bf16[512,1024]{1,0:T(8,128)(2,1)} %param.19) | copy-start | bytes 3145732
  328.3 60.2 %copy-start.5 = (bf16[512,1024]{1,0:T(8,128)(2,1)S(1)}, bf16[512,1024]{1,0:T(8,128)(2,1)}, u32[]{:S(2)}) copy-start(bf16[512,1024]{1,0:T(8,128)(2,1)} %param.18) | copy-start | bytes 3145732
  329.8 122.3 %all-reduce.6.cloned.1.call-start = ((), (), s32[]{:S(2)}) async-start(), calls=%async_computation.3 | async-start | bytes 2097152 | tf_op jit(solution)/shard_map/psum | solution.py:43
  339.3 51.0 %copy-start.14 = (bf16[1024,128]{1,0:T(8,128)(2,1)S(1)}, bf16[1024,128]{1,0:T(8,128)(2,1)}, u32[]{:S(2)}) copy-start(bf16[1024,128]{1,0:T(8,128)(2,1)} %all_gather.28) | copy-start | bytes 786436
  394.2 59.8 %all-gather.2.cloned.1.call-start = ((), (), s32[]{:S(2)}) async-start(), calls=%async_computation.4 | async-start | bytes 1802240 | tf_op jit(solution)/shard_map/all_gather | solution.py:169
  394.8 121.6 %all-reduce.8.cloned.1.call-start = ((), (), s32[]{:S(2)}) async-start(), calls=%async_computation.5 | async-start | bytes 2097152 | tf_op jit(solution)/shard_map/psum | solution.py:43
  458.4 61.7 %copy-start.1 = (bf16[4,512,512]{2,1,0:T(8,128)(2,1)S(1)}, bf16[4,512,512]{2,1,0:T(8,128)(2,1)}, u32[]{:S(2)}) copy-start(bf16[4,512,512]{2,1,0:T(8,128)(2,1)} %param.20) | copy-start | bytes 6291460
  (11 other events, 26.7 us)
Sparse Core Ops, SparseCore 0:
  329.9 58.5 all-reduce.3
  394.3 57.6 all-reduce.5
  458.5 57.8 all-reduce.7
Sparse Core Ops, SparseCore 1:
  396.5 30.4 all-gather.1
where the time goes:
time: 537 us; the launch traced here: 528 us
  local copies, waits for them, and re-layouts  207 us (39%)
  waiting for transfers between devices  145 us (27%)
  blocking collectives  76.8 us (14%)
  matrix products  36.4 us (7%)
  other arithmetic  35.6 us (7%)
  between operations  16.7 us (3%)
  starting transfers between devices  10.5 us (2%)
    psum x3, waiting for transfers between devices, row_total(): return lax.psum(term.astype(jnp.bfloat16), 'blk').astype(jnp.float32)  139 us
    unnamed x68, local copies, waits for them, and re-layouts  108 us
    reshape x2, local copies, waits for them, and re-layouts, shifted_bias(): skewed = flat.reshape(heads_here, row_count, line_len)  34.5 us
    all_to_all x2, local copies, waits for them, and re-layouts, per_device(): lax.all_to_all(ordered, 'req', split_axis=0, concat_axis=2, tiled=True)  21.3 us
    all_gather x1, blocking collectives, per_device(): lax.all_gather(ff_out, 'req', axis=1, tiled=True)  18.6 us
    gather x4, local copies, waits for them, and re-layouts, shifted_bias(): line = bias_dist[:, jnp.clip(base + row_count - 1 - steps, 0, span_len - 1)]  17.9 us
    unnamed x1, other arithmetic  14.1 us
    dot_general x1, matrix products, cached_scores(): jnp.einsum('qhe,khe->hqk', queries, key_rows, preferred_element_type=jnp....  11.3 us
  transfers between devices with their start and end apart: 6, of which 4 were waited for; matrix products, arithmetic and copies ran while one was open for 32% of the time, Pallas kernels for 0%

commit v1 on v0

v1 whole, which is shorter than its diff:
```python
import functools

import jax
import jax.numpy as jnp
from jax import lax
from jax.experimental import pallas as pl
from jax.experimental.pallas import tpu as pltpu
from jax.sharding import PartitionSpec as P

H = 16
HD = 64
EPSILON = 1e-06
NEG_FILL = -1e30
TILE = 128
F32 = jnp.float32
BF16 = jnp.bfloat16


def pick(table, place):
    matches = place == jnp.arange(table.shape[0], dtype=jnp.int32)
    return jnp.sum(jnp.where(matches, table, 0))


def xor_send(value, axis, step):
    size = lax.axis_size(axis)
    return lax.ppermute(value, axis, [(i, i ^ step) for i in range(size)])


def far_first(count):
    return [0, *range(count // 2, count), *range(1, count // 2)]


def chip_sends(parts):
    moved = [parts[0]] + [None] * (len(parts) - 1)
    for k in far_first(len(parts))[1:]:
        moved[k] = xor_send(parts[k], "blk", 2 * k)
    return moved


def reordered(parts):
    return [parts[k] for k in far_first(len(parts))]


def restored(parts):
    found = [None] * len(parts)
    for part, k in zip(parts, far_first(len(parts))):
        found[k] = part
    return found


VMEM = pl.BlockSpec(memory_space=pltpu.VMEM)
SMEM = pl.BlockSpec(memory_space=pltpu.SMEM)


def local_call(kernel, operands, outs, smem=0, scratch=(), flops=0, transcendentals=0):
    moved = sum(x.size * x.dtype.itemsize for x in list(operands) + list(outs))
    return pl.pallas_call(
        kernel,
        out_shape=list(outs),
        in_specs=[SMEM] * smem + [VMEM] * (len(operands) - smem),
        out_specs=[VMEM] * len(outs),
        scratch_shapes=list(scratch),
        compiler_params=pltpu.CompilerParams(vmem_limit_bytes=32 << 20),
        cost_estimate=pl.CostEstimate(
            flops=flops, bytes_accessed=moved, transcendentals=transcendentals
        ),
    )(*operands)


def shaped(shape, dtype=BF16):
    return jax.ShapeDtypeStruct(tuple(shape), dtype)


def after(value, *others):
    return lax.optimization_barrier((value,) + others)[0]


def place_kernel(order, *refs):
    parts, out = refs[:-1], refs[-1]
    for k, part in enumerate(parts):
        size = part.shape[0]
        out[pl.ds(pl.multiple_of(order(k) * size, size), size), :] = part[...]


def place(parts, order):
    rows, cols = parts[0].shape
    out = shaped((len(parts) * rows, cols))
    return local_call(functools.partial(place_kernel, order), parts, [out])[0]


def req_stack(value, moved, stride):
    def order(k):
        return (lax.axis_index("req") // stride) % 2 ^ k

    return place([value, moved], order)


def part_owner(part, strides):
    owner = 0
    for i, stride in enumerate(strides):
        owner += stride * ((part >> i) & 1)
    return owner


def pack_projection(query, pair, out, at):
    depth = query.shape[0]
    value = pair[1]
    out[at : at + depth, :] = jnp.concatenate([query[...], pair[0]], axis=1)
    tail = jnp.concatenate([value[: depth // 2], value[depth // 2 :]], axis=1)
    out[at + depth : at + depth + depth // 2, :] = tail


def packed_projection(ref, at, depth, width):
    head = ref[at : at + depth, :]
    tail = ref[at + depth : at + depth + depth // 2, :]
    value = jnp.concatenate([tail[:, :width], tail[:, width:]], axis=0)
    return head[:, :width], head[:, width:], value


def pack_kernel(*refs):
    q1, kv1, q2, kv2, ff, o1, o2, o3, first, mid, wide, wide_ref = refs
    depth = q1.shape[0]
    done = depth + depth // 2
    pack_projection(q1, kv1, first, 0)
    first[done:, :] = o1[...]
    pack_projection(q2, kv2, mid, 0)
    mid[done:, :] = o2[...]
    span = wide_ref.shape[1] // 2
    wide_ref[...] = jnp.zeros(wide_ref.shape, wide_ref.dtype)
    wide_ref[:, : ff.shape[2]] = ff[0]
    wide_ref[:, span : span + ff.shape[2]] = ff[1]
    lanes = wide.shape[1]
    for block in range(wide_ref.shape[1] // lanes):
        wide[block * depth : (block + 1) * depth, :] = wide_ref[
            :, block * lanes : (block + 1) * lanes
        ]
    wide[wide.shape[0] - o3.shape[0] :, :] = o3[...]


def join_kernel(taken, first, *outs):
    tokens = outs[0].shape[0]
    outs[0][...] = taken[:tokens, :]
    for k, out in enumerate(outs[1:], 1):
        out[:tokens, :] = taken[k * tokens : (k + 1) * tokens, :]
        out[tokens:, :] = first[...]


def project_kernel(tokens, heads_dev, states_ref, gain_ref, first, *refs):
    parts, (query_ref, fresh_ref, share_ref, normed_ref) = refs[:-4], refs[-4:]
    states = states_ref[...].astype(F32)
    mean_square = jnp.mean(states * states, axis=-1, keepdims=True)
    normed = states * lax.rsqrt(mean_square + EPSILON) * gain_ref[0:1, :]
    normed_ref[...] = normed.astype(BF16)
    size = share_ref.shape[0]
    blk = lax.axis_index("blk")
    spot = lax.rem(blk, 2) * (states.shape[0] // (2 * size)) + blk // 2
    share_ref[...] = states_ref[pl.ds(pl.multiple_of(spot * size, size), size), :]
    width = heads_dev * HD
    depth = normed_ref.shape[1] // (1 + len(parts))
    query, key, value = 0.0, 0.0, 0.0
    for k, part in enumerate([first, *parts]):
        at = 0 if k == 0 else tokens
        owner = lax.axis_index("req") ^ k
        rows = normed_ref[:, pl.ds(pl.multiple_of(owner * depth, depth), depth)]
        w_query, w_key, w_value = packed_projection(part, at, depth, width)
        query = query + lax.dot_general(
            w_query, rows, (((0,), (1,)), ((), ())), preferred_element_type=F32
        )
        key = key + jnp.dot(rows, w_key, preferred_element_type=F32)
        value = value + jnp.dot(rows, w_value, preferred_element_type=F32)
    pieces = []
    for head in range(heads_dev):
        own = slice(head * HD, (head + 1) * HD)
        query_ref[head, :HD, :] = query[own, :].astype(BF16)
        query_ref[head, HD:, :] = jnp.zeros((HD, query.shape[1]), BF16)
        pieces += [key[:, own], value[:, own]]
    fresh_ref[...] = jnp.concatenate(pieces, axis=1).astype(BF16)


def cut_kernel(order_ref, cache_ref, *outs):
    kept, given = outs[:-1], outs[-1]
    tokens, cols = kept[0].shape
    core = lax.rem(lax.axis_index("blk"), 2)
    own = pl.ds(pl.multiple_of(core * cols, cols), cols)
    other = pl.ds(pl.multiple_of((1 - core) * cols, cols), cols)
    for k, out in enumerate(kept):
        slot = order_ref[lax.axis_index("req") ^ k]
        out[...] = cache_ref[slot, :, own]
        given[k * tokens : (k + 1) * tokens, :] = cache_ref[slot, :, other]


def cut_cache(cache_in, slot_order):
    count, tokens, cols = cache_in.shape[0], cache_in.shape[1], cache_in.shape[2] // 2
    outs = [shaped((tokens, cols))] * count + [shaped((count * tokens, cols))]
    return local_call(cut_kernel, [slot_order, cache_in], outs, smem=1)


def turn_kernel(count, *refs):
    parts, outs = refs[:count], refs[count:]
    shift = lax.axis_index("req") ^ (lax.axis_index("blk") // 2)
    for case in range(count):

        @pl.when(shift == case)
        def _(case=case):
            for k in range(count):
                outs[k][...] = parts[k ^ case][: outs[k].shape[0], :]


def turn(parts):
    outs = [shaped(parts[0].shape)] * len(parts)
    return local_call(functools.partial(turn_kernel, len(parts)), parts, outs)


def band_kernel(heads_dev, widths, bias_ref, line_ref, out_ref, row_ref):
    head = lax.axis_index("blk") * heads_dev + pl.program_id(0)
    buckets = line_ref[...]
    row = jnp.zeros(buckets.shape, F32)
    for bucket in range(bias_ref.shape[0]):
        row = jnp.where(buckets == bucket, bias_ref[bucket, head], row)
    row_ref[...] = row
    start = 0
    done = 0
    for width in widths:
        for u in range(0, width, TILE):
            window = row_ref[:, start + u : start + u + 2 * TILE]
            wide = jnp.broadcast_to(window, (TILE, 2 * TILE))
            turned = pltpu.roll(wide, TILE + 1, 1, stride=1, stride_axis=0)
            out_ref[0, :, done + u : done + u + TILE] = turned[:, :TILE]
        start += width + TILE
        done += width


def make_band(bucket_of, rel_bias, old_len, heads_dev, cache_len, rows):
    wide_old, wide_new = cache_len - TILE + rows, 2 * rows - TILE
    low = jnp.broadcast_to(bucket_of[:1], (cache_len - 1,))
    padded = jnp.concatenate([low, bucket_of, bucket_of[-1:]])
    line_old = lax.dynamic_slice(padded, (old_len,), (wide_old + TILE,))
    begin = cache_len - rows
    line_new = padded[begin : begin + wide_new + TILE]
    line = jnp.concatenate([line_old, line_new])[None, :]
    total = wide_old + wide_new
    return pl.pallas_call(
        functools.partial(band_kernel, heads_dev, (wide_old, wide_new)),
        grid=(heads_dev,),
        out_shape=jax.ShapeDtypeStruct((heads_dev, TILE, total), F32),
        in_specs=[
            pl.BlockSpec(memory_space=pltpu.SMEM),
            pl.BlockSpec(memory_space=pltpu.VMEM),
        ],
        out_specs=pl.BlockSpec((1, TILE, total), lambda h: (h, 0, 0)),
        scratch_shapes=[pltpu.VMEM(line.shape, F32)],
        compiler_params=pltpu.CompilerParams(vmem_limit_bytes=32 << 20),
        cost_estimate=pl.CostEstimate(
            flops=8 * heads_dev * TILE * total,
            bytes_accessed=4 * heads_dev * TILE * total,
            transcendentals=0,
        ),
    )(rel_bias, line)


def self_kernel(cache_len, places, first_call, *refs):
    order_ref, old_ref, new_ref, query_ref, band_ref = refs[:5]
    count = len(places)
    blocks, refs = refs[5 : 5 + count], refs[5 + count :]
    if first_call:
        fresh_ref, total_ref, top_ref, norm_ref, score_ref = refs
    else:
        total_in, top_in, norm_in, out_ref, total_ref, top_ref, norm_ref, score_ref = refs
    slot = order_ref[lax.axis_index("req")]
    old_len, new_len = old_ref[slot], new_ref[slot]
    rows = query_ref.shape[2]
    wide_old = cache_len - TILE + rows
    blk = lax.axis_index("blk")

    def attend(keys_values, begin, admit):
        size = keys_values.shape[0]
        top = top_ref[0]
        score_ref[:size, :] = jnp.dot(
            keys_values, query_ref[0], preferred_element_type=F32
        )
        for t in range(0, size, TILE):
            bias = band_ref[0, :, pl.ds(pl.multiple_of(begin - t, TILE), rows)]
            scores = score_ref[t : t + TILE, :] + bias
            scores = jnp.where(admit(t), scores, NEG_FILL)
            score_ref[t : t + TILE, :] = scores
            top = jnp.maximum(top, jnp.max(scores, axis=0, keepdims=True))
        weights = jnp.exp(score_ref[:size, :] - top)
        keep = jnp.exp(top_ref[0] - top)
        norm_ref[0] = norm_ref[0] * keep + jnp.sum(weights, axis=0, keepdims=True)
        term = lax.dot_general(
            keys_values, weights.astype(BF16), (((0,), (0,)), ((), ())),
            preferred_element_type=F32,
        )
        total_ref[0] = total_ref[0] * keep + term
        top_ref[0] = top

    if first_call:
        top_ref[...] = jnp.full(top_ref.shape, NEG_FILL, F32)
        norm_ref[...] = jnp.zeros(norm_ref.shape, F32)
        total_ref[...] = jnp.zeros(total_ref.shape, F32)

        def admit_fresh(t):
            keys = t + lax.broadcasted_iota(jnp.int32, (TILE, rows), 0)
            ids = lax.broadcasted_iota(jnp.int32, (TILE, rows), 1)
            return (keys <= ids) & (keys < new_len)

        attend(fresh_ref[...], wide_old + rows - TILE, admit_fresh)
    else:
        top_ref[...] = top_in[...]
        norm_ref[...] = norm_in[...]
        total_ref[...] = total_in[...]

    for block, place_of in zip(blocks, places):
        first = (blk ^ place_of) * block.shape[0]

        @pl.when(first < old_len)
        def _(block=block, first=first):
            def admit(t):
                keys = first + t + lax.broadcasted_iota(jnp.int32, (TILE, rows), 0)
                return keys < old_len

            attend(block[...], cache_len - TILE - first, admit)

    if not first_call:
        out_ref[0] = (total_ref[0, HD:, :] / norm_ref[0]).astype(BF16)


def self_attend(lens, query_t, band, blocks, places, cache_len, fresh=None, state=None):
    heads_dev, pair, rows = query_t.shape
    count, tokens = len(blocks), blocks[0].shape[0]
    first_call = state is None
    head_block = lambda *tail: pl.BlockSpec((1,) + tail, lambda h: (h, 0, 0))
    in_specs = [SMEM] * 3 + [
        head_block(pair, rows),
        head_block(TILE, band.shape[2]),
    ] + [pl.BlockSpec((tokens, pair), lambda h: (0, h))] * count
    held = [(pair, rows), (1, rows), (1, rows)]
    score = pltpu.VMEM((max(tokens, rows), rows), F32)
    if first_call:
        in_specs.append(pl.BlockSpec((rows, pair), lambda h: (0, h)))
        more = [fresh]
        out_specs = [head_block(*shape) for shape in held]
        out_shape = [jax.ShapeDtypeStruct((heads_dev,) + shape, F32) for shape in held]
        scratch = [score]
    else:
        in_specs += [head_block(*shape) for shape in held]
        more = list(state)
        out_specs = head_block(HD, rows)
        out_shape = jax.ShapeDtypeStruct((heads_dev, HD, rows), BF16)
        scratch = [pltpu.VMEM((1,) + shape, F32) for shape in held] + [score]
    keys_all = count * tokens + (rows if first_call else 0)
    return pl.pallas_call(
        functools.partial(self_kernel, cache_len, places, first_call),
        grid=(heads_dev,),
        in_specs=in_specs,
        out_specs=out_specs,
        out_shape=out_shape,
        scratch_shapes=scratch,
        compiler_params=pltpu.CompilerParams(vmem_limit_bytes=40 << 20),
        cost_estimate=pl.CostEstimate(
            flops=4 * heads_dev * pair * rows * keys_all,
            bytes_accessed=2 * heads_dev * pair * keys_all + 4 * band.size,
            transcendentals=heads_dev * rows * keys_all,
        ),
    )(*lens, query_t, band, *blocks, *more)


def project_out(lefts, weights, skip, depth, owners, partial_ref):
    stride = weights[0].shape[0] // len(owners)
    width = weights[0].shape[1]
    for part, owner in enumerate(owners):
        total = 0.0
        for left, weight in zip(lefts, weights):
            block = weight[part * stride + skip : part * stride + skip + depth, :]
            total = total + lax.dot_general(
                left, block, (((0,), (0,)), ((), ())), preferred_element_type=F32
            )
        partial_ref[:, owner * width : (owner + 1) * width] = total.astype(BF16)


def tail_kernel(skip, *refs):
    parts, out = refs[:-1], refs[-1]
    size = out.shape[0] // len(parts)
    for k, part in enumerate(parts):
        at = skip[0] if k == 0 else skip[1]
        spot = (lax.axis_index("req") ^ k) * size
        out[pl.ds(pl.multiple_of(spot, size), size), :] = part[at : at + size, :]


def self_out_kernel(owners, *refs):
    kept, taken, w_own, w_other = refs[:4]
    outs, partial_ref = refs[4:-1], refs[-1]
    lefts = [kept[...], taken[...]]
    project_out(lefts, (w_own, w_other), 0, kept.shape[0], owners, partial_ref)
    chip = lax.axis_index("blk") // 2
    for k, out in enumerate(outs):
        size = out.shape[0]
        out[...] = partial_ref[pl.ds(pl.multiple_of((chip ^ k) * size, size), size), :]


def sum_rows(parts, residual_ref):
    total = residual_ref[...].astype(F32)
    moved = parts[0][...].astype(F32)
    for part in parts[1:]:
        moved = moved + part[...].astype(F32)
    return total + moved


def norm_kernel(which, count, *refs):
    gain_ref, residual_ref = refs[:2]
    parts, (total_ref, normed_ref) = refs[2 : 2 + count], refs[2 + count :]
    total = sum_rows(parts, residual_ref)
    total_ref[...] = total
    mean_square = jnp.mean(total * total, axis=-1, keepdims=True)
    normed = total * lax.rsqrt(mean_square + EPSILON) * gain_ref[which : which + 1, :]
    normed_ref[...] = normed.astype(BF16)


def sum_kernel(*refs):
    residual_ref, parts, out_ref = refs[0], refs[1:-1], refs[-1]
    out_ref[...] = sum_rows(parts, residual_ref).astype(BF16)


def fill_rows(blocks, rows_ref):
    for k, block in enumerate(blocks):
        size = block.shape[0]
        rows_ref[k * size : (k + 1) * size, :] = block[...]


def hand_rows(outs, partial_ref):
    for k, out in enumerate(outs):
        size = out.shape[0]
        out[...] = partial_ref[k * size : (k + 1) * size, :]


def pair_kernel(owners, rows_ref, *refs):
    weights, outs = refs[:2], refs[2:]
    width = outs[0].shape[1]
    depth = rows_ref.shape[1] // len(owners)
    for i, weight in enumerate(weights):
        stride = weight.shape[0] // len(owners)
        key, value = 0.0, 0.0
        for part, owner in enumerate(owners):
            rows = rows_ref[:, owner * depth : (owner + 1) * depth]
            _, w_key, w_value = packed_projection(weight, part * stride, depth, width)
            key = key + jnp.dot(rows, w_key, preferred_element_type=F32)
            value = value + jnp.dot(rows, w_value, preferred_element_type=F32)
        outs[i][...] = key.astype(BF16)
        outs[2 + i][...] = value.astype(BF16)


def cross_kernel(owners, count, heads_dev, order_ref, enc_ref, *refs):
    blocks, refs = refs[:count], refs[count:]
    w_mid, keys, values = refs[0:2], refs[2:4], refs[4:6]
    outs, (rows_ref, partial_ref) = refs[6:-2], refs[-2:]
    fill_rows(blocks, rows_ref)
    width = heads_dev * HD
    depth = rows_ref.shape[1] // len(owners)
    stride = w_mid[0].shape[0] // len(owners)
    enc_len = enc_ref[order_ref[lax.axis_index("req")]]
    contexts = []
    for w, key_ref, value_ref in zip(w_mid, keys, values):
        query = 0.0
        for part, owner in enumerate(owners):
            query = query + lax.dot_general(
                w[part * stride : part * stride + depth, :width],
                rows_ref[:, owner * depth : (owner + 1) * depth],
                (((0,), (1,)), ((), ())),
                preferred_element_type=F32,
            )
        query = query.astype(BF16)
        head_of = lax.broadcasted_iota(jnp.int32, query.shape, 0) // HD
        pieces = []
        for head in range(heads_dev):
            own_query = jnp.where(head_of == head, query, jnp.zeros_like(query))
            scores = jnp.dot(key_ref[...], own_query, preferred_element_type=F32)
            admitted = lax.broadcasted_iota(jnp.int32, scores.shape, 0) < enc_len
            scores = jnp.where(admitted, scores, NEG_FILL)
            weights = jnp.exp(scores - jnp.max(scores, axis=0, keepdims=True))
            norm = jnp.sum(weights, axis=0, keepdims=True)
            context = lax.dot_general(
                value_ref[...], weights.astype(BF16), (((0,), (0,)), ((), ())),
                preferred_element_type=F32,
            )
            pieces.append((context[head * HD : (head + 1) * HD, :] / norm).astype(BF16))
        contexts.append(jnp.concatenate(pieces, axis=0))
    project_out(contexts, w_mid, depth + depth // 2, width, owners, partial_ref)
    hand_rows(outs, partial_ref)


def ffn_kernel(owners, count, hidden_dev, *refs):
    blocks, weights = refs[:count], refs[count : count + 2]
    outs, (rows_ref, partial_ref) = refs[count + 2 : -2], refs[-2:]
    fill_rows(blocks, rows_ref)
    depth = rows_ref.shape[1] // len(owners)
    stride = weights[0].shape[0] // len(owners)
    blocks_in = (stride - hidden_dev) // depth
    hiddens = []
    for w in weights:
        totals = [0.0] * blocks_in
        for part, owner in enumerate(owners):
            rows = rows_ref[:, owner * depth : (owner + 1) * depth]
            for block in range(blocks_in):
                at = part * stride + block * depth
                totals[block] = totals[block] + jnp.dot(
                    rows, w[at : at + depth, :], preferred_element_type=F32
                )
        both = jnp.concatenate(totals, axis=1)
        span = both.shape[1] // 2
        hidden = jax.nn.gelu(both[:, :span], approximate=True) * both[:, span:]
        hiddens.append(hidden[:, :hidden_dev].astype(BF16))
    width = weights[0].shape[1]
    for part, owner in enumerate(owners):
        total = 0.0
        for hidden, w in zip(hiddens, weights):
            at = (part + 1) * stride - hidden_dev
            total = total + jnp.dot(
                hidden, w[at : at + hidden_dev, :], preferred_element_type=F32
            )
        partial_ref[:, owner * width : (owner + 1) * width] = total.astype(BF16)
    hand_rows(outs, partial_ref)


def per_device(
    new_states,
    encoder_out,
    cache_in,
    slot_order,
    new_lengths,
    cache_lengths,
    enc_lengths,
    bucket_of,
    rel_bias,
    norm_gain,
    self_q,
    self_kv,
    self_out,
    cross_q,
    cross_kv,
    cross_out,
    ff_in,
    ff_out,
):
    req_count, blk_count = lax.axis_size("req"), lax.axis_size("blk")
    chips = blk_count // 2
    core = lax.axis_index("blk") % 2
    heads_dev = H // blk_count
    width_dev = heads_dev * HD
    rows, width = new_states.shape
    half, share = rows // 2, rows // blk_count
    depth, hidden_dev = self_q.shape[0], ff_in.shape[2]
    up_strides = [1 << i for i in range(req_count.bit_length() - 1)]
    down_strides = up_strides[::-1]
    down_owners = [part_owner(p, down_strides) for p in range(req_count)]

    tokens = cache_in.shape[1]
    *kept, given = cut_cache(cache_in, slot_order)
    near_req = [kept[0]] + [xor_send(kept[k], "req", k) for k in range(1, req_count)]
    taken = xor_send(given, "blk", 1)
    lanes = 2 * width_dev
    skip = depth + depth // 2
    packed_in = [self_q, self_kv, cross_q, cross_kv, ff_in, self_out, cross_out, ff_out]
    packed_in = [jnp.moveaxis(w, 1, 0) if w.ndim == 3 else w for w in packed_in]
    packed_in[0] = after(packed_in[0], kept[0])
    wide_cols = 2 * TILE * -(-hidden_dev // TILE)
    first, mid, wide = local_call(
        pack_kernel,
        packed_in,
        [
            shaped((skip + width_dev, lanes)),
            shaped((skip + width_dev, lanes)),
            shaped((depth * (wide_cols // lanes) + hidden_dev, lanes)),
        ],
        scratch=[pltpu.VMEM((depth, wide_cols), BF16)],
    )

    joined = shaped((tokens + first.shape[0], taken.shape[1]))
    joined = local_call(
        join_kernel,
        [taken, first],
        [shaped((tokens, taken.shape[1]))] + [joined] * (req_count - 1),
    )
    near = list(turn([after(near_req[0], joined[0]), *near_req[1:]]))
    far_req = [joined[0]]
    far_req += [xor_send(after(joined[k], near[0]), "req", k) for k in range(1, req_count)]
    near[1] = after(near[1], far_req[1])
    near = chip_sends(near)
    far = turn([after(far_req[0], *near[1:]), *far_req[1:]])
    far = chip_sends(far)

    def token_order(i):
        here = lax.axis_index("blk")
        return 2 * ((here // 2) ^ (i % chips)) + (lax.rem(here, 2) ^ (i // chips))

    cache_own = place(near + far, token_order)

    w_self_out = local_call(
        functools.partial(tail_kernel, (skip, tokens + skip)),
        [first, *far_req[1:]],
        [shaped((req_count * width_dev, self_out.shape[1]))],
    )[0]
    w_self_out = (w_self_out, xor_send(w_self_out, "blk", 1))

    old_len = pick(cache_lengths, pick(slot_order, lax.axis_index("req")))
    band = make_band(bucket_of, rel_bias, old_len, heads_dev, tokens * blk_count, rows)
    query_t, fresh, residual = local_call(
        functools.partial(project_kernel, tokens, heads_dev),
        [new_states, norm_gain, first, *far_req[1:]],
        [
            shaped((heads_dev, 2 * HD, rows)),
            shaped((rows, 2 * width_dev)),
            shaped((share, width)),
        ],
        scratch=[pltpu.VMEM((rows, width), BF16)],
        flops=6 * rows * width * width_dev,
    )
    lens = (slot_order, cache_lengths, new_lengths)
    near_places = [2 * k for k in range(chips)]
    far_places = [2 * k + 1 for k in range(chips)]
    cache_len = tokens * blk_count
    state = self_attend(
        lens,
        query_t,
        band,
        [far[0], *reordered(near)],
        [far_places[0], *reordered(near_places)],
        cache_len,
        fresh=fresh,
    )

    moved_mid = xor_send(after(mid, state[0], *far[1:]), "req", up_strides[0])
    moved_wide = xor_send(after(wide, state[0], *far[1:]), "req", down_strides[0])

    def gather_on(value, moved, strides, *hold):
        value = req_stack(after(value, *hold), moved, strides[0])
        for stride in strides[1:-1]:
            value = req_stack(value, xor_send(value, "req", stride), stride)
        return value, xor_send(value, "req", strides[-1])

    context = self_attend(
        lens,
        query_t,
        band,
        reordered(far)[1:],
        reordered(far_places)[1:],
        cache_len,
        state=state,
    )
    context = context.reshape(width_dev, rows)

    kept = lax.dynamic_slice_in_dim(context, core * half, half, 1)
    given = lax.dynamic_slice_in_dim(context, (1 - core) * half, half, 1)
    parts_out = [shaped((share, width))] * chips
    partial_ref = pltpu.VMEM((half, width), BF16)
    parts = local_call(
        functools.partial(self_out_kernel, range(req_count)),
        [kept, xor_send(given, "blk", 1), *w_self_out],
        parts_out,
        scratch=[partial_ref],
        flops=4 * half * width * width_dev,
    )


    mid, moved_mid = gather_on(mid, moved_mid, up_strides, parts[0])

    def add_and_norm(which, residual, parts):
        total, normed = local_call(
            functools.partial(norm_kernel, which, chips),
            [norm_gain, residual, *reordered(parts)],
            [shaped((share, width), F32), shaped((share, width))],
        )
        return total, normed, chip_sends([normed] * chips)

    parts = chip_sends(parts)
    residual, normed, blocks = add_and_norm(1, residual, parts)
    w_mid = req_stack(after(mid, normed), moved_mid, up_strides[-1])
    w_mid = (w_mid, xor_send(w_mid, "blk", 1))
    wide, moved_wide = gather_on(wide, moved_wide, down_strides, normed)

    enc_rows = encoder_out.shape[0]
    pairs = local_call(
        functools.partial(pair_kernel, range(req_count)),
        [encoder_out, *w_mid],
        [shaped((enc_rows, width_dev))] * 4,
        flops=8 * enc_rows * width * width_dev,
    )
    parts = local_call(
        functools.partial(cross_kernel, range(req_count), chips, heads_dev),
        [slot_order, enc_lengths, *reordered(blocks), *w_mid, *pairs],
        parts_out,
        smem=2,
        scratch=[partial_ref, partial_ref],
        flops=8 * half * width_dev * (width + heads_dev * enc_rows),
        transcendentals=2 * heads_dev * half * enc_rows,
    )
    parts = chip_sends(restored(parts))
    w_wide = req_stack(after(wide, *parts[1:]), moved_wide, down_strides[-1])
    w_wide = (w_wide, xor_send(w_wide, "blk", 1))
    residual, _, blocks = add_and_norm(2, residual, parts)

    parts = local_call(
        functools.partial(ffn_kernel, down_owners, chips, hidden_dev),
        [*reordered(blocks), *w_wide],
        parts_out,
        scratch=[partial_ref, partial_ref],
        flops=12 * half * width * hidden_dev,
        transcendentals=2 * half * hidden_dev,
    )
    final = local_call(sum_kernel, [residual, *reordered(chip_sends(restored(parts)))], [shaped((share, width))])[0]

    same = chip_sends([after(final, cache_own)] * chips)
    both = same + [xor_send(part, "blk", 1) for part in same]

    def row_order(i):
        here = lax.axis_index("blk")
        core_at = lax.rem(here, 2) ^ (i // chips)
        return core_at * chips + ((here // 2) ^ (i % chips))

    layer_out = place(both, row_order)
    return (layer_out, cache_own[None])


def solution(mesh):
    in_specs = (
        P("req", None),
        P("req", None),
        P(None, "blk", "req"),
        P(),
        P(),
        P(),
        P(),
        P(),
        P(),
        P(),
        P("req", "blk"),
        P("req", None, "blk"),
        P("blk", "req"),
        P("req", "blk"),
        P("req", None, "blk"),
        P("blk", "req"),
        P("req", None, "blk"),
        P("blk", "req"),
    )
    out_specs = (P("req", None), P("req", None, "blk"))
    return jax.shard_map(
        per_device, mesh=mesh, in_specs=in_specs, out_specs=out_specs, check_vma=False
    )
```

time: 537 us -> 189 us (0.35); the launches traced: 528 us -> 187 us
  local copies, waits for them, and re-layouts: 207 us -> 10.4 us
  blocking collectives: 76.8 us -> 0 us
  waiting for transfers between devices: 145 us -> 88 us
  starting transfers between devices: 10.5 us -> 57.1 us
  matrix products: 36.4 us -> 0 us
  other arithmetic: 35.6 us -> 1.96 us
  Pallas kernels: 0 us -> 27 us
  between operations: 16.7 us -> 2.97 us
    psum x3 -> x0, waiting for transfers between devices: 139 us -> none  [row_total(): return lax.psum(term.astype(jnp.bfloat16), 'blk').astype(jnp.float32)]
    unnamed x68 -> x50, local copies, waits for them, and re-layouts: 108 us -> 6.61 us
    ppermute x0 -> x43, waiting for transfers between devices: none -> 88 us  [xor_send(): return lax.ppermute(value, axis, [(i, i ^ step) for i in range(size)])]
    all_gather x7 -> x0, blocking collectives: 76.8 us -> none  [the longest x1 18.6 us: per_device(): lax.all_gather(ff_out, 'req', axis=1, tiled=True)]
    ppermute x0 -> x43, starting transfers between devices: none -> 57.1 us  [xor_send(): return lax.ppermute(value, axis, [(i, i ^ step) for i in range(size)])]
    dot_general x12 -> x0, matrix products: 35.5 us -> none  [the longest x1 11.3 us: cached_scores(): jnp.einsum('qhe,khe->hqk', queries, key_rows, preferred_element_type=jnp....]
    reshape x2 -> x0, local copies, waits for them, and re-layouts: 34.5 us -> none  [shifted_bias(): skewed = flat.reshape(heads_here, row_count, line_len)]
    all_to_all x4 -> x0, local copies, waits for them, and re-layouts: 27.9 us -> none  [the longest x2 21.3 us: per_device(): lax.all_to_all(ordered, 'req', split_axis=0, concat_axis=2, tiled=True)]
  transfers between devices with their start and end apart: 6 -> 43, of which waited for: 4 -> 23; matrix products, arithmetic and copies ran while one was open for 32% -> 3% of each run, Pallas kernels for 0% -> 11%
where the time goes in v1:
time: 189 us; the launch traced here: 187 us
  waiting for transfers between devices  88 us (47%)
  starting transfers between devices  57.1 us (30%)
  Pallas kernels  27 us (14%)
  local copies, waits for them, and re-layouts  10.4 us (6%)
  between operations  2.97 us (2%)
  other arithmetic  1.96 us (1%)
    ppermute x43, waiting for transfers between devices, xor_send(): return lax.ppermute(value, axis, [(i, i ^ step) for i in range(size)])  88 us
    ppermute x43, starting transfers between devices, xor_send(): return lax.ppermute(value, axis, [(i, i ^ step) for i in range(size)])  57.1 us
    pallas_call x20, Pallas kernels, local_call(): pl.pallas_call(kernel, out_shape=list(outs), in_specs=[SMEM] * smem + [VM...  17.1 us
    unnamed x50, local copies, waits for them, and re-layouts  6.61 us
    pallas_call x2, Pallas kernels, self_attend(): pl.pallas_call(functools.partial(self_kernel, cache_len, places, first_ca...  5.97 us
    pallas_call x1, Pallas kernels, make_band(): pl.pallas_call(functools.partial(band_kernel, heads_dev, (wide_old, wide_...  3.89 us
  transfers between devices with their start and end apart: 43, of which 23 were waited for; matrix products, arithmetic and copies ran while one was open for 3% of the time, Pallas kernels for 11%

profile of v1, /device:TPU:0, one launch (start us, length us, event | category | flops | bytes accessed | tf_op | source)
XLA Modules:
  0.0 187.3 jit_solution(7074576934745313984)
XLA Ops:
  5.3 2.5 %collective-permute-start.1 = (bf16[512,256]{1,0:T(8,128)(2,1)}, bf16[512,256]{1,0:T(8,128)(2,1)S(1)}, u32[]{:S(2)}, u32[]{:S(2)}) collective-permute-start(bf16[512,256]{1,0:T(8,128)(2,1)} %get-tuple-element.69), channel_id=1, source_target_pairs={{0,8},{8,0},{16,24},{24,16},{1,9},{9,1},{17,25},{25,17},{2,10},{10... | collective-permute-start | bytes 786440 | tf_op jit(solution)/shard_map/ppermute | solution.py:26
  15.1 6.9 %collective-permute-done.2.refs_2_ = bf16[512,256]{1,0:T(8,128)(2,1)S(1)} collective-permute-done((bf16[512,256]{1,0:T(8,128)(2,1)}, bf16[512,256]{1,0:T(8,128)(2,1)S(1)}, u32[]{:S(2)}, u32[]{:S(2)}) %collective-permute-start.2) | collective-permute-done | bytes 262176 | tf_op jit(solution)/shard_map/ppermute | solution.py:26
  28.4 2.6 %collective-permute-start.8 = (bf16[512,256]{1,0:T(8,128)(2,1)}, bf16[512,256]{1,0:T(8,128)(2,1)S(1)}, u32[]{:S(2)}, u32[]{:S(2)}) collective-permute-start(bf16[512,256]{1,0:T(8,128)(2,1)} %copy-done.20), channel_id=1, source_target_pairs={{0,4},{1,5},{2,6},{3,7},{4,0},{5,1},{6,2},{7,3},{8,12},{9,13},{10,... | collective-permute-start | bytes 786440 | tf_op jit(solution)/shard_map/ppermute | solution.py:26
  32.4 7.0 %collective-permute-done.4.refs_0_.refs_1_ = bf16[1024,256]{1,0:T(8,128)(2,1)S(1)} collective-permute-done((bf16[1024,256]{1,0:T(8,128)(2,1)}, bf16[1024,256]{1,0:T(8,128)(2,1)S(1)}, u32[]{:S(2)}, u32[]{:S(2)}) %collective-permute-start.4) | collective-permute-done | bytes 524320 | tf_op jit(solution)/shard_map/ppermute | solution.py:26
  48.9 4.1 %collective-permute-done.7.refs_9_.refs_1_ = bf16[512,256]{1,0:T(8,128)(2,1)S(1)} collective-permute-done((bf16[512,256]{1,0:T(8,128)(2,1)}, bf16[512,256]{1,0:T(8,128)(2,1)S(1)}, u32[]{:S(2)}, u32[]{:S(2)}) %collective-permute-start.7) | collective-permute-done | bytes 262176 | tf_op jit(solution)/shard_map/ppermute | solution.py:26
  53.9 3.0 %collective-permute-start.10 = (bf16[512,256]{1,0:T(8,128)(2,1)}, bf16[512,256]{1,0:T(8,128)(2,1)S(1)}, u32[]{:S(2)}, u32[]{:S(2)}) collective-permute-start(bf16[512,256]{1,0:T(8,128)(2,1)} %get-tuple-element.85), channel_id=1, source_target_pairs={{0,4},{1,5},{2,6},{3,7},{4,0},{5,1},{6,2},{7,3},{8,12},{9,13},{10,... | collective-permute-start | bytes 786440 | tf_op jit(solution)/shard_map/ppermute | solution.py:26
  58.4 3.9 %shard_map.190.refs_4_ = f32[2,128,5376]{2,1,0:T(8,128)S(1)} custom-call(f32[32,16]{1,0:T(8,128)S(1)} %copy.23.bias_ref, s32[1,5632]{1,0:T(1,128)S(1)} %broadcast_in_dim.21.line_ref), custom_call_target="tpu_custom_call" | custom-call | flops 11010048 | bytes 5505024 | tf_op jit(solution)/shard_map/pallas_call | solution.py:242
  65.1 4.5 %shard_map.192 = (f32[2,128,512]{2,1,0:T(8,128)S(1)}, f32[2,1,512]{2,1,0:T(1,128)S(1)}, f32[2,1,512]{2,1,0:T(1,128)S(1)}) custom-call(s32[4]{0:T(128)S(1)} %copy-done.14, s32[4]{0:T(128)S(1)} %copy-done.15, s32[4]{0:T(128)S(1)} %copy-done.16, bf16[2,128,512]{2,1,0:T(8,128)(2,1)S(1)} %get-tuple-element.79.refs_3_, f32[2,128,5376]{2,1,0:T(8,128)S(1)} %shard_map.190.refs_4_, ...), custom_call_target="tpu_custom_call" | custom-call | flops 1610612736 | bytes 7077888 | tf_op jit(solution)/shard_map/pallas_call | solution.py:352
  69.6 5.9 %collective-permute-done.10.refs_5_.refs_6_ = bf16[512,256]{1,0:T(8,128)(2,1)S(1)} collective-permute-done((bf16[512,256]{1,0:T(8,128)(2,1)}, bf16[512,256]{1,0:T(8,128)(2,1)S(1)}, u32[]{:S(2)}, u32[]{:S(2)}) %collective-permute-start.10) | collective-permute-done | bytes 262176 | tf_op jit(solution)/shard_map/ppermute | solution.py:26
  82.7 2.7 %collective-permute-start.22 = (bf16[1024,256]{1,0:T(8,128)(2,1)S(1)}, bf16[1024,256]{1,0:T(8,128)(2,1)S(1)}, u32[]{:S(2)}, u32[]{:S(2)}) collective-permute-start(bf16[1024,256]{1,0:T(8,128)(2,1)S(1)} %shard_map.197.refs_0_), channel_id=1, source_target_pairs={{0,16},{8,24},{16,0},{24,8},{1,17},{9,25},{17,1},{25,9},{2,18},{10... | collective-permute-start | bytes 1572872 | tf_op jit(solution)/shard_map/ppermute | solution.py:26
  85.5 8.0 %collective-permute-start.15 = (bf16[64,1024]{1,0:T(8,128)(2,1)S(1)}, bf16[64,1024]{1,0:T(8,128)(2,1)S(1)}, u32[]{:S(2)}, u32[]{:S(2)}) collective-permute-start(bf16[64,1024]{1,0:T(8,128)(2,1)S(1)} %get-tuple-element.94), channel_id=1, source_target_pairs={{0,4},{1,5},{2,6},{3,7},{4,0},{5,1},{6,2},{7,3},{8,12},{9,13},{10,... | collective-permute-start | bytes 393224 | tf_op jit(solution)/shard_map/ppermute | solution.py:26
  94.1 8.1 %collective-permute-done.15.refs_3_ = bf16[64,1024]{1,0:T(8,128)(2,1)S(1)} collective-permute-done((bf16[64,1024]{1,0:T(8,128)(2,1)S(1)}, bf16[64,1024]{1,0:T(8,128)(2,1)S(1)}, u32[]{:S(2)}, u32[]{:S(2)}) %collective-permute-start.15) | collective-permute-done | bytes 131104 | tf_op jit(solution)/shard_map/ppermute | solution.py:26
  103.4 6.6 %collective-permute-done.30.refs_1_ = bf16[1120,256]{1,0:T(8,128)(2,1)S(1)} collective-permute-done((bf16[1120,256]{1,0:T(8,128)(2,1)S(1)}, bf16[1120,256]{1,0:T(8,128)(2,1)S(1)}, u32[]{:S(2)}, u32[]{:S(2)}) %collective-permute-start.30) | collective-permute-done | bytes 573472 | tf_op jit(solution)/shard_map/ppermute | solution.py:26
  110.2 8.1 %collective-permute-start.18 = (bf16[64,1024]{1,0:T(8,128)(2,1)S(1)}, bf16[64,1024]{1,0:T(8,128)(2,1)S(1)}, u32[]{:S(2)}, u32[]{:S(2)}) collective-permute-start(bf16[64,1024]{1,0:T(8,128)(2,1)S(1)} %get-tuple-element.98.refs_0_), channel_id=1, source_target_pairs={{0,4},{1,5},{2,6},{3,7},{4,0},{5,1},{6,2},{7,3},{8,12},{9,13},{10,... | collective-permute-start | bytes 393224 | tf_op jit(solution)/shard_map/ppermute | solution.py:26
  120.2 6.8 %collective-permute-done.18.refs_1_ = bf16[64,1024]{1,0:T(8,128)(2,1)S(1)} collective-permute-done((bf16[64,1024]{1,0:T(8,128)(2,1)S(1)}, bf16[64,1024]{1,0:T(8,128)(2,1)S(1)}, u32[]{:S(2)}, u32[]{:S(2)}) %collective-permute-start.18) | collective-permute-done | bytes 131104 | tf_op jit(solution)/shard_map/ppermute | solution.py:26
  127.0 3.3 %shard_map.200 = (bf16[64,1024]{1,0:T(8,128)(2,1)S(1)}, bf16[64,1024]{1,0:T(8,128)(2,1)S(1)}, bf16[64,1024]{1,0:T(8,128)(2,1)S(1)}, bf16[64,1024]{1,0:T(8,128)(2,1)S(1)}) custom-call(s32[4]{0:T(128)S(1)} %copy-done.14, s32[4]{0:T(128)S(1)} %copy-done.17, bf16[64,1024]{1,0:T(8,128)(2,1)S(1)} %get-tuple-element.98.refs_0_, ...), custom_call_target="tpu_custom_call" | custom-call | flops 536870912 | bytes 3670048 | tf_op jit(solution)/shard_map/pallas_call | solution.py:57
  132.1 2.6 %collective-permute-start.25 = (bf16[64,1024]{1,0:T(8,128)(2,1)S(1)}, bf16[64,1024]{1,0:T(8,128)(2,1)S(1)}, u32[]{:S(2)}, u32[]{:S(2)}) collective-permute-start(bf16[64,1024]{1,0:T(8,128)(2,1)S(1)} %get-tuple-element.109), channel_id=1, source_target_pairs={{0,6},{1,7},{2,4},{3,5},{4,2},{5,3},{6,0},{7,1},{8,14},{9,15},{10,... | collective-permute-start | bytes 393224 | tf_op jit(solution)/shard_map/ppermute | solution.py:26
  134.7 6.9 %collective-permute-done.24.refs_3_ = bf16[64,1024]{1,0:T(8,128)(2,1)S(1)} collective-permute-done((bf16[64,1024]{1,0:T(8,128)(2,1)S(1)}, bf16[64,1024]{1,0:T(8,128)(2,1)S(1)}, u32[]{:S(2)}, u32[]{:S(2)}) %collective-permute-start.24) | collective-permute-done | bytes 131104 | tf_op jit(solution)/shard_map/ppermute | solution.py:26
  142.9 2.2 %collective-permute-start.27 = (bf16[64,1024]{1,0:T(8,128)(2,1)S(1)}, bf16[64,1024]{1,0:T(8,128)(2,1)S(1)}, u32[]{:S(2)}, u32[]{:S(2)}) collective-permute-start(bf16[64,1024]{1,0:T(8,128)(2,1)S(1)} %get-tuple-element.112.refs_0_), channel_id=1, source_target_pairs={{0,4},{1,5},{2,6},{3,7},{4,0},{5,1},{6,2},{7,3},{8,12},{9,13},{10,... | collective-permute-start | bytes 393224 | tf_op jit(solution)/shard_map/ppermute | solution.py:26
  146.4 9.4 %collective-permute-done.27.refs_1_ = bf16[64,1024]{1,0:T(8,128)(2,1)S(1)} collective-permute-done((bf16[64,1024]{1,0:T(8,128)(2,1)S(1)}, bf16[64,1024]{1,0:T(8,128)(2,1)S(1)}, u32[]{:S(2)}, u32[]{:S(2)}) %collective-permute-start.27) | collective-permute-done | bytes 131104 | tf_op jit(solution)/shard_map/ppermute | solution.py:26
  158.4 2.3 %collective-permute-start.33 = (bf16[64,1024]{1,0:T(8,128)(2,1)S(1)}, bf16[64,1024]{1,0:T(8,128)(2,1)S(1)}, u32[]{:S(2)}, u32[]{:S(2)}) collective-permute-start(bf16[64,1024]{1,0:T(8,128)(2,1)S(1)} %get-tuple-element.118), channel_id=1, source_target_pairs={{0,4},{1,5},{2,6},{3,7},{4,0},{5,1},{6,2},{7,3},{8,12},{9,13},{10,... | collective-permute-start | bytes 393224 | tf_op jit(solution)/shard_map/ppermute | solution.py:26
  162.8 2.5 %shard_map.206 = bf16[4096,256]{1,0:T(8,128)(2,1)} custom-call(bf16[512,256]{1,0:T(8,128)(2,1)S(1)} %get-tuple-element.72.refs_6_.refs_0_, bf16[512,256]{1,0:T(8,128)(2,1)S(1)} %collective-permute-done.7.refs_9_.refs_1_, bf16[512,256]{1,0:T(8,128)(2,1)S(1)} %collective-permute-done.8.refs_7_.refs_2_, ...), custom_call_target="tpu_custom_call" | custom-call | bytes 4194304 | tf_op jit(solution)/shard_map/pallas_call | solution.py:57
  165.3 5.7 %collective-permute-done.33.refs_2_ = bf16[64,1024]{1,0:T(8,128)(2,1)S(1)} collective-permute-done((bf16[64,1024]{1,0:T(8,128)(2,1)S(1)}, bf16[64,1024]{1,0:T(8,128)(2,1)S(1)}, u32[]{:S(2)}, u32[]{:S(2)}) %collective-permute-start.33) | collective-permute-done | bytes 131104 | tf_op jit(solution)/shard_map/ppermute | solution.py:26
  177.5 7.2 %collective-permute-done.37.refs_2_ = bf16[64,1024]{1,0:T(8,128)(2,1)S(1)} collective-permute-done((bf16[64,1024]{1,0:T(8,128)(2,1)S(1)}, bf16[64,1024]{1,0:T(8,128)(2,1)S(1)}, u32[]{:S(2)}, u32[]{:S(2)}) %collective-permute-start.37) | collective-permute-done | bytes 131104 | tf_op jit(solution)/shard_map/ppermute | solution.py:26
  (146 shorter events, 61.7 us)
Async XLA Ops:
  7.8 14.3 %collective-permute-start.2 = (bf16[512,256]{1,0:T(8,128)(2,1)}, bf16[512,256]{1,0:T(8,128)(2,1)S(1)}, u32[]{:S(2)}, u32[]{:S(2)}) collective-permute-start(bf16[512,256]{1,0:T(8,128)(2,1)} %get-tuple-element.70), channel_id=1, source_target_pairs={{0,16},{8,24},{16,0},{24,8},{1,17},{9,25},{17,1},{25,9},{2,18},{10... | collective-permute-start | bytes 786440 | tf_op jit(solution)/shard_map/ppermute | solution.py:26
  9.3 12.8 %collective-permute-start.3 = (bf16[512,256]{1,0:T(8,128)(2,1)}, bf16[512,256]{1,0:T(8,128)(2,1)S(1)}, u32[]{:S(2)}, u32[]{:S(2)}) collective-permute-start(bf16[512,256]{1,0:T(8,128)(2,1)} %get-tuple-element.71), channel_id=1, source_target_pairs={{0,24},{8,16},{16,8},{24,0},{1,25},{9,17},{17,9},{25,1},{2,26},{10... | collective-permute-start | bytes 786440 | tf_op jit(solution)/shard_map/ppermute | solution.py:26
  24.2 15.1 %collective-permute-start.4 = (bf16[1024,256]{1,0:T(8,128)(2,1)}, bf16[1024,256]{1,0:T(8,128)(2,1)S(1)}, u32[]{:S(2)}, u32[]{:S(2)}) collective-permute-start(bf16[1024,256]{1,0:T(8,128)(2,1)} %get-tuple-element.73), channel_id=1, source_target_pairs={{0,8},{8,0},{16,24},{24,16},{1,9},{9,1},{17,25},{25,17},{2,10},{10... | collective-permute-start | bytes 1572872 | tf_op jit(solution)/shard_map/ppermute | solution.py:26
  25.5 27.5 %collective-permute-start.5 = (bf16[1024,256]{1,0:T(8,128)(2,1)}, bf16[1024,256]{1,0:T(8,128)(2,1)S(1)}, u32[]{:S(2)}, u32[]{:S(2)}) collective-permute-start(bf16[1024,256]{1,0:T(8,128)(2,1)} %get-tuple-element.75), channel_id=1, source_target_pairs={{0,16},{8,24},{16,0},{24,8},{1,17},{9,25},{17,1},{25,9},{2,18},{10... | collective-permute-start | bytes 1572872 | tf_op jit(solution)/shard_map/ppermute | solution.py:26
  26.3 26.7 %collective-permute-start.6 = (bf16[1024,256]{1,0:T(8,128)(2,1)}, bf16[1024,256]{1,0:T(8,128)(2,1)S(1)}, u32[]{:S(2)}, u32[]{:S(2)}) collective-permute-start(bf16[1024,256]{1,0:T(8,128)(2,1)} %get-tuple-element.77), channel_id=1, source_target_pairs={{0,24},{8,16},{16,8},{24,0},{1,25},{9,17},{17,9},{25,1},{2,26},{10... | collective-permute-start | bytes 1572872 | tf_op jit(solution)/shard_map/ppermute | solution.py:26
  28.4 20.4 %collective-permute-start.8 = (bf16[512,256]{1,0:T(8,128)(2,1)}, bf16[512,256]{1,0:T(8,128)(2,1)S(1)}, u32[]{:S(2)}, u32[]{:S(2)}) collective-permute-start(bf16[512,256]{1,0:T(8,128)(2,1)} %copy-done.20), channel_id=1, source_target_pairs={{0,4},{1,5},{2,6},{3,7},{4,0},{5,1},{6,2},{7,3},{8,12},{9,13},{10,... | collective-permute-start | bytes 786440 | tf_op jit(solution)/shard_map/ppermute | solution.py:26
  31.0 17.9 %collective-permute-start.9 = (bf16[512,256]{1,0:T(8,128)(2,1)}, bf16[512,256]{1,0:T(8,128)(2,1)S(1)}, u32[]{:S(2)}, u32[]{:S(2)}) collective-permute-start(bf16[512,256]{1,0:T(8,128)(2,1)} %copy-done.19), channel_id=1, source_target_pairs={{0,6},{1,7},{2,4},{3,5},{4,2},{5,3},{6,0},{7,1},{8,14},{9,15},{10,... | collective-permute-start | bytes 786440 | tf_op jit(solution)/shard_map/ppermute | solution.py:26
  39.3 13.6 %collective-permute-start.7 = (bf16[512,256]{1,0:T(8,128)(2,1)}, bf16[512,256]{1,0:T(8,128)(2,1)S(1)}, u32[]{:S(2)}, u32[]{:S(2)}) collective-permute-start(bf16[512,256]{1,0:T(8,128)(2,1)} %copy-done.18), channel_id=1, source_target_pairs={{0,2},{1,3},{2,0},{3,1},{4,6},{5,7},{6,4},{7,5},{8,10},{9,11},{10,... | collective-permute-start | bytes 786440 | tf_op jit(solution)/shard_map/ppermute | solution.py:26
  53.9 21.6 %collective-permute-start.10 = (bf16[512,256]{1,0:T(8,128)(2,1)}, bf16[512,256]{1,0:T(8,128)(2,1)S(1)}, u32[]{:S(2)}, u32[]{:S(2)}) collective-permute-start(bf16[512,256]{1,0:T(8,128)(2,1)} %get-tuple-element.85), channel_id=1, source_target_pairs={{0,4},{1,5},{2,6},{3,7},{4,0},{5,1},{6,2},{7,3},{8,12},{9,13},{10,... | collective-permute-start | bytes 786440 | tf_op jit(solution)/shard_map/ppermute | solution.py:26
  56.9 18.6 %collective-permute-start.11 = (bf16[512,256]{1,0:T(8,128)(2,1)}, bf16[512,256]{1,0:T(8,128)(2,1)}, u32[]{:S(2)}, u32[]{:S(2)}) collective-permute-start(bf16[512,256]{1,0:T(8,128)(2,1)} %get-tuple-element.86), channel_id=1, source_target_pairs={{0,6},{1,7},{2,4},{3,5},{4,2},{5,3},{6,0},{7,1},{8,14},{9,15},{10,... | collective-permute-start | bytes 786440 | tf_op jit(solution)/shard_map/ppermute | solution.py:26
  57.7 18.6 %collective-permute-start.12 = (bf16[512,256]{1,0:T(8,128)(2,1)}, bf16[512,256]{1,0:T(8,128)(2,1)}, u32[]{:S(2)}, u32[]{:S(2)}) collective-permute-start(bf16[512,256]{1,0:T(8,128)(2,1)} %get-tuple-element.87), channel_id=1, source_target_pairs={{0,2},{1,3},{2,0},{3,1},{4,6},{5,7},{6,4},{7,5},{8,10},{9,11},{10,... | collective-permute-start | bytes 786440 | tf_op jit(solution)/shard_map/ppermute | solution.py:26
  62.3 17.0 %collective-permute-start.14 = (bf16[512,256]{1,0:T(8,128)(2,1)S(1)}, bf16[512,256]{1,0:T(8,128)(2,1)S(1)}, u32[]{:S(2)}, u32[]{:S(2)}) collective-permute-start(bf16[512,256]{1,0:T(8,128)(2,1)S(1)} %shard_map.194.refs_2_), channel_id=1, source_target_pairs={{0,1},{1,0},{2,3},{3,2},{4,5},{5,4},{6,7},{7,6},{8,9},{9,8},{10,11... | collective-permute-start | bytes 786440 | tf_op jit(solution)/shard_map/ppermute | solution.py:26
  82.7 20.5 %collective-permute-start.22 = (bf16[1024,256]{1,0:T(8,128)(2,1)S(1)}, bf16[1024,256]{1,0:T(8,128)(2,1)S(1)}, u32[]{:S(2)}, u32[]{:S(2)}) collective-permute-start(bf16[1024,256]{1,0:T(8,128)(2,1)S(1)} %shard_map.197.refs_0_), channel_id=1, source_target_pairs={{0,16},{8,24},{16,0},{24,8},{1,17},{9,25},{17,1},{25,9},{2,18},{10... | collective-permute-start | bytes 1572872 | tf_op jit(solution)/shard_map/ppermute | solution.py:26
  85.5 24.5 %collective-permute-start.30 = (bf16[1120,256]{1,0:T(8,128)(2,1)S(1)}, bf16[1120,256]{1,0:T(8,128)(2,1)S(1)}, u32[]{:S(2)}, u32[]{:S(2)}) collective-permute-start(bf16[1120,256]{1,0:T(8,128)(2,1)S(1)} %copy-done.4), channel_id=1, source_target_pairs={{0,16},{8,24},{16,0},{24,8},{1,17},{9,25},{17,1},{25,9},{2,18},{10... | collective-permute-start | bytes 1720328 | tf_op jit(solution)/shard_map/ppermute | solution.py:26
  85.5 16.6 %collective-permute-start.15 = (bf16[64,1024]{1,0:T(8,128)(2,1)S(1)}, bf16[64,1024]{1,0:T(8,128)(2,1)S(1)}, u32[]{:S(2)}, u32[]{:S(2)}) collective-permute-start(bf16[64,1024]{1,0:T(8,128)(2,1)S(1)} %get-tuple-element.94), channel_id=1, source_target_pairs={{0,4},{1,5},{2,6},{3,7},{4,0},{5,1},{6,2},{7,3},{8,12},{9,13},{10,... | collective-permute-start | bytes 393224 | tf_op jit(solution)/shard_map/ppermute | solution.py:26
  103.3 15.6 %collective-permute-start.23 = (bf16[2048,256]{1,0:T(8,128)(2,1)S(1)}, bf16[2048,256]{1,0:T(8,128)(2,1)S(1)}, u32[]{:S(2)}, u32[]{:S(2)}) collective-permute-start(bf16[2048,256]{1,0:T(8,128)(2,1)S(1)} %shard_map.198.refs_0_.refs_4_), channel_id=1, source_target_pairs={{0,1},{1,0},{2,3},{3,2},{4,5},{5,4},{6,7},{7,6},{8,9},{9,8},{10,11... | collective-permute-start | bytes 3145736 | tf_op jit(solution)/shard_map/ppermute | solution.py:26
  110.1 32.3 %collective-permute-start.31 = (bf16[2240,256]{1,0:T(8,128)(2,1)S(1)}, bf16[2240,256]{1,0:T(8,128)(2,1)S(1)}, u32[]{:S(2)}, u32[]{:S(2)}) collective-permute-start(bf16[2240,256]{1,0:T(8,128)(2,1)S(1)} %shard_map.202.refs_0_), channel_id=1, source_target_pairs={{0,8},{8,0},{16,24},{24,16},{1,9},{9,1},{17,25},{25,17},{2,10},{10... | collective-permute-start | bytes 3440648 | tf_op jit(solution)/shard_map/ppermute | solution.py:26
  110.2 16.8 %collective-permute-start.18 = (bf16[64,1024]{1,0:T(8,128)(2,1)S(1)}, bf16[64,1024]{1,0:T(8,128)(2,1)S(1)}, u32[]{:S(2)}, u32[]{:S(2)}) collective-permute-start(bf16[64,1024]{1,0:T(8,128)(2,1)S(1)} %get-tuple-element.98.refs_0_), channel_id=1, source_target_pairs={{0,4},{1,5},{2,6},{3,7},{4,0},{5,1},{6,2},{7,3},{8,12},{9,13},{10,... | collective-permute-start | bytes 393224 | tf_op jit(solution)/shard_map/ppermute | solution.py:26
  130.3 11.3 %collective-permute-start.24 = (bf16[64,1024]{1,0:T(8,128)(2,1)S(1)}, bf16[64,1024]{1,0:T(8,128)(2,1)S(1)}, u32[]{:S(2)}, u32[]{:S(2)}) collective-permute-start(bf16[64,1024]{1,0:T(8,128)(2,1)S(1)} %get-tuple-element.108), channel_id=1, source_target_pairs={{0,4},{1,5},{2,6},{3,7},{4,0},{5,1},{6,2},{7,3},{8,12},{9,13},{10,... | collective-permute-start | bytes 393224 | tf_op jit(solution)/shard_map/ppermute | solution.py:26
  142.6 14.1 %collective-permute-start.32 = (bf16[4480,256]{1,0:T(8,128)(2,1)S(1)}, bf16[4480,256]{1,0:T(8,128)(2,1)S(1)}, u32[]{:S(2)}, u32[]{:S(2)}) collective-permute-start(bf16[4480,256]{1,0:T(8,128)(2,1)S(1)} %shard_map.203.refs_4_), channel_id=1, source_target_pairs={{0,1},{1,0},{2,3},{3,2},{4,5},{5,4},{6,7},{7,6},{8,9},{9,8},{10,11... | collective-permute-start | bytes 6881288 | tf_op jit(solution)/shard_map/ppermute | solution.py:26
  142.9 12.9 %collective-permute-start.27 = (bf16[64,1024]{1,0:T(8,128)(2,1)S(1)}, bf16[64,1024]{1,0:T(8,128)(2,1)S(1)}, u32[]{:S(2)}, u32[]{:S(2)}) collective-permute-start(bf16[64,1024]{1,0:T(8,128)(2,1)S(1)} %get-tuple-element.112.refs_0_), channel_id=1, source_target_pairs={{0,4},{1,5},{2,6},{3,7},{4,0},{5,1},{6,2},{7,3},{8,12},{9,13},{10,... | collective-permute-start | bytes 393224 | tf_op jit(solution)/shard_map/ppermute | solution.py:26
  158.4 12.7 %collective-permute-start.33 = (bf16[64,1024]{1,0:T(8,128)(2,1)S(1)}, bf16[64,1024]{1,0:T(8,128)(2,1)S(1)}, u32[]{:S(2)}, u32[]{:S(2)}) collective-permute-start(bf16[64,1024]{1,0:T(8,128)(2,1)S(1)} %get-tuple-element.118), channel_id=1, source_target_pairs={{0,4},{1,5},{2,6},{3,7},{4,0},{5,1},{6,2},{7,3},{8,12},{9,13},{10,... | collective-permute-start | bytes 393224 | tf_op jit(solution)/shard_map/ppermute | solution.py:26
  173.1 11.6 %collective-permute-start.37 = (bf16[64,1024]{1,0:T(8,128)(2,1)S(1)}, bf16[64,1024]{1,0:T(8,128)(2,1)S(1)}, u32[]{:S(2)}, u32[]{:S(2)}) collective-permute-start(bf16[64,1024]{1,0:T(8,128)(2,1)S(1)} %shard_map.205.refs_0_), channel_id=1, source_target_pairs={{0,4},{1,5},{2,6},{3,7},{4,0},{5,1},{6,2},{7,3},{8,12},{9,13},{10,... | collective-permute-start | bytes 393224 | tf_op jit(solution)/shard_map/ppermute | solution.py:26
  174.0 10.8 %collective-permute-start.38 = (bf16[64,1024]{1,0:T(8,128)(2,1)S(1)}, bf16[64,1024]{1,0:T(8,128)(2,1)S(1)}, u32[]{:S(2)}, u32[]{:S(2)}) collective-permute-start(bf16[64,1024]{1,0:T(8,128)(2,1)S(1)} %shard_map.205.refs_0_), channel_id=1, source_target_pairs={{0,6},{1,7},{2,4},{3,5},{4,2},{5,3},{6,0},{7,1},{8,14},{9,15},{10,... | collective-permute-start | bytes 393224 | tf_op jit(solution)/shard_map/ppermute | solution.py:26
  (43 other events, 375.6 us)

commit v2 on v1

--- a/solution.py
+++ b/solution.py
@@ -60,7 +60,7 @@
         in_specs=[SMEM] * smem + [VMEM] * (len(operands) - smem),
         out_specs=[VMEM] * len(outs),
         scratch_shapes=list(scratch),
-        compiler_params=pltpu.CompilerParams(vmem_limit_bytes=32 << 20),
+        compiler_params=pltpu.CompilerParams(vmem_limit_bytes=8 << 20),
         cost_estimate=pl.CostEstimate(
             flops=flops, bytes_accessed=moved, transcendentals=transcendentals
         ),
@@ -88,11 +88,42 @@
     return local_call(functools.partial(place_kernel, order), parts, [out])[0]
 
 
+def stack_order(stride):
+    return lambda k: (lax.axis_index("req") // stride) % 2 ^ k
+
+
 def req_stack(value, moved, stride):
-    def order(k):
-        return (lax.axis_index("req") // stride) % 2 ^ k
-
-    return place([value, moved], order)
+    return place([value, moved], stack_order(stride))
+
+
+def req_split(values, moved, strides, rows):
+    ins, outs = [], []
+    for value, other, size in zip(values, moved, rows):
+        ins += [value, other]
+        outs += [shaped((2 * n, value.shape[1])) for n in (size, value.shape[0] - size)]
+    orders = [stack_order(stride) for stride in strides]
+    return local_call(functools.partial(split_kernel, orders), ins, outs)
+
+
+def double_place_kernel(orders, *refs):
+    ins, outs = refs[: 2 * len(orders)], refs[2 * len(orders) :]
+    for i, order in enumerate(orders):
+        place_kernel(order, *ins[2 * i : 2 * i + 2], outs[i])
+
+
+def req_stack_two(values, moved, strides):
+    ins, outs = [], []
+    for value, other in zip(values, moved):
+        ins += [value, other]
+        outs.append(shaped((2 * value.shape[0], value.shape[1])))
+    orders = [stack_order(stride) for stride in strides]
+    return local_call(functools.partial(double_place_kernel, orders), ins, outs)
+
+
+def gather_on(value, strides):
+    for stride in strides[1:-1]:
+        value = req_stack(value, xor_send(value, "req", stride), stride)
+    return value, xor_send(value, "req", strides[-1])
 
 
 def part_owner(part, strides):
@@ -117,24 +148,62 @@
     return head[:, :width], head[:, width:], value
 
 
+def beside(block, width):
+    return jnp.concatenate([block[:width], block[width:]], axis=1)
+
+
+def stacked(block, width):
+    return jnp.concatenate([block[:, :width], block[:, width:]], axis=0)
+
+
+def pack_cross_kernel(query, out, packed):
+    depth = query.shape[0]
+    packed[: depth // 2, :] = beside(query[...], depth // 2)
+    packed[depth // 2 :, :] = out[...]
+
+
 def pack_kernel(*refs):
-    q1, kv1, q2, kv2, ff, o1, o2, o3, first, mid, wide, wide_ref = refs
-    depth = q1.shape[0]
+    q1, kv1, kv2, ff, o1, o3, first, rest_a, rest_b, wide_ref = refs
+    depth, lanes = q1.shape[0], first.shape[1]
     done = depth + depth // 2
     pack_projection(q1, kv1, first, 0)
     first[done:, :] = o1[...]
-    pack_projection(q2, kv2, mid, 0)
-    mid[done:, :] = o2[...]
+    rest_a[: depth // 2, :] = beside(kv2[0], depth // 2)
+    rest_a[depth // 2 : depth, :] = beside(kv2[1], depth // 2)
     span = wide_ref.shape[1] // 2
     wide_ref[...] = jnp.zeros(wide_ref.shape, wide_ref.dtype)
     wide_ref[:, : ff.shape[2]] = ff[0]
     wide_ref[:, span : span + ff.shape[2]] = ff[1]
-    lanes = wide.shape[1]
-    for block in range(wide_ref.shape[1] // lanes):
-        wide[block * depth : (block + 1) * depth, :] = wide_ref[
-            :, block * lanes : (block + 1) * lanes
-        ]
-    wide[wide.shape[0] - o3.shape[0] :, :] = o3[...]
+    blocks = [wide_ref[:, at : at + lanes] for at in range(0, wide_ref.shape[1], lanes)]
+    count_a = rest_a.shape[0] // depth - 1
+    for i, block in enumerate(blocks):
+        out, at = (rest_a, i + 1) if i < count_a else (rest_b, i - count_a)
+        out[at * depth : (at + 1) * depth, :] = block
+    rest_b[rest_b.shape[0] - o3.shape[0] :, :] = o3[...]
+
+
+def weave_kernel(count, *refs):
+    parts, (rest_a, rest_b, out_a, out_b) = refs[:count], refs[count:]
+    width = parts[0].shape[1] // 2
+    half_depth = parts[0].shape[0] - width
+    for k in range(0, count, 2):
+        pair = [stacked(part[:half_depth, :], width) for part in parts[k : k + 2]]
+        out_a[k * half_depth : (k + 2) * half_depth, :] = jnp.concatenate(pair, axis=1)
+    for k, part in enumerate(parts):
+        out_b[k * width : (k + 1) * width, :] = part[half_depth:, :]
+    out_a[count * half_depth :, :] = rest_a[...]
+    out_b[count * width :, :] = rest_b[...]
+
+
+def split_kernel(orders, *refs):
+    ins, outs = refs[: 2 * len(orders)], refs[2 * len(orders) :]
+    for i, order in enumerate(orders):
+        head, tail = outs[2 * i : 2 * i + 2]
+        at = head.shape[0] // 2
+        for k, part in enumerate(ins[2 * i : 2 * i + 2]):
+            for out, rows in ((head, part[:at, :]), (tail, part[at:, :])):
+                size = rows.shape[0]
+                out[pl.ds(pl.multiple_of(order(k) * size, size), size), :] = rows
 
 
 def join_kernel(taken, first, *outs):
@@ -249,7 +318,7 @@
         ],
         out_specs=pl.BlockSpec((1, TILE, total), lambda h: (h, 0, 0)),
         scratch_shapes=[pltpu.VMEM(line.shape, F32)],
-        compiler_params=pltpu.CompilerParams(vmem_limit_bytes=32 << 20),
+        compiler_params=pltpu.CompilerParams(vmem_limit_bytes=8 << 20),
         cost_estimate=pl.CostEstimate(
             flops=8 * heads_dev * TILE * total,
             bytes_accessed=4 * heads_dev * TILE * total,
@@ -356,7 +425,7 @@
         out_specs=out_specs,
         out_shape=out_shape,
         scratch_shapes=scratch,
-        compiler_params=pltpu.CompilerParams(vmem_limit_bytes=40 << 20),
+        compiler_params=pltpu.CompilerParams(vmem_limit_bytes=16 << 20),
         cost_estimate=pl.CostEstimate(
             flops=4 * heads_dev * pair * rows * keys_all,
             bytes_accessed=2 * heads_dev * pair * keys_all + 4 * band.size,
@@ -406,14 +475,58 @@
     return total + moved
 
 
-def norm_kernel(which, count, *refs):
-    gain_ref, residual_ref = refs[:2]
-    parts, (total_ref, normed_ref) = refs[2 : 2 + count], refs[2 + count :]
+def norm_rows(total, gain):
+    mean_square = jnp.mean(total * total, axis=-1, keepdims=True)
+    return (total * lax.rsqrt(mean_square + EPSILON) * gain).astype(BF16)
+
+
+def query_kernel(owners, count, *refs):
+    gain_ref, residual_ref, refs = refs[0], refs[1], refs[2:]
+    parts, weights, (total_ref, *outs) = refs[:count], refs[count : count + 2], refs[count + 2 :]
     total = sum_rows(parts, residual_ref)
     total_ref[...] = total
-    mean_square = jnp.mean(total * total, axis=-1, keepdims=True)
-    normed = total * lax.rsqrt(mean_square + EPSILON) * gain_ref[which : which + 1, :]
-    normed_ref[...] = normed.astype(BF16)
+    normed = norm_rows(total, gain_ref[1:2, :])
+    depth = normed.shape[1] // len(owners)
+    stride = weights[0].shape[0] // len(owners)
+    width = outs[0].shape[1] // 2
+    for pair in range(count // 2):
+        found = []
+        for w in weights:
+            query = 0.0
+            for part, owner in enumerate(owners):
+                at = part * stride + pair * depth
+                query = query + jnp.dot(
+                    normed[:, owner * depth : (owner + 1) * depth],
+                    w[at : at + depth, :],
+                    preferred_element_type=F32,
+                )
+            found.append(query)
+        for k in range(2):
+            own = slice(k * width, (k + 1) * width)
+            both = jnp.concatenate([query[:, own] for query in found], axis=1)
+            outs[2 * pair + k][...] = both.astype(BF16)
+
+
+def cross_out_kernel(owners, count, *refs):
+    gain_ref, residual_ref, refs = refs[0], refs[1], refs[2:]
+    blocks, weights, (total_ref, normed_ref) = (
+        refs[:count], refs[count : count + 2], refs[count + 2 :],
+    )
+    width = blocks[0].shape[1] // 2
+    stride = weights[0].shape[0] // len(owners)
+    lanes = weights[0].shape[1]
+    for part, owner in enumerate(owners):
+        total = 0.0
+        for i, w in enumerate(weights):
+            left = [block[:, i * width : (i + 1) * width] for block in blocks]
+            total = total + jnp.dot(
+                jnp.concatenate(left, axis=1),
+                w[part * stride : part * stride + count * width, :],
+                preferred_element_type=F32,
+            )
+        cols = slice(owner * lanes, (owner + 1) * lanes)
+        total_ref[:, cols] = residual_ref[:, cols] + total
+    normed_ref[...] = norm_rows(total_ref[...], gain_ref[2:3, :])
 
 
 def sum_kernel(*refs):
@@ -437,43 +550,33 @@
     weights, outs = refs[:2], refs[2:]
     width = outs[0].shape[1]
     depth = rows_ref.shape[1] // len(owners)
-    for i, weight in enumerate(weights):
+    for core, weight in enumerate(weights):
         stride = weight.shape[0] // len(owners)
-        key, value = 0.0, 0.0
-        for part, owner in enumerate(owners):
-            rows = rows_ref[:, owner * depth : (owner + 1) * depth]
-            _, w_key, w_value = packed_projection(weight, part * stride, depth, width)
-            key = key + jnp.dot(rows, w_key, preferred_element_type=F32)
-            value = value + jnp.dot(rows, w_value, preferred_element_type=F32)
-        outs[i][...] = key.astype(BF16)
-        outs[2 + i][...] = value.astype(BF16)
-
-
-def cross_kernel(owners, count, heads_dev, order_ref, enc_ref, *refs):
-    blocks, refs = refs[:count], refs[count:]
-    w_mid, keys, values = refs[0:2], refs[2:4], refs[4:6]
-    outs, (rows_ref, partial_ref) = refs[6:-2], refs[-2:]
+        for i in range(2):
+            total = 0.0
+            for part, owner in enumerate(owners):
+                rows = rows_ref[:, owner * depth : (owner + 1) * depth]
+                at = (part + 1) * stride - depth + i * (depth // 2)
+                block = stacked(weight[at : at + depth // 2, :], width)
+                total = total + jnp.dot(rows, block, preferred_element_type=F32)
+            outs[2 * i + core][...] = total.astype(BF16)
+
+
+def cross_kernel(count, heads_dev, order_ref, enc_ref, *refs):
+    blocks, keys, values = refs[:count], refs[count : count + 2], refs[count + 2 : count + 4]
+    outs, rows_ref = refs[count + 4 : -1], refs[-1]
     fill_rows(blocks, rows_ref)
     width = heads_dev * HD
-    depth = rows_ref.shape[1] // len(owners)
-    stride = w_mid[0].shape[0] // len(owners)
     enc_len = enc_ref[order_ref[lax.axis_index("req")]]
     contexts = []
-    for w, key_ref, value_ref in zip(w_mid, keys, values):
-        query = 0.0
-        for part, owner in enumerate(owners):
-            query = query + lax.dot_general(
-                w[part * stride : part * stride + depth, :width],
-                rows_ref[:, owner * depth : (owner + 1) * depth],
-                (((0,), (1,)), ((), ())),
-                preferred_element_type=F32,
-            )
-        query = query.astype(BF16)
-        head_of = lax.broadcasted_iota(jnp.int32, query.shape, 0) // HD
-        pieces = []
+    for core, (key_ref, value_ref) in enumerate(zip(keys, values)):
+        query = rows_ref[:, core * width : (core + 1) * width]
+        head_of = lax.broadcasted_iota(jnp.int32, query.shape, 1) // HD
         for head in range(heads_dev):
             own_query = jnp.where(head_of == head, query, jnp.zeros_like(query))
-            scores = jnp.dot(key_ref[...], own_query, preferred_element_type=F32)
+            scores = lax.dot_general(
+                key_ref[...], own_query, (((1,), (1,)), ((), ())), preferred_element_type=F32
+            )
             admitted = lax.broadcasted_iota(jnp.int32, scores.shape, 0) < enc_len
             scores = jnp.where(admitted, scores, NEG_FILL)
             weights = jnp.exp(scores - jnp.max(scores, axis=0, keepdims=True))
@@ -482,42 +585,50 @@
                 value_ref[...], weights.astype(BF16), (((0,), (0,)), ((), ())),
                 preferred_element_type=F32,
             )
-            pieces.append((context[head * HD : (head + 1) * HD, :] / norm).astype(BF16))
-        contexts.append(jnp.concatenate(pieces, axis=0))
-    project_out(contexts, w_mid, depth + depth // 2, width, owners, partial_ref)
-    hand_rows(outs, partial_ref)
-
-
-def ffn_kernel(owners, count, hidden_dev, *refs):
-    blocks, weights = refs[:count], refs[count : count + 2]
-    outs, (rows_ref, partial_ref) = refs[count + 2 : -2], refs[-2:]
+            contexts.append(context[head * HD : (head + 1) * HD, :] / norm)
+    context = jnp.concatenate(contexts, axis=0).T.astype(BF16)
+    for k, out in enumerate(outs):
+        size = out.shape[0]
+        out[...] = context[k * size : (k + 1) * size, :]
+
+
+def ffn_kernel(owners_a, owners_b, count, hidden_dev, *refs):
+    blocks, weights_a, weights_b = refs[:count], refs[count : count + 2], refs[count + 2 : count + 4]
+    outs, (rows_ref, partial_ref) = refs[count + 4 : -2], refs[-2:]
     fill_rows(blocks, rows_ref)
-    depth = rows_ref.shape[1] // len(owners)
-    stride = weights[0].shape[0] // len(owners)
-    blocks_in = (stride - hidden_dev) // depth
+    depth = rows_ref.shape[1] // len(owners_a)
+    stride_a = weights_a[0].shape[0] // len(owners_a)
+    stride_b = weights_b[0].shape[0] // len(owners_b)
     hiddens = []
-    for w in weights:
-        totals = [0.0] * blocks_in
-        for part, owner in enumerate(owners):
-            rows = rows_ref[:, owner * depth : (owner + 1) * depth]
-            for block in range(blocks_in):
-                at = part * stride + block * depth
-                totals[block] = totals[block] + jnp.dot(
-                    rows, w[at : at + depth, :], preferred_element_type=F32
-                )
+    for w_a, w_b in zip(weights_a, weights_b):
+        totals = []
+        for w, owners, stride, last in (
+            (w_a, owners_a, stride_a, stride_a),
+            (w_b, owners_b, stride_b, stride_b - hidden_dev),
+        ):
+            for block in range(last // depth):
+                total = 0.0
+                for part, owner in enumerate(owners):
+                    at = part * stride + block * depth
+                    total = total + jnp.dot(
+                        rows_ref[:, owner * depth : (owner + 1) * depth],
+                        w[at : at + depth, :],
+                        preferred_element_type=F32,
+                    )
+                totals.append(total)
         both = jnp.concatenate(totals, axis=1)
         span = both.shape[1] // 2
         hidden = jax.nn.gelu(both[:, :span], approximate=True) * both[:, span:]
         hiddens.append(hidden[:, :hidden_dev].astype(BF16))
-    width = weights[0].shape[1]
-    for part, owner in enumerate(owners):
+    lanes = weights_b[0].shape[1]
+    for part, owner in enumerate(owners_b):
         total = 0.0
-        for hidden, w in zip(hiddens, weights):
-            at = (part + 1) * stride - hidden_dev
+        for hidden, w in zip(hiddens, weights_b):
+            at = (part + 1) * stride_b - hidden_dev
             total = total + jnp.dot(
                 hidden, w[at : at + hidden_dev, :], preferred_element_type=F32
             )
-        partial_ref[:, owner * width : (owner + 1) * width] = total.astype(BF16)
+        partial_ref[:, owner * lanes : (owner + 1) * lanes] = total.astype(BF16)
     hand_rows(outs, partial_ref)
 
 
@@ -553,25 +664,45 @@
     down_strides = up_strides[::-1]
     down_owners = [part_owner(p, down_strides) for p in range(req_count)]
 
+    lanes = 2 * width_dev
+    cross = local_call(
+        pack_cross_kernel,
+        [cross_q, cross_out],
+        [shaped((depth // 2 + width_dev, lanes))],
+    )[0]
+    cross_parts = chip_sends([cross] * chips)
     tokens = cache_in.shape[1]
     *kept, given = cut_cache(cache_in, slot_order)
+    old_len = pick(cache_lengths, pick(slot_order, lax.axis_index("req")))
+    band = make_band(bucket_of, rel_bias, old_len, heads_dev, tokens * blk_count, rows)
     near_req = [kept[0]] + [xor_send(kept[k], "req", k) for k in range(1, req_count)]
-    taken = xor_send(given, "blk", 1)
-    lanes = 2 * width_dev
+    taken = xor_send(after(given, cross_parts[1]), "blk", 1)
     skip = depth + depth // 2
-    packed_in = [self_q, self_kv, cross_q, cross_kv, ff_in, self_out, cross_out, ff_out]
+    packed_in = [self_q, self_kv, cross_kv, ff_in, self_out, ff_out]
     packed_in = [jnp.moveaxis(w, 1, 0) if w.ndim == 3 else w for w in packed_in]
     packed_in[0] = after(packed_in[0], kept[0])
     wide_cols = 2 * TILE * -(-hidden_dev // TILE)
-    first, mid, wide = local_call(
+    blocks_in = wide_cols // lanes
+    blocks_a = -(-blocks_in // 2)
+    first, rest_a, rest_b = local_call(
         pack_kernel,
         packed_in,
         [
             shaped((skip + width_dev, lanes)),
-            shaped((skip + width_dev, lanes)),
-            shaped((depth * (wide_cols // lanes) + hidden_dev, lanes)),
+            shaped((depth + blocks_a * depth, lanes)),
+            shaped(((blocks_in - blocks_a) * depth + hidden_dev, lanes)),
         ],
         scratch=[pltpu.VMEM((depth, wide_cols), BF16)],
+    )
+
+    all_depth = chips * (depth // 2)
+    later_a, later_b = local_call(
+        functools.partial(weave_kernel, chips),
+        [*cross_parts, rest_a, rest_b],
+        [
+            shaped((all_depth + rest_a.shape[0], lanes)),
+            shaped((chips * width_dev + rest_b.shape[0], lanes)),
+        ],
     )
 
     joined = shaped((tokens + first.shape[0], taken.shape[1]))
@@ -580,12 +711,14 @@
         [taken, first],
         [shaped((tokens, taken.shape[1]))] + [joined] * (req_count - 1),
     )
-    near = list(turn([after(near_req[0], joined[0]), *near_req[1:]]))
+    near = list(turn([after(near_req[0], joined[0], later_a), *near_req[1:]]))
     far_req = [joined[0]]
-    far_req += [xor_send(after(joined[k], near[0]), "req", k) for k in range(1, req_count)]
+    far_req += [
+        xor_send(after(joined[k], near[0]), "req", k) for k in range(1, req_count)
+    ]
     near[1] = after(near[1], far_req[1])
     near = chip_sends(near)
-    far = turn([after(far_req[0], *near[1:]), *far_req[1:]])
+    far = turn([after(far_req[0], band, *near[1:]), *far_req[1:]])
     far = chip_sends(far)
 
     def token_order(i):
@@ -601,8 +734,6 @@
     )[0]
     w_self_out = (w_self_out, xor_send(w_self_out, "blk", 1))
 
-    old_len = pick(cache_lengths, pick(slot_order, lax.axis_index("req")))
-    band = make_band(bucket_of, rel_bias, old_len, heads_dev, tokens * blk_count, rows)
     query_t, fresh, residual = local_call(
         functools.partial(project_kernel, tokens, heads_dev),
         [new_states, norm_gain, first, *far_req[1:]],
@@ -628,15 +759,16 @@
         fresh=fresh,
     )
 
-    moved_mid = xor_send(after(mid, state[0], *far[1:]), "req", up_strides[0])
-    moved_wide = xor_send(after(wide, state[0], *far[1:]), "req", down_strides[0])
-
-    def gather_on(value, moved, strides, *hold):
-        value = req_stack(after(value, *hold), moved, strides[0])
-        for stride in strides[1:-1]:
-            value = req_stack(value, xor_send(value, "req", stride), stride)
-        return value, xor_send(value, "req", strides[-1])
-
+    moved_a = xor_send(after(later_a, far[0]), "req", up_strides[0])
+    moved_b = xor_send(after(later_b, far[0]), "req", down_strides[0])
+    w_query, w_wide, w_cross, w_down = req_split(
+        [after(later_a, state[0], *far[1:]), later_b],
+        [moved_a, moved_b],
+        [up_strides[0], down_strides[0]],
+        [all_depth + depth, chips * width_dev],
+    )
+    w_query, moved_a = gather_on(w_query, up_strides)
+    w_cross, moved_b = gather_on(w_cross, down_strides)
     context = self_attend(
         lens,
         query_t,
@@ -661,52 +793,64 @@
     )
 
 
-    mid, moved_mid = gather_on(mid, moved_mid, up_strides, parts[0])
-
-    def add_and_norm(which, residual, parts):
-        total, normed = local_call(
-            functools.partial(norm_kernel, which, chips),
-            [norm_gain, residual, *reordered(parts)],
-            [shaped((share, width), F32), shaped((share, width))],
-        )
-        return total, normed, chip_sends([normed] * chips)
-
     parts = chip_sends(parts)
-    residual, normed, blocks = add_and_norm(1, residual, parts)
-    w_mid = req_stack(after(mid, normed), moved_mid, up_strides[-1])
-    w_mid = (w_mid, xor_send(w_mid, "blk", 1))
-    wide, moved_wide = gather_on(wide, moved_wide, down_strides, normed)
-
+    last = [up_strides[-1], down_strides[-1]]
+    w_query, w_cross = req_stack_two(
+        [after(w_query, *parts[1:]), w_cross], [moved_a, moved_b], last
+    )
+    w_query = (w_query, xor_send(w_query, "blk", 1))
+    w_wide, moved_a = gather_on(after(w_wide, *parts[1:]), up_strides)
+    w_down, moved_b = gather_on(after(w_down, *parts[1:]), down_strides)
+    total, *queries = local_call(
+        functools.partial(query_kernel, range(req_count), chips),
+        [norm_gain, residual, *reordered(parts), *w_query],
+        [shaped((share, width), F32)] + [shaped((share, lanes))] * chips,
+        flops=2 * share * width * width,
+    )
+    residual = total
+    w_cross = (w_cross, xor_send(w_cross, "blk", 1))
     enc_rows = encoder_out.shape[0]
     pairs = local_call(
         functools.partial(pair_kernel, range(req_count)),
-        [encoder_out, *w_mid],
+        [encoder_out, *w_query],
         [shaped((enc_rows, width_dev))] * 4,
         flops=8 * enc_rows * width * width_dev,
     )
+    contexts = local_call(
+        functools.partial(cross_kernel, chips, heads_dev),
+        [slot_order, enc_lengths, *reordered(chip_sends(queries)), *pairs],
+        [shaped((share, lanes))] * chips,
+        smem=2,
+        scratch=[pltpu.VMEM((half, lanes), BF16)],
+        flops=8 * half * width_dev * heads_dev * enc_rows,
+        transcendentals=2 * heads_dev * half * enc_rows,
+    )
+    contexts = chip_sends(restored(contexts))
+
+    residual, normed = local_call(
+        functools.partial(cross_out_kernel, down_owners, chips),
+        [norm_gain, residual, *contexts, *w_cross],
+        [shaped((share, width), F32), shaped((share, width))],
+        flops=2 * share * width * width,
+    )
+    blocks = chip_sends([normed] * chips)
+    w_wide, w_down = req_stack_two([after(w_wide, normed), w_down], [moved_a, moved_b], last)
+    w_wide = (w_wide, xor_send(w_wide, "blk", 1))
+    w_down = (w_down, xor_send(w_down, "blk", 1))
+
     parts = local_call(
-        functools.partial(cross_kernel, range(req_count), chips, heads_dev),
-        [slot_order, enc_lengths, *reordered(blocks), *w_mid, *pairs],
-        parts_out,
-        smem=2,
-        scratch=[partial_ref, partial_ref],
-        flops=8 * half * width_dev * (width + heads_dev * enc_rows),
-        transcendentals=2 * heads_dev * half * enc_rows,
-    )
-    parts = chip_sends(restored(parts))
-    w_wide = req_stack(after(wide, *parts[1:]), moved_wide, down_strides[-1])
-    w_wide = (w_wide, xor_send(w_wide, "blk", 1))
-    residual, _, blocks = add_and_norm(2, residual, parts)
-
-    parts = local_call(
-        functools.partial(ffn_kernel, down_owners, chips, hidden_dev),
-        [*reordered(blocks), *w_wide],
+        functools.partial(ffn_kernel, range(req_count), down_owners, chips, hidden_dev),
+        [*reordered(blocks), *w_wide, *w_down],
         parts_out,
         scratch=[partial_ref, partial_ref],
         flops=12 * half * width * hidden_dev,
         transcendentals=2 * half * hidden_dev,
     )
-    final = local_call(sum_kernel, [residual, *reordered(chip_sends(restored(parts)))], [shaped((share, width))])[0]
+    final = local_call(
+        sum_kernel,
+        [residual, *reordered(chip_sends(restored(parts)))],
+        [shaped((share, width))],
+    )[0]
 
     same = chip_sends([after(final, cache_own)] * chips)
     both = same + [xor_send(part, "blk", 1) for part in same]

time: 189 us -> 194 us (1.026)
  waiting for transfers between devices: 88 us -> 69.8 us
  local copies, waits for them, and re-layouts: 10.4 us -> 27 us
  starting transfers between devices: 57.1 us -> 63.8 us
    ppermute x43 -> x50, waiting for transfers between devices: 88 us -> 69.8 us  [xor_send(): return lax.ppermute(value, axis, [(i, i ^ step) for i in range(size)])]
    unnamed x50 -> x100, local copies, waits for them, and re-layouts: 6.61 us -> 22.1 us
    ppermute x43 -> x50, starting transfers between devices: 57.1 us -> 63.8 us  [xor_send(): return lax.ppermute(value, axis, [(i, i ^ step) for i in range(size)])]
    pallas_call x20 -> x21, Pallas kernels: 17.1 us -> 19.5 us  [local_call(): pl.pallas_call(kernel, out_shape=list(outs), in_specs=[SMEM] * smem + [VM...]
  transfers between devices with their start and end apart: 43 -> 50, of which waited for: 23 -> 21; matrix products, arithmetic and copies ran while one was open for 3% -> 5% of each run, Pallas kernels for 11% -> 11%
where the time goes in v2:
time: 194 us; the launch traced here: 193 us
  waiting for transfers between devices  69.8 us (36%)
  starting transfers between devices  63.8 us (33%)
  Pallas kernels  27.6 us (14%)
  local copies, waits for them, and re-layouts  27 us (14%)
  between operations  3.14 us (2%)
    ppermute x50, waiting for transfers between devices, xor_send(): return lax.ppermute(value, axis, [(i, i ^ step) for i in range(size)])  69.8 us
    ppermute x50, starting transfers between devices, xor_send(): return lax.ppermute(value, axis, [(i, i ^ step) for i in range(size)])  63.8 us
    unnamed x100, local copies, waits for them, and re-layouts  22.1 us
    pallas_call x21, Pallas kernels, local_call(): pl.pallas_call(kernel, out_shape=list(outs), in_specs=[SMEM] * smem + [VM...  19.5 us
    pallas_call x2, Pallas kernels, self_attend(): pl.pallas_call(functools.partial(self_kernel, cache_len, places, first_ca...  4.24 us
    pallas_call x1, Pallas kernels, make_band(): pl.pallas_call(functools.partial(band_kernel, heads_dev, (wide_old, wide_...  3.89 us
  transfers between devices with their start and end apart: 50, of which 21 were waited for; matrix products, arithmetic and copies ran while one was open for 5% of the time, Pallas kernels for 11%

profile of v2, /device:TPU:0, one launch (start us, length us, event | category | flops | bytes accessed | tf_op | source)
XLA Modules:
  0.0 193.3 jit_solution(4087064108393748531)
XLA Ops:
  2.3 3.1 %collective-permute-start = (bf16[256,256]{1,0:T(8,128)(2,1)S(1)}, bf16[256,256]{1,0:T(8,128)(2,1)S(1)}, u32[]{:S(2)}, u32[]{:S(2)}) collective-permute-start(bf16[256,256]{1,0:T(8,128)(2,1)S(1)} %shard_map.187.refs_0_), channel_id=1, source_target_pairs={{0,2},{1,3},{2,0},{3,1},{4,6},{5,7},{6,4},{7,5},{8,10},{9,11},{10,... | collective-permute-start | bytes 393224 | tf_op jit(solution)/shard_map/ppermute | solution.py:26
  9.6 3.1 %collective-permute-start.3 = (bf16[256,256]{1,0:T(8,128)(2,1)S(1)}, bf16[256,256]{1,0:T(8,128)(2,1)S(1)}, u32[]{:S(2)}, u32[]{:S(2)}) collective-permute-start(bf16[256,256]{1,0:T(8,128)(2,1)S(1)} %shard_map.187.refs_0_), channel_id=1, source_target_pairs={{0,6},{1,7},{2,4},{3,5},{4,2},{5,3},{6,0},{7,1},{8,14},{9,15},{10,... | collective-permute-start | bytes 393224 | tf_op jit(solution)/shard_map/ppermute | solution.py:26
  17.4 3.5 %collective-permute-start.2 = (bf16[256,256]{1,0:T(8,128)(2,1)S(1)}, bf16[256,256]{1,0:T(8,128)(2,1)S(1)}, u32[]{:S(2)}, u32[]{:S(2)}) collective-permute-start(bf16[256,256]{1,0:T(8,128)(2,1)S(1)} %shard_map.187.refs_0_), channel_id=1, source_target_pairs={{0,4},{1,5},{2,6},{3,7},{4,0},{5,1},{6,2},{7,3},{8,12},{9,13},{10,... | collective-permute-start | bytes 393224 | tf_op jit(solution)/shard_map/ppermute | solution.py:26
  21.1 5.9 %collective-permute-done.2.refs_2_ = bf16[256,256]{1,0:T(8,128)(2,1)S(1)} collective-permute-done((bf16[256,256]{1,0:T(8,128)(2,1)S(1)}, bf16[256,256]{1,0:T(8,128)(2,1)S(1)}, u32[]{:S(2)}, u32[]{:S(2)}) %collective-permute-start.2) | collective-permute-done | bytes 131104 | tf_op jit(solution)/shard_map/ppermute | solution.py:26
  37.6 2.3 %collective-permute-start.12 = (bf16[512,256]{1,0:T(8,128)(2,1)}, bf16[512,256]{1,0:T(8,128)(2,1)S(1)}, u32[]{:S(2)}, u32[]{:S(2)}) collective-permute-start(bf16[512,256]{1,0:T(8,128)(2,1)} %copy-done.44), channel_id=1, source_target_pairs={{0,6},{1,7},{2,4},{3,5},{4,2},{5,3},{6,0},{7,1},{8,14},{9,15},{10,... | collective-permute-start | bytes 786440 | tf_op jit(solution)/shard_map/ppermute | solution.py:26
  39.8 7.3 %collective-permute-done.7.refs_0_.refs_1_ = bf16[1024,256]{1,0:T(8,128)(2,1)S(1)} collective-permute-done((bf16[1024,256]{1,0:T(8,128)(2,1)}, bf16[1024,256]{1,0:T(8,128)(2,1)S(1)}, u32[]{:S(2)}, u32[]{:S(2)}) %collective-permute-start.7) | collective-permute-done | bytes 524320 | tf_op jit(solution)/shard_map/ppermute | solution.py:26
  54.7 3.9 %shard_map.192.refs_4_ = f32[2,128,5376]{2,1,0:T(8,128)S(1)} custom-call(f32[32,16]{1,0:T(8,128)S(1)} %copy.23.bias_ref, s32[1,5632]{1,0:T(1,128)S(1)} %broadcast_in_dim.21.line_ref), custom_call_target="tpu_custom_call" | custom-call | flops 11010048 | bytes 5505024 | tf_op jit(solution)/shard_map/pallas_call | solution.py:311
  58.7 2.0 %collective-permute-done.10.refs_9_.refs_1_ = bf16[512,256]{1,0:T(8,128)(2,1)S(1)} collective-permute-done((bf16[512,256]{1,0:T(8,128)(2,1)}, bf16[512,256]{1,0:T(8,128)(2,1)S(1)}, u32[]{:S(2)}, u32[]{:S(2)}) %collective-permute-start.10) | collective-permute-done | bytes 262176 | tf_op jit(solution)/shard_map/ppermute | solution.py:26
  69.2 3.3 %shard_map.194 = (f32[2,128,512]{2,1,0:T(8,128)S(1)}, f32[2,1,512]{2,1,0:T(1,128)S(1)}, f32[2,1,512]{2,1,0:T(1,128)S(1)}) custom-call(s32[4]{0:T(128)S(1)} %copy-done.29, s32[4]{0:T(128)S(1)} %copy-done.37, s32[4]{0:T(128)S(1)} %copy-done.39, bf16[2,128,512]{2,1,0:T(8,128)(2,1)S(1)} %get-tuple-element.98.refs_3_, f32[2,128,5376]{2,1,0:T(8,128)S(1)} %shard_map.192.refs_4_, ...), custom_call_target="tpu_custom_call" | custom-call | flops 1610612736 | bytes 7077888 | tf_op jit(solution)/shard_map/pallas_call | solution.py:421
  72.5 2.4 %copy-done = f32[2,128,5376]{2,1,0:T(8,128)} copy-done((f32[2,128,5376]{2,1,0:T(8,128)}, f32[2,128,5376]{2,1,0:T(8,128)S(1)}, u32[]{:S(2)}) %copy-start) | copy-done | bytes 5505048
  74.9 9.7 %collective-permute-done.13.refs_5_.refs_6_ = bf16[512,256]{1,0:T(8,128)(2,1)S(1)} collective-permute-done((bf16[512,256]{1,0:T(8,128)(2,1)S(1)}, bf16[512,256]{1,0:T(8,128)(2,1)S(1)}, u32[]{:S(2)}, u32[]{:S(2)}) %collective-permute-start.13) | collective-permute-done | bytes 262176 | tf_op jit(solution)/shard_map/ppermute | solution.py:26
  87.9 2.6 %copy-done.1 = f32[2,128,5376]{2,1,0:T(8,128)S(1)} copy-done((f32[2,128,5376]{2,1,0:T(8,128)S(1)}, f32[2,128,5376]{2,1,0:T(8,128)}, u32[]{:S(2)}) %copy-start.1) | copy-done | bytes 5505048
  101.6 6.5 %collective-permute-start.18 = (bf16[64,1024]{1,0:T(8,128)(2,1)S(1)}, bf16[64,1024]{1,0:T(8,128)(2,1)S(1)}, u32[]{:S(2)}, u32[]{:S(2)}) collective-permute-start(bf16[64,1024]{1,0:T(8,128)(2,1)S(1)} %get-tuple-element.113), channel_id=1, source_target_pairs={{0,4},{1,5},{2,6},{3,7},{4,0},{5,1},{6,2},{7,3},{8,12},{9,13},{10,... | collective-permute-start | bytes 393224 | tf_op jit(solution)/shard_map/ppermute | solution.py:26
  110.0 8.1 %collective-permute-done.18.refs_3_ = bf16[64,1024]{1,0:T(8,128)(2,1)S(1)} collective-permute-done((bf16[64,1024]{1,0:T(8,128)(2,1)S(1)}, bf16[64,1024]{1,0:T(8,128)(2,1)S(1)}, u32[]{:S(2)}, u32[]{:S(2)}) %collective-permute-start.18) | collective-permute-done | bytes 131104 | tf_op jit(solution)/shard_map/ppermute | solution.py:26
  121.6 4.0 %collective-permute-start.37 = (bf16[1216,256]{1,0:T(8,128)(2,1)S(1)}, bf16[1216,256]{1,0:T(8,128)(2,1)S(1)}, u32[]{:S(2)}, u32[]{:S(2)}) collective-permute-start(bf16[1216,256]{1,0:T(8,128)(2,1)S(1)} %copy-done.14), channel_id=1, source_target_pairs={{0,8},{8,0},{16,24},{24,16},{1,9},{9,1},{17,25},{25,17},{2,10},{10... | collective-permute-start | bytes 1867784 | tf_op jit(solution)/shard_map/ppermute | solution.py:26
  126.5 2.5 %collective-permute-start.26 = (bf16[64,256]{1,0:T(8,128)(2,1)S(1)}, bf16[64,256]{1,0:T(8,128)(2,1)S(1)}, u32[]{:S(2)}, u32[]{:S(2)}) collective-permute-start(bf16[64,256]{1,0:T(8,128)(2,1)S(1)} %get-tuple-element.126), channel_id=1, source_target_pairs={{0,4},{1,5},{2,6},{3,7},{4,0},{5,1},{6,2},{7,3},{8,12},{9,13},{10,... | collective-permute-start | bytes 98312 | tf_op jit(solution)/shard_map/ppermute | solution.py:26
  135.6 2.4 %shard_map.202 = (bf16[64,256]{1,0:T(8,128)(2,1)S(1)}, bf16[64,256]{1,0:T(8,128)(2,1)S(1)}, bf16[64,256]{1,0:T(8,128)(2,1)S(1)}, bf16[64,256]{1,0:T(8,128)(2,1)S(1)}) custom-call(s32[4]{0:T(128)S(1)} %copy-done.31, s32[4]{0:T(128)S(1)} %copy-done.46, bf16[64,256]{1,0:T(8,128)(2,1)S(1)} %get-tuple-element.125.refs_0_, ...), custom_call_target="tpu_custom_call" | custom-call | flops 268435456 | bytes 786464 | tf_op jit(solution)/shard_map/pallas_call | solution.py:57
  142.5 2.3 %collective-permute-done.30.refs_4_ = bf16[64,256]{1,0:T(8,128)(2,1)S(1)} collective-permute-done((bf16[64,256]{1,0:T(8,128)(2,1)S(1)}, bf16[64,256]{1,0:T(8,128)(2,1)S(1)}, u32[]{:S(2)}, u32[]{:S(2)}) %collective-permute-start.30) | collective-permute-done | bytes 32800 | tf_op jit(solution)/shard_map/ppermute | solution.py:26
  151.1 2.4 %collective-permute-done.35.refs_3_ = bf16[64,1024]{1,0:T(8,128)(2,1)S(1)} collective-permute-done((bf16[64,1024]{1,0:T(8,128)(2,1)S(1)}, bf16[64,1024]{1,0:T(8,128)(2,1)S(1)}, u32[]{:S(2)}, u32[]{:S(2)}) %collective-permute-start.35) | collective-permute-done | bytes 131104 | tf_op jit(solution)/shard_map/ppermute | solution.py:26
  153.6 3.3 %collective-permute-done.34.refs_2_ = bf16[64,1024]{1,0:T(8,128)(2,1)S(1)} collective-permute-done((bf16[64,1024]{1,0:T(8,128)(2,1)S(1)}, bf16[64,1024]{1,0:T(8,128)(2,1)S(1)}, u32[]{:S(2)}, u32[]{:S(2)}) %collective-permute-start.34) | collective-permute-done | bytes 131104 | tf_op jit(solution)/shard_map/ppermute | solution.py:26
  156.9 5.9 %collective-permute-done.33.refs_1_ = bf16[64,1024]{1,0:T(8,128)(2,1)S(1)} collective-permute-done((bf16[64,1024]{1,0:T(8,128)(2,1)S(1)}, bf16[64,1024]{1,0:T(8,128)(2,1)S(1)}, u32[]{:S(2)}, u32[]{:S(2)}) %collective-permute-start.33) | collective-permute-done | bytes 131104 | tf_op jit(solution)/shard_map/ppermute | solution.py:26
  169.4 5.4 %collective-permute-done.40.refs_2_ = bf16[64,1024]{1,0:T(8,128)(2,1)S(1)} collective-permute-done((bf16[64,1024]{1,0:T(8,128)(2,1)S(1)}, bf16[64,1024]{1,0:T(8,128)(2,1)S(1)}, u32[]{:S(2)}, u32[]{:S(2)}) %collective-permute-start.40) | collective-permute-done | bytes 131104 | tf_op jit(solution)/shard_map/ppermute | solution.py:26
  180.5 3.9 %collective-permute-done.45.refs_3_ = bf16[64,1024]{1,0:T(8,128)(2,1)S(1)} collective-permute-done((bf16[64,1024]{1,0:T(8,128)(2,1)S(1)}, bf16[64,1024]{1,0:T(8,128)(2,1)S(1)}, u32[]{:S(2)}, u32[]{:S(2)}) %collective-permute-start.45) | collective-permute-done | bytes 131104 | tf_op jit(solution)/shard_map/ppermute | solution.py:26
  184.4 6.4 %collective-permute-done.44.refs_2_ = bf16[64,1024]{1,0:T(8,128)(2,1)S(1)} collective-permute-done((bf16[64,1024]{1,0:T(8,128)(2,1)S(1)}, bf16[64,1024]{1,0:T(8,128)(2,1)S(1)}, u32[]{:S(2)}, u32[]{:S(2)}) %collective-permute-start.44) | collective-permute-done | bytes 131104 | tf_op jit(solution)/shard_map/ppermute | solution.py:26
  (211 shorter events, 88.0 us)
Async XLA Ops:
  9.6 19.2 %collective-permute-start.1 = (bf16[2048,256]{1,0:T(8,128)(2,1)}, bf16[2048,256]{1,0:T(8,128)(2,1)S(1)}, u32[]{:S(2)}, u32[]{:S(2)}) collective-permute-start(bf16[2048,256]{1,0:T(8,128)(2,1)} %get-tuple-element.81), channel_id=1, source_target_pairs={{0,1},{1,0},{2,3},{3,2},{4,5},{5,4},{6,7},{7,6},{8,9},{9,8},{10,11... | collective-permute-start | bytes 3145736 | tf_op jit(solution)/shard_map/ppermute | solution.py:26
  12.7 17.0 %collective-permute-start.4 = (bf16[512,256]{1,0:T(8,128)(2,1)}, bf16[512,256]{1,0:T(8,128)(2,1)S(1)}, u32[]{:S(2)}, u32[]{:S(2)}) collective-permute-start(bf16[512,256]{1,0:T(8,128)(2,1)} %get-tuple-element.88), channel_id=1, source_target_pairs={{0,8},{8,0},{16,24},{24,16},{1,9},{9,1},{17,25},{25,17},{2,10},{10... | collective-permute-start | bytes 786440 | tf_op jit(solution)/shard_map/ppermute | solution.py:26
  14.2 15.5 %collective-permute-start.5 = (bf16[512,256]{1,0:T(8,128)(2,1)}, bf16[512,256]{1,0:T(8,128)(2,1)S(1)}, u32[]{:S(2)}, u32[]{:S(2)}) collective-permute-start(bf16[512,256]{1,0:T(8,128)(2,1)} %get-tuple-element.89), channel_id=1, source_target_pairs={{0,16},{8,24},{16,0},{24,8},{1,17},{9,25},{17,1},{25,9},{2,18},{10... | collective-permute-start | bytes 786440 | tf_op jit(solution)/shard_map/ppermute | solution.py:26
  15.7 14.0 %collective-permute-start.6 = (bf16[512,256]{1,0:T(8,128)(2,1)}, bf16[512,256]{1,0:T(8,128)(2,1)S(1)}, u32[]{:S(2)}, u32[]{:S(2)}) collective-permute-start(bf16[512,256]{1,0:T(8,128)(2,1)} %get-tuple-element.90), channel_id=1, source_target_pairs={{0,24},{8,16},{16,8},{24,0},{1,25},{9,17},{17,9},{25,1},{2,26},{10... | collective-permute-start | bytes 786440 | tf_op jit(solution)/shard_map/ppermute | solution.py:26
  32.1 15.1 %collective-permute-start.7 = (bf16[1024,256]{1,0:T(8,128)(2,1)}, bf16[1024,256]{1,0:T(8,128)(2,1)S(1)}, u32[]{:S(2)}, u32[]{:S(2)}) collective-permute-start(bf16[1024,256]{1,0:T(8,128)(2,1)} %get-tuple-element.92), channel_id=1, source_target_pairs={{0,8},{8,0},{16,24},{24,16},{1,9},{9,1},{17,25},{25,17},{2,10},{10... | collective-permute-start | bytes 1572872 | tf_op jit(solution)/shard_map/ppermute | solution.py:26
  33.6 27.2 %collective-permute-start.8 = (bf16[1024,256]{1,0:T(8,128)(2,1)}, bf16[1024,256]{1,0:T(8,128)(2,1)S(1)}, u32[]{:S(2)}, u32[]{:S(2)}) collective-permute-start(bf16[1024,256]{1,0:T(8,128)(2,1)} %copy-done.42), channel_id=1, source_target_pairs={{0,16},{8,24},{16,0},{24,8},{1,17},{9,25},{17,1},{25,9},{2,18},{10... | collective-permute-start | bytes 1572872 | tf_op jit(solution)/shard_map/ppermute | solution.py:26
  35.1 25.6 %collective-permute-start.9 = (bf16[1024,256]{1,0:T(8,128)(2,1)}, bf16[1024,256]{1,0:T(8,128)(2,1)S(1)}, u32[]{:S(2)}, u32[]{:S(2)}) collective-permute-start(bf16[1024,256]{1,0:T(8,128)(2,1)} %copy-done.41), channel_id=1, source_target_pairs={{0,24},{8,16},{16,8},{24,0},{1,25},{9,17},{17,9},{25,1},{2,26},{10... | collective-permute-start | bytes 1572872 | tf_op jit(solution)/shard_map/ppermute | solution.py:26
  37.6 21.1 %collective-permute-start.11 = (bf16[512,256]{1,0:T(8,128)(2,1)}, bf16[512,256]{1,0:T(8,128)(2,1)S(1)}, u32[]{:S(2)}, u32[]{:S(2)}) collective-permute-start(bf16[512,256]{1,0:T(8,128)(2,1)} %copy-done.45), channel_id=1, source_target_pairs={{0,4},{1,5},{2,6},{3,7},{4,0},{5,1},{6,2},{7,3},{8,12},{9,13},{10,... | collective-permute-start | bytes 786440 | tf_op jit(solution)/shard_map/ppermute | solution.py:26
  37.6 21.1 %collective-permute-start.12 = (bf16[512,256]{1,0:T(8,128)(2,1)}, bf16[512,256]{1,0:T(8,128)(2,1)S(1)}, u32[]{:S(2)}, u32[]{:S(2)}) collective-permute-start(bf16[512,256]{1,0:T(8,128)(2,1)} %copy-done.44), channel_id=1, source_target_pairs={{0,6},{1,7},{2,4},{3,5},{4,2},{5,3},{6,0},{7,1},{8,14},{9,15},{10,... | collective-permute-start | bytes 786440 | tf_op jit(solution)/shard_map/ppermute | solution.py:26
  47.2 13.6 %collective-permute-start.10 = (bf16[512,256]{1,0:T(8,128)(2,1)}, bf16[512,256]{1,0:T(8,128)(2,1)S(1)}, u32[]{:S(2)}, u32[]{:S(2)}) collective-permute-start(bf16[512,256]{1,0:T(8,128)(2,1)} %copy-done.43), channel_id=1, source_target_pairs={{0,2},{1,3},{2,0},{3,1},{4,6},{5,7},{6,4},{7,5},{8,10},{9,11},{10,... | collective-permute-start | bytes 786440 | tf_op jit(solution)/shard_map/ppermute | solution.py:26
  60.9 23.8 %collective-permute-start.21 = (bf16[1280,256]{1,0:T(8,128)(2,1)S(1)}, bf16[1280,256]{1,0:T(8,128)(2,1)S(1)}, u32[]{:S(2)}, u32[]{:S(2)}) collective-permute-start(bf16[1280,256]{1,0:T(8,128)(2,1)S(1)} %copy-done.12), channel_id=1, source_target_pairs={{0,8},{8,0},{16,24},{24,16},{1,9},{9,1},{17,25},{25,17},{2,10},{10... | collective-permute-start | bytes 1966088 | tf_op jit(solution)/shard_map/ppermute | solution.py:26
  62.4 22.2 %collective-permute-start.22 = (bf16[1120,256]{1,0:T(8,128)(2,1)S(1)}, bf16[1120,256]{1,0:T(8,128)(2,1)S(1)}, u32[]{:S(2)}, u32[]{:S(2)}) collective-permute-start(bf16[1120,256]{1,0:T(8,128)(2,1)S(1)} %copy-done.16), channel_id=1, source_target_pairs={{0,16},{8,24},{16,0},{24,8},{1,17},{9,25},{17,1},{25,9},{2,18},{10... | collective-permute-start | bytes 1720328 | tf_op jit(solution)/shard_map/ppermute | solution.py:26
  63.9 20.7 %collective-permute-start.13 = (bf16[512,256]{1,0:T(8,128)(2,1)S(1)}, bf16[512,256]{1,0:T(8,128)(2,1)S(1)}, u32[]{:S(2)}, u32[]{:S(2)}) collective-permute-start(bf16[512,256]{1,0:T(8,128)(2,1)S(1)} %get-tuple-element.104), channel_id=1, source_target_pairs={{0,4},{1,5},{2,6},{3,7},{4,0},{5,1},{6,2},{7,3},{8,12},{9,13},{10,... | collective-permute-start | bytes 786440 | tf_op jit(solution)/shard_map/ppermute | solution.py:26
  65.6 19.0 %collective-permute-start.14 = (bf16[512,256]{1,0:T(8,128)(2,1)S(1)}, bf16[512,256]{1,0:T(8,128)(2,1)S(1)}, u32[]{:S(2)}, u32[]{:S(2)}) collective-permute-start(bf16[512,256]{1,0:T(8,128)(2,1)S(1)} %get-tuple-element.105), channel_id=1, source_target_pairs={{0,6},{1,7},{2,4},{3,5},{4,2},{5,3},{6,0},{7,1},{8,14},{9,15},{10,... | collective-permute-start | bytes 786440 | tf_op jit(solution)/shard_map/ppermute | solution.py:26
  67.5 17.1 %collective-permute-start.15 = (bf16[512,256]{1,0:T(8,128)(2,1)S(1)}, bf16[512,256]{1,0:T(8,128)(2,1)S(1)}, u32[]{:S(2)}, u32[]{:S(2)}) collective-permute-start(bf16[512,256]{1,0:T(8,128)(2,1)S(1)} %get-tuple-element.106), channel_id=1, source_target_pairs={{0,2},{1,3},{2,0},{3,1},{4,6},{5,7},{6,4},{7,5},{8,10},{9,11},{10,... | collective-permute-start | bytes 786440 | tf_op jit(solution)/shard_map/ppermute | solution.py:26
  85.9 33.2 %collective-permute-start.23 = (bf16[1536,256]{1,0:T(8,128)(2,1)}, bf16[1536,256]{1,0:T(8,128)(2,1)}, u32[]{:S(2)}, u32[]{:S(2)}) collective-permute-start(bf16[1536,256]{1,0:T(8,128)(2,1)} %get-tuple-element.121.refs_0_), channel_id=1, source_target_pairs={{0,16},{8,24},{16,0},{24,8},{1,17},{9,25},{17,1},{25,9},{2,18},{10... | collective-permute-start | bytes 2359304 | tf_op jit(solution)/shard_map/ppermute | solution.py:26
  86.4 32.7 %collective-permute-start.24 = (bf16[1024,256]{1,0:T(8,128)(2,1)}, bf16[1024,256]{1,0:T(8,128)(2,1)}, u32[]{:S(2)}, u32[]{:S(2)}) collective-permute-start(bf16[1024,256]{1,0:T(8,128)(2,1)} %get-tuple-element.122.refs_2_), channel_id=1, source_target_pairs={{0,8},{8,0},{16,24},{24,16},{1,9},{9,1},{17,25},{25,17},{2,10},{10... | collective-permute-start | bytes 1572872 | tf_op jit(solution)/shard_map/ppermute | solution.py:26
  101.6 16.5 %collective-permute-start.18 = (bf16[64,1024]{1,0:T(8,128)(2,1)S(1)}, bf16[64,1024]{1,0:T(8,128)(2,1)S(1)}, u32[]{:S(2)}, u32[]{:S(2)}) collective-permute-start(bf16[64,1024]{1,0:T(8,128)(2,1)S(1)} %get-tuple-element.113), channel_id=1, source_target_pairs={{0,4},{1,5},{2,6},{3,7},{4,0},{5,1},{6,2},{7,3},{8,12},{9,13},{10,... | collective-permute-start | bytes 393224 | tf_op jit(solution)/shard_map/ppermute | solution.py:26
  121.1 19.5 %collective-permute-start.32 = (bf16[2048,256]{1,0:T(8,128)(2,1)S(1)}, bf16[2048,256]{1,0:T(8,128)(2,1)S(1)}, u32[]{:S(2)}, u32[]{:S(2)}) collective-permute-start(bf16[2048,256]{1,0:T(8,128)(2,1)S(1)} %get-tuple-element.137.refs_6_), channel_id=1, source_target_pairs={{0,1},{1,0},{2,3},{3,2},{4,5},{5,4},{6,7},{7,6},{8,9},{9,8},{10,11... | collective-permute-start | bytes 3145736 | tf_op jit(solution)/shard_map/ppermute | solution.py:26
  121.6 25.3 %collective-permute-start.37 = (bf16[1216,256]{1,0:T(8,128)(2,1)S(1)}, bf16[1216,256]{1,0:T(8,128)(2,1)S(1)}, u32[]{:S(2)}, u32[]{:S(2)}) collective-permute-start(bf16[1216,256]{1,0:T(8,128)(2,1)S(1)} %copy-done.14), channel_id=1, source_target_pairs={{0,8},{8,0},{16,24},{24,16},{1,9},{9,1},{17,25},{25,17},{2,10},{10... | collective-permute-start | bytes 1867784 | tf_op jit(solution)/shard_map/ppermute | solution.py:26
  125.6 21.3 %collective-permute-start.36 = (bf16[1024,256]{1,0:T(8,128)(2,1)S(1)}, bf16[1024,256]{1,0:T(8,128)(2,1)S(1)}, u32[]{:S(2)}, u32[]{:S(2)}) collective-permute-start(bf16[1024,256]{1,0:T(8,128)(2,1)S(1)} %copy-done.20), channel_id=1, source_target_pairs={{0,16},{8,24},{16,0},{24,8},{1,17},{9,25},{17,1},{25,9},{2,18},{10... | collective-permute-start | bytes 1572872 | tf_op jit(solution)/shard_map/ppermute | solution.py:26
  147.1 15.7 %collective-permute-start.39 = (bf16[2432,256]{1,0:T(8,128)(2,1)S(1)}, bf16[2432,256]{1,0:T(8,128)(2,1)S(1)}, u32[]{:S(2)}, u32[]{:S(2)}) collective-permute-start(bf16[2432,256]{1,0:T(8,128)(2,1)S(1)} %get-tuple-element.146.refs_6_), channel_id=1, source_target_pairs={{0,1},{1,0},{2,3},{3,2},{4,5},{5,4},{6,7},{7,6},{8,9},{9,8},{10,11... | collective-permute-start | bytes 3735560 | tf_op jit(solution)/shard_map/ppermute | solution.py:26
  147.2 15.6 %collective-permute-start.38 = (bf16[2048,256]{1,0:T(8,128)(2,1)S(1)}, bf16[2048,256]{1,0:T(8,128)(2,1)S(1)}, u32[]{:S(2)}, u32[]{:S(2)}) collective-permute-start(bf16[2048,256]{1,0:T(8,128)(2,1)S(1)} %get-tuple-element.145.refs_4_), channel_id=1, source_target_pairs={{0,1},{1,0},{2,3},{3,2},{4,5},{5,4},{6,7},{7,6},{8,9},{9,8},{10,11... | collective-permute-start | bytes 3145736 | tf_op jit(solution)/shard_map/ppermute | solution.py:26
  149.7 13.1 %collective-permute-start.33 = (bf16[64,1024]{1,0:T(8,128)(2,1)S(1)}, bf16[64,1024]{1,0:T(8,128)(2,1)S(1)}, u32[]{:S(2)}, u32[]{:S(2)}) collective-permute-start(bf16[64,1024]{1,0:T(8,128)(2,1)S(1)} %get-tuple-element.139.refs_0_), channel_id=1, source_target_pairs={{0,4},{1,5},{2,6},{3,7},{4,0},{5,1},{6,2},{7,3},{8,12},{9,13},{10,... | collective-permute-start | bytes 393224 | tf_op jit(solution)/shard_map/ppermute | solution.py:26
  (75 other events, 487.4 us)

commit v3 on v2

--- a/solution.py
+++ b/solution.py
@@ -14,11 +14,6 @@
 TILE = 128
 F32 = jnp.float32
 BF16 = jnp.bfloat16
-
-
-def pick(table, place):
-    matches = place == jnp.arange(table.shape[0], dtype=jnp.int32)
-    return jnp.sum(jnp.where(matches, table, 0))
 
 
 def xor_send(value, axis, step):
@@ -172,8 +167,9 @@
     rest_a[depth // 2 : depth, :] = beside(kv2[1], depth // 2)
     span = wide_ref.shape[1] // 2
     wide_ref[...] = jnp.zeros(wide_ref.shape, wide_ref.dtype)
-    wide_ref[:, : ff.shape[2]] = ff[0]
-    wide_ref[:, span : span + ff.shape[2]] = ff[1]
+    for i in range(2):
+        block = ff[i].astype(F32).T.astype(BF16)
+        wide_ref[:, i * span : i * span + block.shape[1]] = block
     blocks = [wide_ref[:, at : at + lanes] for at in range(0, wide_ref.shape[1], lanes)]
     count_a = rest_a.shape[0] // depth - 1
     for i, block in enumerate(blocks):
@@ -280,51 +276,54 @@
     return local_call(functools.partial(turn_kernel, len(parts)), parts, outs)
 
 
-def band_kernel(heads_dev, widths, bias_ref, line_ref, out_ref, row_ref):
+def band_kernel(heads_dev, cache_len, widths, order_ref, old_ref, bias_ref, bucket_ref, *refs):
+    out_ref, line_ref, row_ref = refs
     head = lax.axis_index("blk") * heads_dev + pl.program_id(0)
-    buckets = line_ref[...]
-    row = jnp.zeros(buckets.shape, F32)
-    for bucket in range(bias_ref.shape[0]):
-        row = jnp.where(buckets == bucket, bias_ref[bucket, head], row)
-    row_ref[...] = row
+    old_len = old_ref[order_ref[lax.axis_index("req")]]
+    heads = lax.broadcasted_iota(jnp.int32, bias_ref.shape, 0)
+    bias = jnp.sum(jnp.where(heads == head, bias_ref[...], 0.0), axis=0, keepdims=True)
+    buckets = bucket_ref[...]
+    copies, size = line_ref.shape
+    line_ref[:, :cache_len] = jnp.broadcast_to(buckets[:, :1], (copies, cache_len))
+    line_ref[:, cache_len:] = jnp.broadcast_to(buckets, (copies, size - cache_len))
     start = 0
     done = 0
-    for width in widths:
+    rows = (widths[1] + TILE) // 2
+    for width, first in zip(widths, (old_len + 1, cache_len - rows + 1)):
+        turned = pltpu.roll(line_ref[...], size - first, 1)[:, : width + TILE]
+        row = jnp.zeros(turned.shape, F32)
+        for bucket in range(bias_ref.shape[1]):
+            row = jnp.where(turned == bucket, bias[:, bucket : bucket + 1], row)
+        row_ref[:, start : start + width + TILE] = row
         for u in range(0, width, TILE):
-            window = row_ref[:, start + u : start + u + 2 * TILE]
+            window = row_ref[0:1, start + u : start + u + 2 * TILE]
             wide = jnp.broadcast_to(window, (TILE, 2 * TILE))
-            turned = pltpu.roll(wide, TILE + 1, 1, stride=1, stride_axis=0)
-            out_ref[0, :, done + u : done + u + TILE] = turned[:, :TILE]
+            skewed = pltpu.roll(wide, TILE + 1, 1, stride=1, stride_axis=0)
+            out_ref[0, :, done + u : done + u + TILE] = skewed[:, :TILE]
         start += width + TILE
         done += width
 
 
-def make_band(bucket_of, rel_bias, old_len, heads_dev, cache_len, rows):
-    wide_old, wide_new = cache_len - TILE + rows, 2 * rows - TILE
-    low = jnp.broadcast_to(bucket_of[:1], (cache_len - 1,))
-    padded = jnp.concatenate([low, bucket_of, bucket_of[-1:]])
-    line_old = lax.dynamic_slice(padded, (old_len,), (wide_old + TILE,))
-    begin = cache_len - rows
-    line_new = padded[begin : begin + wide_new + TILE]
-    line = jnp.concatenate([line_old, line_new])[None, :]
-    total = wide_old + wide_new
+def make_band(bucket_of, rel_bias, slot_order, cache_lengths, heads_dev, cache_len, rows):
+    widths = (cache_len - TILE + rows, 2 * rows - TILE)
+    total = sum(widths)
     return pl.pallas_call(
-        functools.partial(band_kernel, heads_dev, (wide_old, wide_new)),
+        functools.partial(band_kernel, heads_dev, cache_len, widths),
         grid=(heads_dev,),
         out_shape=jax.ShapeDtypeStruct((heads_dev, TILE, total), F32),
-        in_specs=[
-            pl.BlockSpec(memory_space=pltpu.SMEM),
-            pl.BlockSpec(memory_space=pltpu.VMEM),
+        in_specs=[SMEM, SMEM, VMEM, VMEM],
+        out_specs=pl.BlockSpec((1, TILE, total), lambda h: (h, 0, 0)),
+        scratch_shapes=[
+            pltpu.VMEM((8, cache_len + bucket_of.shape[0]), jnp.int32),
+            pltpu.VMEM((8, total + 2 * TILE), F32),
         ],
-        out_specs=pl.BlockSpec((1, TILE, total), lambda h: (h, 0, 0)),
-        scratch_shapes=[pltpu.VMEM(line.shape, F32)],
-        compiler_params=pltpu.CompilerParams(vmem_limit_bytes=8 << 20),
+        compiler_params=pltpu.CompilerParams(vmem_limit_bytes=12 << 20),
         cost_estimate=pl.CostEstimate(
             flops=8 * heads_dev * TILE * total,
             bytes_accessed=4 * heads_dev * TILE * total,
             transcendentals=0,
         ),
-    )(rel_bias, line)
+    )(slot_order, cache_lengths, rel_bias.T, bucket_of[None, :])
 
 
 def self_kernel(cache_len, places, first_call, *refs):
@@ -334,7 +333,8 @@
     if first_call:
         fresh_ref, total_ref, top_ref, norm_ref, score_ref = refs
     else:
-        total_in, top_in, norm_in, out_ref, total_ref, top_ref, norm_ref, score_ref = refs
+        total_in, top_in, norm_in, kept_ref, given_ref = refs[:5]
+        total_ref, top_ref, norm_ref, score_ref = refs[5:]
     slot = order_ref[lax.axis_index("req")]
     old_len, new_len = old_ref[slot], new_ref[slot]
     rows = query_ref.shape[2]
@@ -391,7 +391,11 @@
             attend(block[...], cache_len - TILE - first, admit)
 
     if not first_call:
-        out_ref[0] = (total_ref[0, HD:, :] / norm_ref[0]).astype(BF16)
+        total_ref[0, :HD, :] = total_ref[0, HD:, :] / norm_ref[0]
+        half = rows // 2
+        for out_ref, core in ((kept_ref, lax.rem(blk, 2)), (given_ref, 1 - lax.rem(blk, 2))):
+            spot = pl.ds(pl.multiple_of(core * half, half), half)
+            out_ref[0] = total_ref[0, :HD, spot].astype(BF16)
 
 
 def self_attend(lens, query_t, band, blocks, places, cache_len, fresh=None, state=None):
@@ -414,8 +418,8 @@
     else:
         in_specs += [head_block(*shape) for shape in held]
         more = list(state)
-        out_specs = head_block(HD, rows)
-        out_shape = jax.ShapeDtypeStruct((heads_dev, HD, rows), BF16)
+        out_specs = [head_block(HD, rows // 2)] * 2
+        out_shape = [shaped((heads_dev, HD, rows // 2))] * 2
         scratch = [pltpu.VMEM((1,) + shape, F32) for shape in held] + [score]
     keys_all = count * tokens + (rows if first_call else 0)
     return pl.pallas_call(
@@ -654,7 +658,6 @@
 ):
     req_count, blk_count = lax.axis_size("req"), lax.axis_size("blk")
     chips = blk_count // 2
-    core = lax.axis_index("blk") % 2
     heads_dev = H // blk_count
     width_dev = heads_dev * HD
     rows, width = new_states.shape
@@ -673,13 +676,15 @@
     cross_parts = chip_sends([cross] * chips)
     tokens = cache_in.shape[1]
     *kept, given = cut_cache(cache_in, slot_order)
-    old_len = pick(cache_lengths, pick(slot_order, lax.axis_index("req")))
-    band = make_band(bucket_of, rel_bias, old_len, heads_dev, tokens * blk_count, rows)
+    band = make_band(
+        bucket_of, rel_bias, slot_order, cache_lengths, heads_dev, tokens * blk_count, rows
+    )
     near_req = [kept[0]] + [xor_send(kept[k], "req", k) for k in range(1, req_count)]
     taken = xor_send(after(given, cross_parts[1]), "blk", 1)
     skip = depth + depth // 2
     packed_in = [self_q, self_kv, cross_kv, ff_in, self_out, ff_out]
-    packed_in = [jnp.moveaxis(w, 1, 0) if w.ndim == 3 else w for w in packed_in]
+    packed_in[1], packed_in[2] = jnp.moveaxis(self_kv, 1, 0), jnp.moveaxis(cross_kv, 1, 0)
+    packed_in[3] = ff_in.transpose(1, 2, 0)
     packed_in[0] = after(packed_in[0], kept[0])
     wide_cols = 2 * TILE * -(-hidden_dev // TILE)
     blocks_in = wide_cols // lanes
@@ -769,7 +774,7 @@
     )
     w_query, moved_a = gather_on(w_query, up_strides)
     w_cross, moved_b = gather_on(w_cross, down_strides)
-    context = self_attend(
+    kept, given = self_attend(
         lens,
         query_t,
         band,
@@ -778,10 +783,8 @@
         cache_len,
         state=state,
     )
-    context = context.reshape(width_dev, rows)
-
-    kept = lax.dynamic_slice_in_dim(context, core * half, half, 1)
-    given = lax.dynamic_slice_in_dim(context, (1 - core) * half, half, 1)
+    kept, given = kept.reshape(width_dev, half), given.reshape(width_dev, half)
+
     parts_out = [shaped((share, width))] * chips
     partial_ref = pltpu.VMEM((half, width), BF16)
     parts = local_call(

time: 194 us -> 175 us (0.902)
  local copies, waits for them, and re-layouts: 27 us -> 4.07 us
  waiting for transfers between devices: 69.8 us -> 82.6 us
  Pallas kernels: 27.6 us -> 21.5 us
  between operations: 3.14 us -> 1.03 us
    unnamed x100 -> x38, local copies, waits for them, and re-layouts: 22.1 us -> 4.02 us
    ppermute x50, waiting for transfers between devices: 69.8 us -> 82.6 us  [xor_send(): return lax.ppermute(value, axis, [(i, i ^ step) for i in range(size)])]
    pallas_call x21, Pallas kernels: 19.5 us -> 13 us  [local_call(): pl.pallas_call(kernel, out_shape=list(outs), in_specs=[SMEM] * smem + [VM...]
    slice x2 -> x0, local copies, waits for them, and re-layouts: 2.73 us -> none  [the longest x1 1.38 us: make_band(): line_new = padded[begin:begin + wide_new + TILE]]
  transfers between devices with their start and end apart: 50 -> 50, of which waited for: 21 -> 25; matrix products, arithmetic and copies ran while one was open for 5% -> 0% of each run, Pallas kernels for 11% -> 10%
where the time goes in v3:
time: 175 us; the launch traced here: 174 us
  waiting for transfers between devices  82.6 us (47%)
  starting transfers between devices  64.3 us (37%)
  Pallas kernels  21.5 us (12%)
  local copies, waits for them, and re-layouts  4.07 us (2%)
    ppermute x50, waiting for transfers between devices, xor_send(): return lax.ppermute(value, axis, [(i, i ^ step) for i in range(size)])  82.6 us
    ppermute x50, starting transfers between devices, xor_send(): return lax.ppermute(value, axis, [(i, i ^ step) for i in range(size)])  64.3 us
    pallas_call x21, Pallas kernels, local_call(): pl.pallas_call(kernel, out_shape=list(outs), in_specs=[SMEM] * smem + [VM...  13 us
    pallas_call x2, Pallas kernels, self_attend(): pl.pallas_call(functools.partial(self_kernel, cache_len, places, first_ca...  4.27 us
    pallas_call x1, Pallas kernels, make_band(): pl.pallas_call(functools.partial(band_kernel, heads_dev, cache_len, width...  4.22 us
    unnamed x38, local copies, waits for them, and re-layouts  4.02 us
  transfers between devices with their start and end apart: 50, of which 25 were waited for; matrix products, arithmetic and copies ran while one was open for 0% of the time, Pallas kernels for 10%

profile of v3, /device:TPU:0, one launch (start us, length us, event | category | flops | bytes accessed | tf_op | source)
XLA Modules:
  0.0 173.5 jit_solution(10128697169544824436)
XLA Ops:
  2.4 3.1 %collective-permute-start = (bf16[256,256]{1,0:T(8,128)(2,1)S(1)}, bf16[256,256]{1,0:T(8,128)(2,1)S(1)}, u32[]{:S(2)}, u32[]{:S(2)}) collective-permute-start(bf16[256,256]{1,0:T(8,128)(2,1)S(1)} %shard_map.187.refs_0_), channel_id=1, source_target_pairs={{0,2},{1,3},{2,0},{3,1},{4,6},{5,7},{6,4},{7,5},{8,10},{9,11},{10,... | collective-permute-start | bytes 393224 | tf_op jit(solution)/shard_map/ppermute | solution.py:21
  9.0 3.8 %collective-permute-start.3 = (bf16[256,256]{1,0:T(8,128)(2,1)S(1)}, bf16[256,256]{1,0:T(8,128)(2,1)S(1)}, u32[]{:S(2)}, u32[]{:S(2)}) collective-permute-start(bf16[256,256]{1,0:T(8,128)(2,1)S(1)} %shard_map.187.refs_0_), channel_id=1, source_target_pairs={{0,6},{1,7},{2,4},{3,5},{4,2},{5,3},{6,0},{7,1},{8,14},{9,15},{10,... | collective-permute-start | bytes 393224 | tf_op jit(solution)/shard_map/ppermute | solution.py:21
  17.0 3.4 %collective-permute-start.2 = (bf16[256,256]{1,0:T(8,128)(2,1)S(1)}, bf16[256,256]{1,0:T(8,128)(2,1)S(1)}, u32[]{:S(2)}, u32[]{:S(2)}) collective-permute-start(bf16[256,256]{1,0:T(8,128)(2,1)S(1)} %shard_map.187.refs_0_), channel_id=1, source_target_pairs={{0,4},{1,5},{2,6},{3,7},{4,0},{5,1},{6,2},{7,3},{8,12},{9,13},{10,... | collective-permute-start | bytes 393224 | tf_op jit(solution)/shard_map/ppermute | solution.py:21
  20.8 5.9 %collective-permute-done.2.refs_2_ = bf16[256,256]{1,0:T(8,128)(2,1)S(1)} collective-permute-done((bf16[256,256]{1,0:T(8,128)(2,1)S(1)}, bf16[256,256]{1,0:T(8,128)(2,1)S(1)}, u32[]{:S(2)}, u32[]{:S(2)}) %collective-permute-start.2) | collective-permute-done | bytes 131104 | tf_op jit(solution)/shard_map/ppermute | solution.py:21
  33.6 9.5 %collective-permute-done.7.refs_0_.refs_1_ = bf16[1024,256]{1,0:T(8,128)(2,1)S(1)} collective-permute-done((bf16[1024,256]{1,0:T(8,128)(2,1)S(1)}, bf16[1024,256]{1,0:T(8,128)(2,1)S(1)}, u32[]{:S(2)}, u32[]{:S(2)}) %collective-permute-start.7) | collective-permute-done | bytes 524320 | tf_op jit(solution)/shard_map/ppermute | solution.py:21
  43.1 4.2 %shard_map.192.refs_4_ = f32[2,128,5376]{2,1,0:T(8,128)S(1)} custom-call(s32[4]{0:T(128)S(1)} %copy-done.12, s32[4]{0:T(128)S(1)} %copy-done.13, f32[16,32]{1,0:T(8,128)S(1)} %bitcast.11, s32[1,4608]{1,0:T(1,128)S(1)} %broadcast_in_dim.6.bucket_ref), custom_call_target="tpu_custom_call" | custom-call | flops 11010048 | bytes 5505024 | tf_op jit(solution)/shard_map/pallas_call | solution.py:310
  49.5 5.5 %collective-permute-done.10.refs_9_.refs_1_ = bf16[512,256]{1,0:T(8,128)(2,1)S(1)} collective-permute-done((bf16[512,256]{1,0:T(8,128)(2,1)S(1)}, bf16[512,256]{1,0:T(8,128)(2,1)S(1)}, u32[]{:S(2)}, u32[]{:S(2)}) %collective-permute-start.10) | collective-permute-done | bytes 262176 | tf_op jit(solution)/shard_map/ppermute | solution.py:21
  58.5 2.6 %collective-permute-start.14 = (bf16[512,256]{1,0:T(8,128)(2,1)S(1)}, bf16[512,256]{1,0:T(8,128)(2,1)S(1)}, u32[]{:S(2)}, u32[]{:S(2)}) collective-permute-start(bf16[512,256]{1,0:T(8,128)(2,1)S(1)} %get-tuple-element.107), channel_id=1, source_target_pairs={{0,6},{1,7},{2,4},{3,5},{4,2},{5,3},{6,0},{7,1},{8,14},{9,15},{10,... | collective-permute-start | bytes 786440 | tf_op jit(solution)/shard_map/ppermute | solution.py:21
  63.2 3.3 %shard_map.194 = (f32[2,128,512]{2,1,0:T(8,128)S(1)}, f32[2,1,512]{2,1,0:T(1,128)S(1)}, f32[2,1,512]{2,1,0:T(1,128)S(1)}) custom-call(s32[4]{0:T(128)S(1)} %copy-done.12, s32[4]{0:T(128)S(1)} %copy-done.13, s32[4]{0:T(128)S(1)} %copy-done.14, bf16[2,128,512]{2,1,0:T(8,128)(2,1)S(1)} %get-tuple-element.100.refs_3_, f32[2,128,5376]{2,1,0:T(8,128)S(1)} %shard_map.192.refs_4_, ...), custom_call_target="tpu_custom_call" | custom-call | flops 1610612736 | bytes 7077888 | tf_op jit(solution)/shard_map/pallas_call | solution.py:425
  66.4 11.6 %collective-permute-done.13.refs_5_.refs_6_ = bf16[512,256]{1,0:T(8,128)(2,1)S(1)} collective-permute-done((bf16[512,256]{1,0:T(8,128)(2,1)S(1)}, bf16[512,256]{1,0:T(8,128)(2,1)S(1)}, u32[]{:S(2)}, u32[]{:S(2)}) %collective-permute-start.13) | collective-permute-done | bytes 262176 | tf_op jit(solution)/shard_map/ppermute | solution.py:21
  83.7 6.9 %collective-permute-start.18 = (bf16[64,1024]{1,0:T(8,128)(2,1)S(1)}, bf16[64,1024]{1,0:T(8,128)(2,1)S(1)}, u32[]{:S(2)}, u32[]{:S(2)}) collective-permute-start(bf16[64,1024]{1,0:T(8,128)(2,1)S(1)} %get-tuple-element.117), channel_id=1, source_target_pairs={{0,4},{1,5},{2,6},{3,7},{4,0},{5,1},{6,2},{7,3},{8,12},{9,13},{10,... | collective-permute-start | bytes 393224 | tf_op jit(solution)/shard_map/ppermute | solution.py:21
  92.2 8.4 %collective-permute-done.18.refs_3_ = bf16[64,1024]{1,0:T(8,128)(2,1)S(1)} collective-permute-done((bf16[64,1024]{1,0:T(8,128)(2,1)S(1)}, bf16[64,1024]{1,0:T(8,128)(2,1)S(1)}, u32[]{:S(2)}, u32[]{:S(2)}) %collective-permute-start.18) | collective-permute-done | bytes 131104 | tf_op jit(solution)/shard_map/ppermute | solution.py:21
  102.4 2.7 %collective-permute-start.37 = (bf16[1216,256]{1,0:T(8,128)(2,1)S(1)}, bf16[1216,256]{1,0:T(8,128)(2,1)S(1)}, u32[]{:S(2)}, u32[]{:S(2)}) collective-permute-start(bf16[1216,256]{1,0:T(8,128)(2,1)S(1)} %get-tuple-element.148.refs_2_), channel_id=1, source_target_pairs={{0,8},{8,0},{16,24},{24,16},{1,9},{9,1},{17,25},{25,17},{2,10},{10... | collective-permute-start | bytes 1867784 | tf_op jit(solution)/shard_map/ppermute | solution.py:21
  106.9 2.3 %collective-permute-start.26 = (bf16[64,256]{1,0:T(8,128)(2,1)S(1)}, bf16[64,256]{1,0:T(8,128)(2,1)S(1)}, u32[]{:S(2)}, u32[]{:S(2)}) collective-permute-start(bf16[64,256]{1,0:T(8,128)(2,1)S(1)} %get-tuple-element.130), channel_id=1, source_target_pairs={{0,4},{1,5},{2,6},{3,7},{4,0},{5,1},{6,2},{7,3},{8,12},{9,13},{10,... | collective-permute-start | bytes 98312 | tf_op jit(solution)/shard_map/ppermute | solution.py:21
  109.2 2.2 %collective-permute-start.27 = (bf16[64,256]{1,0:T(8,128)(2,1)S(1)}, bf16[64,256]{1,0:T(8,128)(2,1)S(1)}, u32[]{:S(2)}, u32[]{:S(2)}) collective-permute-start(bf16[64,256]{1,0:T(8,128)(2,1)S(1)} %get-tuple-element.131), channel_id=1, source_target_pairs={{0,6},{1,7},{2,4},{3,5},{4,2},{5,3},{6,0},{7,1},{8,14},{9,15},{10,... | collective-permute-start | bytes 98312 | tf_op jit(solution)/shard_map/ppermute | solution.py:21
  111.8 2.2 %collective-permute-start.28 = (bf16[64,256]{1,0:T(8,128)(2,1)S(1)}, bf16[64,256]{1,0:T(8,128)(2,1)S(1)}, u32[]{:S(2)}, u32[]{:S(2)}) collective-permute-start(bf16[64,256]{1,0:T(8,128)(2,1)S(1)} %get-tuple-element.132), channel_id=1, source_target_pairs={{0,2},{1,3},{2,0},{3,1},{4,6},{5,7},{6,4},{7,5},{8,10},{9,11},{10,... | collective-permute-start | bytes 98312 | tf_op jit(solution)/shard_map/ppermute | solution.py:21
  115.9 2.4 %shard_map.202 = (bf16[64,256]{1,0:T(8,128)(2,1)S(1)}, bf16[64,256]{1,0:T(8,128)(2,1)S(1)}, bf16[64,256]{1,0:T(8,128)(2,1)S(1)}, bf16[64,256]{1,0:T(8,128)(2,1)S(1)}) custom-call(s32[4]{0:T(128)S(1)} %copy-done.12, s32[4]{0:T(128)S(1)} %copy-done.15, bf16[64,256]{1,0:T(8,128)(2,1)S(1)} %get-tuple-element.129.refs_0_, ...), custom_call_target="tpu_custom_call" | custom-call | flops 268435456 | bytes 786464 | tf_op jit(solution)/shard_map/pallas_call | solution.py:52
  122.9 2.4 %collective-permute-done.30.refs_4_ = bf16[64,256]{1,0:T(8,128)(2,1)S(1)} collective-permute-done((bf16[64,256]{1,0:T(8,128)(2,1)S(1)}, bf16[64,256]{1,0:T(8,128)(2,1)S(1)}, u32[]{:S(2)}, u32[]{:S(2)}) %collective-permute-start.30) | collective-permute-done | bytes 32800 | tf_op jit(solution)/shard_map/ppermute | solution.py:21
  131.5 2.5 %collective-permute-done.35.refs_3_ = bf16[64,1024]{1,0:T(8,128)(2,1)S(1)} collective-permute-done((bf16[64,1024]{1,0:T(8,128)(2,1)S(1)}, bf16[64,1024]{1,0:T(8,128)(2,1)S(1)}, u32[]{:S(2)}, u32[]{:S(2)}) %collective-permute-start.35) | collective-permute-done | bytes 131104 | tf_op jit(solution)/shard_map/ppermute | solution.py:21
  134.1 3.2 %collective-permute-done.34.refs_2_ = bf16[64,1024]{1,0:T(8,128)(2,1)S(1)} collective-permute-done((bf16[64,1024]{1,0:T(8,128)(2,1)S(1)}, bf16[64,1024]{1,0:T(8,128)(2,1)S(1)}, u32[]{:S(2)}, u32[]{:S(2)}) %collective-permute-start.34) | collective-permute-done | bytes 131104 | tf_op jit(solution)/shard_map/ppermute | solution.py:21
  137.3 5.8 %collective-permute-done.33.refs_1_ = bf16[64,1024]{1,0:T(8,128)(2,1)S(1)} collective-permute-done((bf16[64,1024]{1,0:T(8,128)(2,1)S(1)}, bf16[64,1024]{1,0:T(8,128)(2,1)S(1)}, u32[]{:S(2)}, u32[]{:S(2)}) %collective-permute-start.33) | collective-permute-done | bytes 131104 | tf_op jit(solution)/shard_map/ppermute | solution.py:21
  149.8 5.6 %collective-permute-done.40.refs_2_ = bf16[64,1024]{1,0:T(8,128)(2,1)S(1)} collective-permute-done((bf16[64,1024]{1,0:T(8,128)(2,1)S(1)}, bf16[64,1024]{1,0:T(8,128)(2,1)S(1)}, u32[]{:S(2)}, u32[]{:S(2)}) %collective-permute-start.40) | collective-permute-done | bytes 131104 | tf_op jit(solution)/shard_map/ppermute | solution.py:21
  160.9 3.7 %collective-permute-done.45.refs_3_ = bf16[64,1024]{1,0:T(8,128)(2,1)S(1)} collective-permute-done((bf16[64,1024]{1,0:T(8,128)(2,1)S(1)}, bf16[64,1024]{1,0:T(8,128)(2,1)S(1)}, u32[]{:S(2)}, u32[]{:S(2)}) %collective-permute-start.45) | collective-permute-done | bytes 131104 | tf_op jit(solution)/shard_map/ppermute | solution.py:21
  164.5 6.4 %collective-permute-done.44.refs_2_ = bf16[64,1024]{1,0:T(8,128)(2,1)S(1)} collective-permute-done((bf16[64,1024]{1,0:T(8,128)(2,1)S(1)}, bf16[64,1024]{1,0:T(8,128)(2,1)S(1)}, u32[]{:S(2)}, u32[]{:S(2)}) %collective-permute-start.44) | collective-permute-done | bytes 131104 | tf_op jit(solution)/shard_map/ppermute | solution.py:21
  (140 shorter events, 63.0 us)
Async XLA Ops:
  9.0 17.8 %collective-permute-start.1 = (bf16[2048,256]{1,0:T(8,128)(2,1)S(1)}, bf16[2048,256]{1,0:T(8,128)(2,1)S(1)}, u32[]{:S(2)}, u32[]{:S(2)}) collective-permute-start(bf16[2048,256]{1,0:T(8,128)(2,1)S(1)} %get-tuple-element.83), channel_id=1, source_target_pairs={{0,1},{1,0},{2,3},{3,2},{4,5},{5,4},{6,7},{7,6},{8,9},{9,8},{10,11... | collective-permute-start | bytes 3145736 | tf_op jit(solution)/shard_map/ppermute | solution.py:21
  12.7 14.1 %collective-permute-start.4 = (bf16[512,256]{1,0:T(8,128)(2,1)S(1)}, bf16[512,256]{1,0:T(8,128)(2,1)S(1)}, u32[]{:S(2)}, u32[]{:S(2)}) collective-permute-start(bf16[512,256]{1,0:T(8,128)(2,1)S(1)} %get-tuple-element.90), channel_id=1, source_target_pairs={{0,8},{8,0},{16,24},{24,16},{1,9},{9,1},{17,25},{25,17},{2,10},{10... | collective-permute-start | bytes 786440 | tf_op jit(solution)/shard_map/ppermute | solution.py:21
  14.2 13.8 %collective-permute-start.5 = (bf16[512,256]{1,0:T(8,128)(2,1)S(1)}, bf16[512,256]{1,0:T(8,128)(2,1)S(1)}, u32[]{:S(2)}, u32[]{:S(2)}) collective-permute-start(bf16[512,256]{1,0:T(8,128)(2,1)S(1)} %get-tuple-element.91), channel_id=1, source_target_pairs={{0,16},{8,24},{16,0},{24,8},{1,17},{9,25},{17,1},{25,9},{2,18},{10... | collective-permute-start | bytes 786440 | tf_op jit(solution)/shard_map/ppermute | solution.py:21
  15.8 12.3 %collective-permute-start.6 = (bf16[512,256]{1,0:T(8,128)(2,1)S(1)}, bf16[512,256]{1,0:T(8,128)(2,1)S(1)}, u32[]{:S(2)}, u32[]{:S(2)}) collective-permute-start(bf16[512,256]{1,0:T(8,128)(2,1)S(1)} %get-tuple-element.92), channel_id=1, source_target_pairs={{0,24},{8,16},{16,8},{24,0},{1,25},{9,17},{17,9},{25,1},{2,26},{10... | collective-permute-start | bytes 786440 | tf_op jit(solution)/shard_map/ppermute | solution.py:21
  28.1 14.9 %collective-permute-start.7 = (bf16[1024,256]{1,0:T(8,128)(2,1)S(1)}, bf16[1024,256]{1,0:T(8,128)(2,1)S(1)}, u32[]{:S(2)}, u32[]{:S(2)}) collective-permute-start(bf16[1024,256]{1,0:T(8,128)(2,1)S(1)} %get-tuple-element.94), channel_id=1, source_target_pairs={{0,8},{8,0},{16,24},{24,16},{1,9},{9,1},{17,25},{25,17},{2,10},{10... | collective-permute-start | bytes 1572872 | tf_op jit(solution)/shard_map/ppermute | solution.py:21
  29.4 25.6 %collective-permute-start.8 = (bf16[1024,256]{1,0:T(8,128)(2,1)S(1)}, bf16[1024,256]{1,0:T(8,128)(2,1)S(1)}, u32[]{:S(2)}, u32[]{:S(2)}) collective-permute-start(bf16[1024,256]{1,0:T(8,128)(2,1)S(1)} %get-tuple-element.96), channel_id=1, source_target_pairs={{0,16},{8,24},{16,0},{24,8},{1,17},{9,25},{17,1},{25,9},{2,18},{10... | collective-permute-start | bytes 1572872 | tf_op jit(solution)/shard_map/ppermute | solution.py:21
  30.2 24.8 %collective-permute-start.9 = (bf16[1024,256]{1,0:T(8,128)(2,1)S(1)}, bf16[1024,256]{1,0:T(8,128)(2,1)S(1)}, u32[]{:S(2)}, u32[]{:S(2)}) collective-permute-start(bf16[1024,256]{1,0:T(8,128)(2,1)S(1)} %get-tuple-element.98), channel_id=1, source_target_pairs={{0,24},{8,16},{16,8},{24,0},{1,25},{9,17},{17,9},{25,1},{2,26},{10... | collective-permute-start | bytes 1572872 | tf_op jit(solution)/shard_map/ppermute | solution.py:21
  31.7 17.8 %collective-permute-start.11 = (bf16[512,256]{1,0:T(8,128)(2,1)S(1)}, bf16[512,256]{1,0:T(8,128)(2,1)S(1)}, u32[]{:S(2)}, u32[]{:S(2)}) collective-permute-start(bf16[512,256]{1,0:T(8,128)(2,1)S(1)} %get-tuple-element.103), channel_id=1, source_target_pairs={{0,4},{1,5},{2,6},{3,7},{4,0},{5,1},{6,2},{7,3},{8,12},{9,13},{10,... | collective-permute-start | bytes 786440 | tf_op jit(solution)/shard_map/ppermute | solution.py:21
  31.7 17.8 %collective-permute-start.12 = (bf16[512,256]{1,0:T(8,128)(2,1)S(1)}, bf16[512,256]{1,0:T(8,128)(2,1)S(1)}, u32[]{:S(2)}, u32[]{:S(2)}) collective-permute-start(bf16[512,256]{1,0:T(8,128)(2,1)S(1)} %get-tuple-element.104), channel_id=1, source_target_pairs={{0,6},{1,7},{2,4},{3,5},{4,2},{5,3},{6,0},{7,1},{8,14},{9,15},{10,... | collective-permute-start | bytes 786440 | tf_op jit(solution)/shard_map/ppermute | solution.py:21
  55.1 24.1 %collective-permute-start.21 = (bf16[1280,256]{1,0:T(8,128)(2,1)S(1)}, bf16[1280,256]{1,0:T(8,128)(2,1)S(1)}, u32[]{:S(2)}, u32[]{:S(2)}) collective-permute-start(bf16[1280,256]{1,0:T(8,128)(2,1)S(1)} %get-tuple-element.121.refs_0_), channel_id=1, source_target_pairs={{0,8},{8,0},{16,24},{24,16},{1,9},{9,1},{17,25},{25,17},{2,10},{10... | collective-permute-start | bytes 1966088 | tf_op jit(solution)/shard_map/ppermute | solution.py:21
  56.6 22.6 %collective-permute-start.22 = (bf16[1120,256]{1,0:T(8,128)(2,1)S(1)}, bf16[1120,256]{1,0:T(8,128)(2,1)S(1)}, u32[]{:S(2)}, u32[]{:S(2)}) collective-permute-start(bf16[1120,256]{1,0:T(8,128)(2,1)S(1)} %get-tuple-element.123.refs_2_), channel_id=1, source_target_pairs={{0,16},{8,24},{16,0},{24,8},{1,17},{9,25},{17,1},{25,9},{2,18},{10... | collective-permute-start | bytes 1720328 | tf_op jit(solution)/shard_map/ppermute | solution.py:21
  58.0 20.0 %collective-permute-start.13 = (bf16[512,256]{1,0:T(8,128)(2,1)S(1)}, bf16[512,256]{1,0:T(8,128)(2,1)S(1)}, u32[]{:S(2)}, u32[]{:S(2)}) collective-permute-start(bf16[512,256]{1,0:T(8,128)(2,1)S(1)} %get-tuple-element.106), channel_id=1, source_target_pairs={{0,4},{1,5},{2,6},{3,7},{4,0},{5,1},{6,2},{7,3},{8,12},{9,13},{10,... | collective-permute-start | bytes 786440 | tf_op jit(solution)/shard_map/ppermute | solution.py:21
  58.5 19.6 %collective-permute-start.14 = (bf16[512,256]{1,0:T(8,128)(2,1)S(1)}, bf16[512,256]{1,0:T(8,128)(2,1)S(1)}, u32[]{:S(2)}, u32[]{:S(2)}) collective-permute-start(bf16[512,256]{1,0:T(8,128)(2,1)S(1)} %get-tuple-element.107), channel_id=1, source_target_pairs={{0,6},{1,7},{2,4},{3,5},{4,2},{5,3},{6,0},{7,1},{8,14},{9,15},{10,... | collective-permute-start | bytes 786440 | tf_op jit(solution)/shard_map/ppermute | solution.py:21
  61.1 18.2 %collective-permute-start.15 = (bf16[512,256]{1,0:T(8,128)(2,1)S(1)}, bf16[512,256]{1,0:T(8,128)(2,1)S(1)}, u32[]{:S(2)}, u32[]{:S(2)}) collective-permute-start(bf16[512,256]{1,0:T(8,128)(2,1)S(1)} %get-tuple-element.108), channel_id=1, source_target_pairs={{0,2},{1,3},{2,0},{3,1},{4,6},{5,7},{6,4},{7,5},{8,10},{9,11},{10,... | collective-permute-start | bytes 786440 | tf_op jit(solution)/shard_map/ppermute | solution.py:21
  79.4 22.2 %collective-permute-start.23 = (bf16[1536,256]{1,0:T(8,128)(2,1)S(1)}, bf16[1536,256]{1,0:T(8,128)(2,1)S(1)}, u32[]{:S(2)}, u32[]{:S(2)}) collective-permute-start(bf16[1536,256]{1,0:T(8,128)(2,1)S(1)} %get-tuple-element.125.refs_0_), channel_id=1, source_target_pairs={{0,16},{8,24},{16,0},{24,8},{1,17},{9,25},{17,1},{25,9},{2,18},{10... | collective-permute-start | bytes 2359304 | tf_op jit(solution)/shard_map/ppermute | solution.py:21
  80.0 21.6 %collective-permute-start.24 = (bf16[1024,256]{1,0:T(8,128)(2,1)S(1)}, bf16[1024,256]{1,0:T(8,128)(2,1)S(1)}, u32[]{:S(2)}, u32[]{:S(2)}) collective-permute-start(bf16[1024,256]{1,0:T(8,128)(2,1)S(1)} %get-tuple-element.126.refs_2_), channel_id=1, source_target_pairs={{0,8},{8,0},{16,24},{24,16},{1,9},{9,1},{17,25},{25,17},{2,10},{10... | collective-permute-start | bytes 1572872 | tf_op jit(solution)/shard_map/ppermute | solution.py:21
  83.7 16.9 %collective-permute-start.18 = (bf16[64,1024]{1,0:T(8,128)(2,1)S(1)}, bf16[64,1024]{1,0:T(8,128)(2,1)S(1)}, u32[]{:S(2)}, u32[]{:S(2)}) collective-permute-start(bf16[64,1024]{1,0:T(8,128)(2,1)S(1)} %get-tuple-element.117), channel_id=1, source_target_pairs={{0,4},{1,5},{2,6},{3,7},{4,0},{5,1},{6,2},{7,3},{8,12},{9,13},{10,... | collective-permute-start | bytes 393224 | tf_op jit(solution)/shard_map/ppermute | solution.py:21
  101.9 19.1 %collective-permute-start.32 = (bf16[2048,256]{1,0:T(8,128)(2,1)S(1)}, bf16[2048,256]{1,0:T(8,128)(2,1)S(1)}, u32[]{:S(2)}, u32[]{:S(2)}) collective-permute-start(bf16[2048,256]{1,0:T(8,128)(2,1)S(1)} %get-tuple-element.141.refs_6_), channel_id=1, source_target_pairs={{0,1},{1,0},{2,3},{3,2},{4,5},{5,4},{6,7},{7,6},{8,9},{9,8},{10,11... | collective-permute-start | bytes 3145736 | tf_op jit(solution)/shard_map/ppermute | solution.py:21
  102.4 24.9 %collective-permute-start.37 = (bf16[1216,256]{1,0:T(8,128)(2,1)S(1)}, bf16[1216,256]{1,0:T(8,128)(2,1)S(1)}, u32[]{:S(2)}, u32[]{:S(2)}) collective-permute-start(bf16[1216,256]{1,0:T(8,128)(2,1)S(1)} %get-tuple-element.148.refs_2_), channel_id=1, source_target_pairs={{0,8},{8,0},{16,24},{24,16},{1,9},{9,1},{17,25},{25,17},{2,10},{10... | collective-permute-start | bytes 1867784 | tf_op jit(solution)/shard_map/ppermute | solution.py:21
  105.1 22.2 %collective-permute-start.36 = (bf16[1024,256]{1,0:T(8,128)(2,1)S(1)}, bf16[1024,256]{1,0:T(8,128)(2,1)S(1)}, u32[]{:S(2)}, u32[]{:S(2)}) collective-permute-start(bf16[1024,256]{1,0:T(8,128)(2,1)S(1)} %get-tuple-element.146.refs_0_), channel_id=1, source_target_pairs={{0,16},{8,24},{16,0},{24,8},{1,17},{9,25},{17,1},{25,9},{2,18},{10... | collective-permute-start | bytes 1572872 | tf_op jit(solution)/shard_map/ppermute | solution.py:21
  127.5 15.7 %collective-permute-start.39 = (bf16[2432,256]{1,0:T(8,128)(2,1)S(1)}, bf16[2432,256]{1,0:T(8,128)(2,1)S(1)}, u32[]{:S(2)}, u32[]{:S(2)}) collective-permute-start(bf16[2432,256]{1,0:T(8,128)(2,1)S(1)} %get-tuple-element.150.refs_6_), channel_id=1, source_target_pairs={{0,1},{1,0},{2,3},{3,2},{4,5},{5,4},{6,7},{7,6},{8,9},{9,8},{10,11... | collective-permute-start | bytes 3735560 | tf_op jit(solution)/shard_map/ppermute | solution.py:21
  127.5 15.6 %collective-permute-start.38 = (bf16[2048,256]{1,0:T(8,128)(2,1)S(1)}, bf16[2048,256]{1,0:T(8,128)(2,1)S(1)}, u32[]{:S(2)}, u32[]{:S(2)}) collective-permute-start(bf16[2048,256]{1,0:T(8,128)(2,1)S(1)} %get-tuple-element.149.refs_4_), channel_id=1, source_target_pairs={{0,1},{1,0},{2,3},{3,2},{4,5},{5,4},{6,7},{7,6},{8,9},{9,8},{10,11... | collective-permute-start | bytes 3145736 | tf_op jit(solution)/shard_map/ppermute | solution.py:21
  130.1 13.0 %collective-permute-start.33 = (bf16[64,1024]{1,0:T(8,128)(2,1)S(1)}, bf16[64,1024]{1,0:T(8,128)(2,1)S(1)}, u32[]{:S(2)}, u32[]{:S(2)}) collective-permute-start(bf16[64,1024]{1,0:T(8,128)(2,1)S(1)} %get-tuple-element.143.refs_0_), channel_id=1, source_target_pairs={{0,4},{1,5},{2,6},{3,7},{4,0},{5,1},{6,2},{7,3},{8,12},{9,13},{10,... | collective-permute-start | bytes 393224 | tf_op jit(solution)/shard_map/ppermute | solution.py:21
  158.5 12.5 %collective-permute-start.44 = (bf16[64,1024]{1,0:T(8,128)(2,1)S(1)}, bf16[64,1024]{1,0:T(8,128)(2,1)S(1)}, u32[]{:S(2)}, u32[]{:S(2)}) collective-permute-start(bf16[64,1024]{1,0:T(8,128)(2,1)S(1)} %shard_map.206.refs_0_), channel_id=1, source_target_pairs={{0,4},{1,5},{2,6},{3,7},{4,0},{5,1},{6,2},{7,3},{8,12},{9,13},{10,... | collective-permute-start | bytes 393224 | tf_op jit(solution)/shard_map/ppermute | solution.py:21
  (45 other events, 387.4 us)

commit v4 on v3

--- a/solution.py
+++ b/solution.py
@@ -178,10 +178,10 @@
     rest_b[rest_b.shape[0] - o3.shape[0] :, :] = o3[...]
 
 
-def weave_kernel(count, *refs):
-    parts, (rest_a, rest_b, out_a, out_b) = refs[:count], refs[count:]
-    width = parts[0].shape[1] // 2
-    half_depth = parts[0].shape[0] - width
+def weave_kernel(count, all_parts, rest_a, rest_b, out_a, out_b):
+    size, width = all_parts.shape[0] // count, all_parts.shape[1] // 2
+    parts = [all_parts[k * size : (k + 1) * size, :] for k in range(count)]
+    half_depth = size - width
     for k in range(0, count, 2):
         pair = [stacked(part[:half_depth, :], width) for part in parts[k : k + 2]]
         out_a[k * half_depth : (k + 2) * half_depth, :] = jnp.concatenate(pair, axis=1)
@@ -326,15 +326,17 @@
     )(slot_order, cache_lengths, rel_bias.T, bucket_of[None, :])
 
 
-def self_kernel(cache_len, places, first_call, *refs):
+def self_kernel(cache_len, places, first_call, last_call, *refs):
     order_ref, old_ref, new_ref, query_ref, band_ref = refs[:5]
     count = len(places)
     blocks, refs = refs[5 : 5 + count], refs[5 + count :]
     if first_call:
-        fresh_ref, total_ref, top_ref, norm_ref, score_ref = refs
+        fresh_ref, refs = refs[0], refs[1:]
     else:
-        total_in, top_in, norm_in, kept_ref, given_ref = refs[:5]
-        total_ref, top_ref, norm_ref, score_ref = refs[5:]
+        (total_in, top_in, norm_in), refs = refs[:3], refs[3:]
+    if last_call:
+        (kept_ref, given_ref), refs = refs[:2], refs[2:]
+    total_ref, top_ref, norm_ref, score_ref = refs
     slot = order_ref[lax.axis_index("req")]
     old_len, new_len = old_ref[slot], new_ref[slot]
     rows = query_ref.shape[2]
@@ -390,7 +392,7 @@
 
             attend(block[...], cache_len - TILE - first, admit)
 
-    if not first_call:
+    if last_call:
         total_ref[0, :HD, :] = total_ref[0, HD:, :] / norm_ref[0]
         half = rows // 2
         for out_ref, core in ((kept_ref, lax.rem(blk, 2)), (given_ref, 1 - lax.rem(blk, 2))):
@@ -398,7 +400,7 @@
             out_ref[0] = total_ref[0, :HD, spot].astype(BF16)
 
 
-def self_attend(lens, query_t, band, blocks, places, cache_len, fresh=None, state=None):
+def self_attend(lens, query_t, band, blocks, places, cache_len, fresh=None, state=None, last_call=False):
     heads_dev, pair, rows = query_t.shape
     count, tokens = len(blocks), blocks[0].shape[0]
     first_call = state is None
@@ -412,18 +414,20 @@
     if first_call:
         in_specs.append(pl.BlockSpec((rows, pair), lambda h: (0, h)))
         more = [fresh]
+    else:
+        in_specs += [head_block(*shape) for shape in held]
+        more = list(state)
+    if not last_call:
         out_specs = [head_block(*shape) for shape in held]
         out_shape = [jax.ShapeDtypeStruct((heads_dev,) + shape, F32) for shape in held]
         scratch = [score]
     else:
-        in_specs += [head_block(*shape) for shape in held]
-        more = list(state)
         out_specs = [head_block(HD, rows // 2)] * 2
         out_shape = [shaped((heads_dev, HD, rows // 2))] * 2
         scratch = [pltpu.VMEM((1,) + shape, F32) for shape in held] + [score]
     keys_all = count * tokens + (rows if first_call else 0)
     return pl.pallas_call(
-        functools.partial(self_kernel, cache_len, places, first_call),
+        functools.partial(self_kernel, cache_len, places, first_call, last_call),
         grid=(heads_dev,),
         in_specs=in_specs,
         out_specs=out_specs,
@@ -668,19 +672,21 @@
     down_owners = [part_owner(p, down_strides) for p in range(req_count)]
 
     lanes = 2 * width_dev
-    cross = local_call(
-        pack_cross_kernel,
-        [cross_q, cross_out],
-        [shaped((depth // 2 + width_dev, lanes))],
-    )[0]
-    cross_parts = chip_sends([cross] * chips)
     tokens = cache_in.shape[1]
     *kept, given = cut_cache(cache_in, slot_order)
     band = make_band(
         bucket_of, rel_bias, slot_order, cache_lengths, heads_dev, tokens * blk_count, rows
     )
     near_req = [kept[0]] + [xor_send(kept[k], "req", k) for k in range(1, req_count)]
-    taken = xor_send(after(given, cross_parts[1]), "blk", 1)
+    cross = local_call(
+        pack_cross_kernel,
+        [after(cross_q, kept[0]), cross_out],
+        [shaped((depth // 2 + width_dev, lanes))],
+    )[0]
+    for step in range(chips.bit_length() - 1):
+        cross = place([cross, xor_send(cross, "blk", 2 << step)], lambda k: k)
+        cross_first = cross if step == 0 else cross_first
+    taken = xor_send(given, "blk", 1)
     skip = depth + depth // 2
     packed_in = [self_q, self_kv, cross_kv, ff_in, self_out, ff_out]
     packed_in[1], packed_in[2] = jnp.moveaxis(self_kv, 1, 0), jnp.moveaxis(cross_kv, 1, 0)
@@ -703,7 +709,7 @@
     all_depth = chips * (depth // 2)
     later_a, later_b = local_call(
         functools.partial(weave_kernel, chips),
-        [*cross_parts, rest_a, rest_b],
+        [cross, rest_a, rest_b],
         [
             shaped((all_depth + rest_a.shape[0], lanes)),
             shaped((chips * width_dev + rest_b.shape[0], lanes)),
@@ -716,14 +722,15 @@
         [taken, first],
         [shaped((tokens, taken.shape[1]))] + [joined] * (req_count - 1),
     )
-    near = list(turn([after(near_req[0], joined[0], later_a), *near_req[1:]]))
+    near = list(turn([after(near_req[0], joined[0], cross_first), *near_req[1:]]))
     far_req = [joined[0]]
     far_req += [
-        xor_send(after(joined[k], near[0]), "req", k) for k in range(1, req_count)
+        xor_send(after(joined[k], near[0]), "req", k) for k in range(1, req_count - 1)
     ]
+    far_req.append(xor_send(after(joined[-1], near[0], cross), "req", req_count - 1))
     near[1] = after(near[1], far_req[1])
     near = chip_sends(near)
-    far = turn([after(far_req[0], band, *near[1:]), *far_req[1:]])
+    far = turn([after(far_req[0], band, later_a, *near[1:]), *far_req[1:]])
     far = chip_sends(far)
 
     def token_order(i):
@@ -763,6 +770,9 @@
         cache_len,
         fresh=fresh,
     )
+    state = self_attend(
+        lens, query_t, band, far[1 : chips // 2], far_places[1 : chips // 2], cache_len, state=state
+    )
 
     moved_a = xor_send(after(later_a, far[0]), "req", up_strides[0])
     moved_b = xor_send(after(later_b, far[0]), "req", down_strides[0])
@@ -778,10 +788,11 @@
         lens,
         query_t,
         band,
-        reordered(far)[1:],
-        reordered(far_places)[1:],
+        far[chips // 2 :],
+        far_places[chips // 2 :],
         cache_len,
         state=state,
+        last_call=True,
     )
     kept, given = kept.reshape(width_dev, half), given.reshape(width_dev, half)
 
@@ -802,6 +813,8 @@
         [after(w_query, *parts[1:]), w_cross], [moved_a, moved_b], last
     )
     w_query = (w_query, xor_send(w_query, "blk", 1))
+    w_cross = (w_cross, xor_send(w_cross, "blk", 1))
+    residual = after(residual, w_cross[1])
     w_wide, moved_a = gather_on(after(w_wide, *parts[1:]), up_strides)
     w_down, moved_b = gather_on(after(w_down, *parts[1:]), down_strides)
     total, *queries = local_call(
@@ -811,7 +824,6 @@
         flops=2 * share * width * width,
     )
     residual = total
-    w_cross = (w_cross, xor_send(w_cross, "blk", 1))
     enc_rows = encoder_out.shape[0]
     pairs = local_call(
         functools.partial(pair_kernel, range(req_count)),

time: 175 us -> 175 us (level)
  Pallas kernels: 21.5 us -> 28.6 us
  starting transfers between devices: 64.3 us -> 62.3 us
  waiting for transfers between devices: 82.6 us -> 80.8 us
    pallas_call x2 -> x3, Pallas kernels: 4.27 us -> 11.3 us  [self_attend(): pl.pallas_call(functools.partial(self_kernel, cache_len, places, first_ca...]
    ppermute x50 -> x49, starting transfers between devices: 64.3 us -> 62.3 us  [xor_send(): return lax.ppermute(value, axis, [(i, i ^ step) for i in range(size)])]
    ppermute x50 -> x49, waiting for transfers between devices: 82.6 us -> 80.8 us  [xor_send(): return lax.ppermute(value, axis, [(i, i ^ step) for i in range(size)])]
    pallas_call x21 -> x23, Pallas kernels: 13 us -> 13.1 us  [local_call(): pl.pallas_call(kernel, out_shape=list(outs), in_specs=[SMEM] * smem + [VM...]
  transfers between devices with their start and end apart: 50 -> 49, of which waited for: 25 -> 24; matrix products, arithmetic and copies ran while one was open for 0% -> 0% of each run, Pallas kernels for 10% -> 14%
where the time goes in v4:
time: 175 us
  waiting for transfers between devices  80.8 us (46%)
  starting transfers between devices  62.3 us (36%)
  Pallas kernels  28.6 us (16%)
  local copies, waits for them, and re-layouts  2.37 us (1%)
    ppermute x49, waiting for transfers between devices, xor_send(): return lax.ppermute(value, axis, [(i, i ^ step) for i in range(size)])  80.8 us
    ppermute x49, starting transfers between devices, xor_send(): return lax.ppermute(value, axis, [(i, i ^ step) for i in range(size)])  62.3 us
    pallas_call x23, Pallas kernels, local_call(): pl.pallas_call(kernel, out_shape=list(outs), in_specs=[SMEM] * smem + [VM...  13.1 us
    pallas_call x3, Pallas kernels, self_attend(): pl.pallas_call(functools.partial(self_kernel, cache_len, places, first_ca...  11.3 us
    pallas_call x1, Pallas kernels, make_band(): pl.pallas_call(functools.partial(band_kernel, heads_dev, cache_len, width...  4.22 us
  transfers between devices with their start and end apart: 49, of which 24 were waited for; matrix products, arithmetic and copies ran while one was open for 0% of the time, Pallas kernels for 14%

profile of v4, /device:TPU:0, one launch (start us, length us, event | category | flops | bytes accessed | tf_op | source)
XLA Modules:
  0.0 175.2 jit_solution(15103820694191591422)
XLA Ops:
  10.7 3.0 %collective-permute-done.1.refs_1_ = bf16[256,256]{1,0:T(8,128)(2,1)S(1)} collective-permute-done((bf16[256,256]{1,0:T(8,128)(2,1)S(1)}, bf16[256,256]{1,0:T(8,128)(2,1)S(1)}, u32[]{:S(2)}, u32[]{:S(2)}) %collective-permute-start.1) | collective-permute-done | bytes 131104 | tf_op jit(solution)/shard_map/ppermute | solution.py:21
  13.7 2.8 %collective-permute-start.7 = (bf16[512,256]{1,0:T(8,128)(2,1)S(1)}, bf16[512,256]{1,0:T(8,128)(2,1)S(1)}, u32[]{:S(2)}, u32[]{:S(2)}) collective-permute-start(bf16[512,256]{1,0:T(8,128)(2,1)S(1)} %shard_map.189.refs_0_), channel_id=1, source_target_pairs={{0,4},{1,5},{2,6},{3,7},{4,0},{5,1},{6,2},{7,3},{8,12},{9,13},{10,... | collective-permute-start | bytes 786440 | tf_op jit(solution)/shard_map/ppermute | solution.py:21
  16.7 4.1 %collective-permute-done.3.refs_2_ = bf16[512,256]{1,0:T(8,128)(2,1)S(1)} collective-permute-done((bf16[512,256]{1,0:T(8,128)(2,1)S(1)}, bf16[512,256]{1,0:T(8,128)(2,1)S(1)}, u32[]{:S(2)}, u32[]{:S(2)}) %collective-permute-start.3) | collective-permute-done | bytes 262176 | tf_op jit(solution)/shard_map/ppermute | solution.py:21
  22.1 5.4 %collective-permute-done.7.refs_1_ = bf16[512,256]{1,0:T(8,128)(2,1)S(1)} collective-permute-done((bf16[512,256]{1,0:T(8,128)(2,1)S(1)}, bf16[512,256]{1,0:T(8,128)(2,1)S(1)}, u32[]{:S(2)}, u32[]{:S(2)}) %collective-permute-start.7) | collective-permute-done | bytes 262176 | tf_op jit(solution)/shard_map/ppermute | solution.py:21
  30.4 3.5 %collective-permute-start.11 = (bf16[512,256]{1,0:T(8,128)(2,1)S(1)}, bf16[512,256]{1,0:T(8,128)(2,1)S(1)}, u32[]{:S(2)}, u32[]{:S(2)}) collective-permute-start(bf16[512,256]{1,0:T(8,128)(2,1)S(1)} %get-tuple-element.108), channel_id=1, source_target_pairs={{0,6},{1,7},{2,4},{3,5},{4,2},{5,3},{6,0},{7,1},{8,14},{9,15},{10,... | collective-permute-start | bytes 786440 | tf_op jit(solution)/shard_map/ppermute | solution.py:21
  37.4 4.2 %shard_map.194.refs_4_ = f32[2,128,5376]{2,1,0:T(8,128)S(1)} custom-call(s32[4]{0:T(128)S(1)} %copy-done.11, s32[4]{0:T(128)S(1)} %copy-done.13, f32[16,32]{1,0:T(8,128)S(1)} %bitcast.11, s32[1,4608]{1,0:T(1,128)S(1)} %broadcast_in_dim.6.bucket_ref), custom_call_target="tpu_custom_call" | custom-call | flops 11010048 | bytes 5505024 | tf_op jit(solution)/shard_map/pallas_call | solution.py:310
  41.7 9.6 %collective-permute-done.10.refs_7_.refs_2_ = bf16[512,256]{1,0:T(8,128)(2,1)S(1)} collective-permute-done((bf16[512,256]{1,0:T(8,128)(2,1)S(1)}, bf16[512,256]{1,0:T(8,128)(2,1)S(1)}, u32[]{:S(2)}, u32[]{:S(2)}) %collective-permute-start.10) | collective-permute-done | bytes 262176 | tf_op jit(solution)/shard_map/ppermute | solution.py:21
  54.6 3.0 %collective-permute-start.12 = (bf16[512,256]{1,0:T(8,128)(2,1)S(1)}, bf16[512,256]{1,0:T(8,128)(2,1)S(1)}, u32[]{:S(2)}, u32[]{:S(2)}) collective-permute-start(bf16[512,256]{1,0:T(8,128)(2,1)S(1)} %get-tuple-element.110), channel_id=1, source_target_pairs={{0,2},{1,3},{2,0},{3,1},{4,6},{5,7},{6,4},{7,5},{8,10},{9,11},{10,... | collective-permute-start | bytes 786440 | tf_op jit(solution)/shard_map/ppermute | solution.py:21
  61.6 7.0 %shard_map.196 = (f32[2,128,512]{2,1,0:T(8,128)S(1)}, f32[2,1,512]{2,1,0:T(1,128)S(1)}, f32[2,1,512]{2,1,0:T(1,128)S(1)}) custom-call(s32[4]{0:T(128)S(1)} %copy-done.11, s32[4]{0:T(128)S(1)} %copy-done.13, s32[4]{0:T(128)S(1)} %copy-done.14, bf16[2,128,512]{2,1,0:T(8,128)(2,1)S(1)} %get-tuple-element.104.refs_3_, f32[2,128,5376]{2,1,0:T(8,128)S(1)} %shard_map.194.refs_4_, ...), custom_call_target="tpu_custom_call" | custom-call | flops 1610612736 | bytes 7077888 | tf_op jit(solution)/shard_map/pallas_call | solution.py:429
  70.7 7.9 %collective-permute-done.13.refs_5_.refs_6_ = bf16[512,256]{1,0:T(8,128)(2,1)S(1)} collective-permute-done((bf16[512,256]{1,0:T(8,128)(2,1)S(1)}, bf16[512,256]{1,0:T(8,128)(2,1)S(1)}, u32[]{:S(2)}, u32[]{:S(2)}) %collective-permute-start.13) | collective-permute-done | bytes 262176 | tf_op jit(solution)/shard_map/ppermute | solution.py:21
  84.5 3.4 %collective-permute-start.19 = (bf16[64,1024]{1,0:T(8,128)(2,1)S(1)}, bf16[64,1024]{1,0:T(8,128)(2,1)S(1)}, u32[]{:S(2)}, u32[]{:S(2)}) collective-permute-start(bf16[64,1024]{1,0:T(8,128)(2,1)S(1)} %get-tuple-element.128), channel_id=1, source_target_pairs={{0,2},{1,3},{2,0},{3,1},{4,6},{5,7},{6,4},{7,5},{8,10},{9,11},{10,... | collective-permute-start | bytes 393224 | tf_op jit(solution)/shard_map/ppermute | solution.py:21
  87.9 3.0 %collective-permute-start.20 = (bf16[64,1024]{1,0:T(8,128)(2,1)S(1)}, bf16[64,1024]{1,0:T(8,128)(2,1)S(1)}, u32[]{:S(2)}, u32[]{:S(2)}) collective-permute-start(bf16[64,1024]{1,0:T(8,128)(2,1)S(1)} %get-tuple-element.129), channel_id=1, source_target_pairs={{0,4},{1,5},{2,6},{3,7},{4,0},{5,1},{6,2},{7,3},{8,12},{9,13},{10,... | collective-permute-start | bytes 393224 | tf_op jit(solution)/shard_map/ppermute | solution.py:21
  92.4 2.8 %collective-permute-done.20.refs_3_ = bf16[64,1024]{1,0:T(8,128)(2,1)S(1)} collective-permute-done((bf16[64,1024]{1,0:T(8,128)(2,1)S(1)}, bf16[64,1024]{1,0:T(8,128)(2,1)S(1)}, u32[]{:S(2)}, u32[]{:S(2)}) %collective-permute-start.20) | collective-permute-done | bytes 131104 | tf_op jit(solution)/shard_map/ppermute | solution.py:21
  95.2 6.6 %collective-permute-done.21.refs_4_ = bf16[64,1024]{1,0:T(8,128)(2,1)S(1)} collective-permute-done((bf16[64,1024]{1,0:T(8,128)(2,1)S(1)}, bf16[64,1024]{1,0:T(8,128)(2,1)S(1)}, u32[]{:S(2)}, u32[]{:S(2)}) %collective-permute-start.21) | collective-permute-done | bytes 131104 | tf_op jit(solution)/shard_map/ppermute | solution.py:21
  102.6 3.0 %collective-permute-start.35 = (bf16[1024,256]{1,0:T(8,128)(2,1)S(1)}, bf16[1024,256]{1,0:T(8,128)(2,1)S(1)}, u32[]{:S(2)}, u32[]{:S(2)}) collective-permute-start(bf16[1024,256]{1,0:T(8,128)(2,1)S(1)} %get-tuple-element.154.refs_0_), channel_id=1, source_target_pairs={{0,16},{8,24},{16,0},{24,8},{1,17},{9,25},{17,1},{25,9},{2,18},{10... | collective-permute-start | bytes 1572872 | tf_op jit(solution)/shard_map/ppermute | solution.py:21
  107.6 4.3 %collective-permute-start.26 = (bf16[64,256]{1,0:T(8,128)(2,1)S(1)}, bf16[64,256]{1,0:T(8,128)(2,1)S(1)}, u32[]{:S(2)}, u32[]{:S(2)}) collective-permute-start(bf16[64,256]{1,0:T(8,128)(2,1)S(1)} %get-tuple-element.139), channel_id=1, source_target_pairs={{0,4},{1,5},{2,6},{3,7},{4,0},{5,1},{6,2},{7,3},{8,12},{9,13},{10,... | collective-permute-start | bytes 98312 | tf_op jit(solution)/shard_map/ppermute | solution.py:21
  114.6 3.1 %collective-permute-done.27.refs_2_ = bf16[64,256]{1,0:T(8,128)(2,1)S(1)} collective-permute-done((bf16[64,256]{1,0:T(8,128)(2,1)S(1)}, bf16[64,256]{1,0:T(8,128)(2,1)S(1)}, u32[]{:S(2)}, u32[]{:S(2)}) %collective-permute-start.27) | collective-permute-done | bytes 32800 | tf_op jit(solution)/shard_map/ppermute | solution.py:21
  120.2 2.6 %collective-permute-start.30 = (bf16[64,256]{1,0:T(8,128)(2,1)S(1)}, bf16[64,256]{1,0:T(8,128)(2,1)S(1)}, u32[]{:S(2)}, u32[]{:S(2)}) collective-permute-start(bf16[64,256]{1,0:T(8,128)(2,1)S(1)} %get-tuple-element.148), channel_id=1, source_target_pairs={{0,4},{1,5},{2,6},{3,7},{4,0},{5,1},{6,2},{7,3},{8,12},{9,13},{10,... | collective-permute-start | bytes 98312 | tf_op jit(solution)/shard_map/ppermute | solution.py:21
  125.0 3.4 %collective-permute-done.31.refs_5_ = bf16[64,256]{1,0:T(8,128)(2,1)S(1)} collective-permute-done((bf16[64,256]{1,0:T(8,128)(2,1)S(1)}, bf16[64,256]{1,0:T(8,128)(2,1)S(1)}, u32[]{:S(2)}, u32[]{:S(2)}) %collective-permute-start.31) | collective-permute-done | bytes 32800 | tf_op jit(solution)/shard_map/ppermute | solution.py:21
  135.8 3.0 %collective-permute-done.33.refs_2_ = bf16[64,1024]{1,0:T(8,128)(2,1)S(1)} collective-permute-done((bf16[64,1024]{1,0:T(8,128)(2,1)S(1)}, bf16[64,1024]{1,0:T(8,128)(2,1)S(1)}, u32[]{:S(2)}, u32[]{:S(2)}) %collective-permute-start.33) | collective-permute-done | bytes 131104 | tf_op jit(solution)/shard_map/ppermute | solution.py:21
  138.8 6.1 %collective-permute-done.32.refs_1_ = bf16[64,1024]{1,0:T(8,128)(2,1)S(1)} collective-permute-done((bf16[64,1024]{1,0:T(8,128)(2,1)S(1)}, bf16[64,1024]{1,0:T(8,128)(2,1)S(1)}, u32[]{:S(2)}, u32[]{:S(2)}) %collective-permute-start.32) | collective-permute-done | bytes 131104 | tf_op jit(solution)/shard_map/ppermute | solution.py:21
  151.6 5.5 %collective-permute-done.39.refs_2_ = bf16[64,1024]{1,0:T(8,128)(2,1)S(1)} collective-permute-done((bf16[64,1024]{1,0:T(8,128)(2,1)S(1)}, bf16[64,1024]{1,0:T(8,128)(2,1)S(1)}, u32[]{:S(2)}, u32[]{:S(2)}) %collective-permute-start.39) | collective-permute-done | bytes 131104 | tf_op jit(solution)/shard_map/ppermute | solution.py:21
  162.5 3.5 %collective-permute-done.44.refs_3_ = bf16[64,1024]{1,0:T(8,128)(2,1)S(1)} collective-permute-done((bf16[64,1024]{1,0:T(8,128)(2,1)S(1)}, bf16[64,1024]{1,0:T(8,128)(2,1)S(1)}, u32[]{:S(2)}, u32[]{:S(2)}) %collective-permute-start.44) | collective-permute-done | bytes 131104 | tf_op jit(solution)/shard_map/ppermute | solution.py:21
  166.1 6.5 %collective-permute-done.43.refs_2_ = bf16[64,1024]{1,0:T(8,128)(2,1)S(1)} collective-permute-done((bf16[64,1024]{1,0:T(8,128)(2,1)S(1)}, bf16[64,1024]{1,0:T(8,128)(2,1)S(1)}, u32[]{:S(2)}, u32[]{:S(2)}) %collective-permute-start.43) | collective-permute-done | bytes 131104 | tf_op jit(solution)/shard_map/ppermute | solution.py:21
  (141 shorter events, 66.8 us)
Async XLA Ops:
  3.6 12.9 %collective-permute-start = (bf16[2048,256]{1,0:T(8,128)(2,1)S(1)}, bf16[2048,256]{1,0:T(8,128)(2,1)S(1)}, u32[]{:S(2)}, u32[]{:S(2)}) collective-permute-start(bf16[2048,256]{1,0:T(8,128)(2,1)S(1)} %get-tuple-element.86), channel_id=1, source_target_pairs={{0,1},{1,0},{2,3},{3,2},{4,5},{5,4},{6,7},{7,6},{8,9},{9,8},{10,11... | collective-permute-start | bytes 3145736 | tf_op jit(solution)/shard_map/ppermute | solution.py:21
  4.2 12.5 %collective-permute-start.2 = (bf16[512,256]{1,0:T(8,128)(2,1)S(1)}, bf16[512,256]{1,0:T(8,128)(2,1)S(1)}, u32[]{:S(2)}, u32[]{:S(2)}) collective-permute-start(bf16[512,256]{1,0:T(8,128)(2,1)S(1)} %get-tuple-element.91), channel_id=1, source_target_pairs={{0,8},{8,0},{16,24},{24,16},{1,9},{9,1},{17,25},{25,17},{2,10},{10... | collective-permute-start | bytes 786440 | tf_op jit(solution)/shard_map/ppermute | solution.py:21
  6.7 14.0 %collective-permute-start.3 = (bf16[512,256]{1,0:T(8,128)(2,1)S(1)}, bf16[512,256]{1,0:T(8,128)(2,1)S(1)}, u32[]{:S(2)}, u32[]{:S(2)}) collective-permute-start(bf16[512,256]{1,0:T(8,128)(2,1)S(1)} %get-tuple-element.92), channel_id=1, source_target_pairs={{0,16},{8,24},{16,0},{24,8},{1,17},{9,25},{17,1},{25,9},{2,18},{10... | collective-permute-start | bytes 786440 | tf_op jit(solution)/shard_map/ppermute | solution.py:21
  8.2 12.5 %collective-permute-start.4 = (bf16[512,256]{1,0:T(8,128)(2,1)S(1)}, bf16[512,256]{1,0:T(8,128)(2,1)S(1)}, u32[]{:S(2)}, u32[]{:S(2)}) collective-permute-start(bf16[512,256]{1,0:T(8,128)(2,1)S(1)} %get-tuple-element.93), channel_id=1, source_target_pairs={{0,24},{8,16},{16,8},{24,0},{1,25},{9,17},{17,9},{25,1},{2,26},{10... | collective-permute-start | bytes 786440 | tf_op jit(solution)/shard_map/ppermute | solution.py:21
  13.7 13.8 %collective-permute-start.7 = (bf16[512,256]{1,0:T(8,128)(2,1)S(1)}, bf16[512,256]{1,0:T(8,128)(2,1)S(1)}, u32[]{:S(2)}, u32[]{:S(2)}) collective-permute-start(bf16[512,256]{1,0:T(8,128)(2,1)S(1)} %shard_map.189.refs_0_), channel_id=1, source_target_pairs={{0,4},{1,5},{2,6},{3,7},{4,0},{5,1},{6,2},{7,3},{8,12},{9,13},{10,... | collective-permute-start | bytes 786440 | tf_op jit(solution)/shard_map/ppermute | solution.py:21
  20.8 14.9 %collective-permute-start.5 = (bf16[1024,256]{1,0:T(8,128)(2,1)S(1)}, bf16[1024,256]{1,0:T(8,128)(2,1)S(1)}, u32[]{:S(2)}, u32[]{:S(2)}) collective-permute-start(bf16[1024,256]{1,0:T(8,128)(2,1)S(1)} %get-tuple-element.95), channel_id=1, source_target_pairs={{0,8},{8,0},{16,24},{24,16},{1,9},{9,1},{17,25},{25,17},{2,10},{10... | collective-permute-start | bytes 1572872 | tf_op jit(solution)/shard_map/ppermute | solution.py:21
  27.5 24.2 %collective-permute-start.6 = (bf16[1024,256]{1,0:T(8,128)(2,1)S(1)}, bf16[1024,256]{1,0:T(8,128)(2,1)S(1)}, u32[]{:S(2)}, u32[]{:S(2)}) collective-permute-start(bf16[1024,256]{1,0:T(8,128)(2,1)S(1)} %get-tuple-element.97), channel_id=1, source_target_pairs={{0,16},{8,24},{16,0},{24,8},{1,17},{9,25},{17,1},{25,9},{2,18},{10... | collective-permute-start | bytes 1572872 | tf_op jit(solution)/shard_map/ppermute | solution.py:21
  29.0 22.8 %collective-permute-start.8 = (bf16[1024,256]{1,0:T(8,128)(2,1)S(1)}, bf16[1024,256]{1,0:T(8,128)(2,1)S(1)}, u32[]{:S(2)}, u32[]{:S(2)}) collective-permute-start(bf16[1024,256]{1,0:T(8,128)(2,1)S(1)} %get-tuple-element.99), channel_id=1, source_target_pairs={{0,24},{8,16},{16,8},{24,0},{1,25},{9,17},{17,9},{25,1},{2,26},{10... | collective-permute-start | bytes 1572872 | tf_op jit(solution)/shard_map/ppermute | solution.py:21
  30.4 20.9 %collective-permute-start.10 = (bf16[512,256]{1,0:T(8,128)(2,1)S(1)}, bf16[512,256]{1,0:T(8,128)(2,1)S(1)}, u32[]{:S(2)}, u32[]{:S(2)}) collective-permute-start(bf16[512,256]{1,0:T(8,128)(2,1)S(1)} %get-tuple-element.107), channel_id=1, source_target_pairs={{0,4},{1,5},{2,6},{3,7},{4,0},{5,1},{6,2},{7,3},{8,12},{9,13},{10,... | collective-permute-start | bytes 786440 | tf_op jit(solution)/shard_map/ppermute | solution.py:21
  30.4 20.9 %collective-permute-start.11 = (bf16[512,256]{1,0:T(8,128)(2,1)S(1)}, bf16[512,256]{1,0:T(8,128)(2,1)S(1)}, u32[]{:S(2)}, u32[]{:S(2)}) collective-permute-start(bf16[512,256]{1,0:T(8,128)(2,1)S(1)} %get-tuple-element.108), channel_id=1, source_target_pairs={{0,6},{1,7},{2,4},{3,5},{4,2},{5,3},{6,0},{7,1},{8,14},{9,15},{10,... | collective-permute-start | bytes 786440 | tf_op jit(solution)/shard_map/ppermute | solution.py:21
  35.7 15.5 %collective-permute-start.9 = (bf16[512,256]{1,0:T(8,128)(2,1)S(1)}, bf16[512,256]{1,0:T(8,128)(2,1)S(1)}, u32[]{:S(2)}, u32[]{:S(2)}) collective-permute-start(bf16[512,256]{1,0:T(8,128)(2,1)S(1)} %get-tuple-element.106), channel_id=1, source_target_pairs={{0,2},{1,3},{2,0},{3,1},{4,6},{5,7},{6,4},{7,5},{8,10},{9,11},{10,... | collective-permute-start | bytes 786440 | tf_op jit(solution)/shard_map/ppermute | solution.py:21
  51.8 26.8 %collective-permute-start.15 = (bf16[1280,256]{1,0:T(8,128)(2,1)S(1)}, bf16[1280,256]{1,0:T(8,128)(2,1)S(1)}, u32[]{:S(2)}, u32[]{:S(2)}) collective-permute-start(bf16[1280,256]{1,0:T(8,128)(2,1)S(1)} %get-tuple-element.120.refs_0_), channel_id=1, source_target_pairs={{0,8},{8,0},{16,24},{24,16},{1,9},{9,1},{17,25},{25,17},{2,10},{10... | collective-permute-start | bytes 1966088 | tf_op jit(solution)/shard_map/ppermute | solution.py:21
  53.1 25.6 %collective-permute-start.16 = (bf16[1120,256]{1,0:T(8,128)(2,1)S(1)}, bf16[1120,256]{1,0:T(8,128)(2,1)S(1)}, u32[]{:S(2)}, u32[]{:S(2)}) collective-permute-start(bf16[1120,256]{1,0:T(8,128)(2,1)S(1)} %get-tuple-element.122.refs_2_), channel_id=1, source_target_pairs={{0,16},{8,24},{16,0},{24,8},{1,17},{9,25},{17,1},{25,9},{2,18},{10... | collective-permute-start | bytes 1720328 | tf_op jit(solution)/shard_map/ppermute | solution.py:21
  54.6 14.0 %collective-permute-start.12 = (bf16[512,256]{1,0:T(8,128)(2,1)S(1)}, bf16[512,256]{1,0:T(8,128)(2,1)S(1)}, u32[]{:S(2)}, u32[]{:S(2)}) collective-permute-start(bf16[512,256]{1,0:T(8,128)(2,1)S(1)} %get-tuple-element.110), channel_id=1, source_target_pairs={{0,2},{1,3},{2,0},{3,1},{4,6},{5,7},{6,4},{7,5},{8,10},{9,11},{10,... | collective-permute-start | bytes 786440 | tf_op jit(solution)/shard_map/ppermute | solution.py:21
  57.6 21.0 %collective-permute-start.13 = (bf16[512,256]{1,0:T(8,128)(2,1)S(1)}, bf16[512,256]{1,0:T(8,128)(2,1)S(1)}, u32[]{:S(2)}, u32[]{:S(2)}) collective-permute-start(bf16[512,256]{1,0:T(8,128)(2,1)S(1)} %get-tuple-element.117), channel_id=1, source_target_pairs={{0,4},{1,5},{2,6},{3,7},{4,0},{5,1},{6,2},{7,3},{8,12},{9,13},{10,... | collective-permute-start | bytes 786440 | tf_op jit(solution)/shard_map/ppermute | solution.py:21
  59.8 18.9 %collective-permute-start.14 = (bf16[512,256]{1,0:T(8,128)(2,1)S(1)}, bf16[512,256]{1,0:T(8,128)(2,1)S(1)}, u32[]{:S(2)}, u32[]{:S(2)}) collective-permute-start(bf16[512,256]{1,0:T(8,128)(2,1)S(1)} %get-tuple-element.118), channel_id=1, source_target_pairs={{0,6},{1,7},{2,4},{3,5},{4,2},{5,3},{6,0},{7,1},{8,14},{9,15},{10,... | collective-permute-start | bytes 786440 | tf_op jit(solution)/shard_map/ppermute | solution.py:21
  78.8 23.0 %collective-permute-start.22 = (bf16[1536,256]{1,0:T(8,128)(2,1)S(1)}, bf16[1536,256]{1,0:T(8,128)(2,1)S(1)}, u32[]{:S(2)}, u32[]{:S(2)}) collective-permute-start(bf16[1536,256]{1,0:T(8,128)(2,1)S(1)} %get-tuple-element.131.refs_0_), channel_id=1, source_target_pairs={{0,16},{8,24},{16,0},{24,8},{1,17},{9,25},{17,1},{25,9},{2,18},{10... | collective-permute-start | bytes 2359304 | tf_op jit(solution)/shard_map/ppermute | solution.py:21
  79.4 22.4 %collective-permute-start.23 = (bf16[1024,256]{1,0:T(8,128)(2,1)S(1)}, bf16[1024,256]{1,0:T(8,128)(2,1)S(1)}, u32[]{:S(2)}, u32[]{:S(2)}) collective-permute-start(bf16[1024,256]{1,0:T(8,128)(2,1)S(1)} %get-tuple-element.132.refs_2_), channel_id=1, source_target_pairs={{0,8},{8,0},{16,24},{24,16},{1,9},{9,1},{17,25},{25,17},{2,10},{10... | collective-permute-start | bytes 1572872 | tf_op jit(solution)/shard_map/ppermute | solution.py:21
  102.6 26.4 %collective-permute-start.36 = (bf16[1216,256]{1,0:T(8,128)(2,1)S(1)}, bf16[1216,256]{1,0:T(8,128)(2,1)S(1)}, u32[]{:S(2)}, u32[]{:S(2)}) collective-permute-start(bf16[1216,256]{1,0:T(8,128)(2,1)S(1)} %get-tuple-element.156.refs_2_), channel_id=1, source_target_pairs={{0,8},{8,0},{16,24},{24,16},{1,9},{9,1},{17,25},{25,17},{2,10},{10... | collective-permute-start | bytes 1867784 | tf_op jit(solution)/shard_map/ppermute | solution.py:21
  102.6 26.4 %collective-permute-start.35 = (bf16[1024,256]{1,0:T(8,128)(2,1)S(1)}, bf16[1024,256]{1,0:T(8,128)(2,1)S(1)}, u32[]{:S(2)}, u32[]{:S(2)}) collective-permute-start(bf16[1024,256]{1,0:T(8,128)(2,1)S(1)} %get-tuple-element.154.refs_0_), channel_id=1, source_target_pairs={{0,16},{8,24},{16,0},{24,8},{1,17},{9,25},{17,1},{25,9},{2,18},{10... | collective-permute-start | bytes 1572872 | tf_op jit(solution)/shard_map/ppermute | solution.py:21
  129.2 15.7 %collective-permute-start.38 = (bf16[2432,256]{1,0:T(8,128)(2,1)S(1)}, bf16[2432,256]{1,0:T(8,128)(2,1)S(1)}, u32[]{:S(2)}, u32[]{:S(2)}) collective-permute-start(bf16[2432,256]{1,0:T(8,128)(2,1)S(1)} %get-tuple-element.158.refs_6_), channel_id=1, source_target_pairs={{0,1},{1,0},{2,3},{3,2},{4,5},{5,4},{6,7},{7,6},{8,9},{9,8},{10,11... | collective-permute-start | bytes 3735560 | tf_op jit(solution)/shard_map/ppermute | solution.py:21
  129.3 15.6 %collective-permute-start.37 = (bf16[2048,256]{1,0:T(8,128)(2,1)S(1)}, bf16[2048,256]{1,0:T(8,128)(2,1)S(1)}, u32[]{:S(2)}, u32[]{:S(2)}) collective-permute-start(bf16[2048,256]{1,0:T(8,128)(2,1)S(1)} %get-tuple-element.157.refs_4_), channel_id=1, source_target_pairs={{0,1},{1,0},{2,3},{3,2},{4,5},{5,4},{6,7},{7,6},{8,9},{9,8},{10,11... | collective-permute-start | bytes 3145736 | tf_op jit(solution)/shard_map/ppermute | solution.py:21
  131.6 13.3 %collective-permute-start.32 = (bf16[64,1024]{1,0:T(8,128)(2,1)S(1)}, bf16[64,1024]{1,0:T(8,128)(2,1)S(1)}, u32[]{:S(2)}, u32[]{:S(2)}) collective-permute-start(bf16[64,1024]{1,0:T(8,128)(2,1)S(1)} %get-tuple-element.151.refs_0_), channel_id=1, source_target_pairs={{0,4},{1,5},{2,6},{3,7},{4,0},{5,1},{6,2},{7,3},{8,12},{9,13},{10,... | collective-permute-start | bytes 393224 | tf_op jit(solution)/shard_map/ppermute | solution.py:21
  160.2 12.4 %collective-permute-start.43 = (bf16[64,1024]{1,0:T(8,128)(2,1)S(1)}, bf16[64,1024]{1,0:T(8,128)(2,1)S(1)}, u32[]{:S(2)}, u32[]{:S(2)}) collective-permute-start(bf16[64,1024]{1,0:T(8,128)(2,1)S(1)} %shard_map.209.refs_0_), channel_id=1, source_target_pairs={{0,4},{1,5},{2,6},{3,7},{4,0},{5,1},{6,2},{7,3},{8,12},{9,13},{10,... | collective-permute-start | bytes 393224 | tf_op jit(solution)/shard_map/ppermute | solution.py:21
  (44 other events, 362.1 us)

commit v5 on v4

--- a/solution.py
+++ b/solution.py
@@ -770,14 +770,10 @@
         cache_len,
         fresh=fresh,
     )
-    state = self_attend(
-        lens, query_t, band, far[1 : chips // 2], far_places[1 : chips // 2], cache_len, state=state
-    )
-
     moved_a = xor_send(after(later_a, far[0]), "req", up_strides[0])
     moved_b = xor_send(after(later_b, far[0]), "req", down_strides[0])
     w_query, w_wide, w_cross, w_down = req_split(
-        [after(later_a, state[0], *far[1:]), later_b],
+        [after(later_a, state[0], *reordered(far)[1:]), later_b],
         [moved_a, moved_b],
         [up_strides[0], down_strides[0]],
         [all_depth + depth, chips * width_dev],
@@ -788,8 +784,8 @@
         lens,
         query_t,
         band,
-        far[chips // 2 :],
-        far_places[chips // 2 :],
+        reordered(far)[1:],
+        reordered(far_places)[1:],
         cache_len,
         state=state,
         last_call=True,
@@ -810,13 +806,13 @@
     parts = chip_sends(parts)
     last = [up_strides[-1], down_strides[-1]]
     w_query, w_cross = req_stack_two(
-        [after(w_query, *parts[1:]), w_cross], [moved_a, moved_b], last
+        [after(w_query, *reordered(parts)[1:]), w_cross], [moved_a, moved_b], last
     )
     w_query = (w_query, xor_send(w_query, "blk", 1))
     w_cross = (w_cross, xor_send(w_cross, "blk", 1))
     residual = after(residual, w_cross[1])
-    w_wide, moved_a = gather_on(after(w_wide, *parts[1:]), up_strides)
-    w_down, moved_b = gather_on(after(w_down, *parts[1:]), down_strides)
+    w_wide, moved_a = gather_on(after(w_wide, *reordered(parts)[1:]), up_strides)
+    w_down, moved_b = gather_on(after(w_down, *reordered(parts)[1:]), down_strides)
     total, *queries = local_call(
         functools.partial(query_kernel, range(req_count), chips),
         [norm_gain, residual, *reordered(parts), *w_query],
@@ -855,7 +851,7 @@
 
     parts = local_call(
         functools.partial(ffn_kernel, range(req_count), down_owners, chips, hidden_dev),
-        [*reordered(blocks), *w_wide, *w_down],
+        [*blocks, *w_wide, *w_down],
         parts_out,
         scratch=[partial_ref, partial_ref],
         flops=12 * half * width * hidden_dev,
@@ -863,7 +859,7 @@
     )
     final = local_call(
         sum_kernel,
-        [residual, *reordered(chip_sends(restored(parts)))],
+        [residual, *reordered(chip_sends(parts))],
         [shaped((share, width))],
     )[0]
 

time: 175 us -> 172 us (0.983)
  Pallas kernels: 28.6 us -> 22.9 us
  starting transfers between devices: 62.3 us -> 65.2 us
    pallas_call x3 -> x2, Pallas kernels: 11.3 us -> 5.54 us  [self_attend(): pl.pallas_call(functools.partial(self_kernel, cache_len, places, first_ca...]
    ppermute x49, starting transfers between devices: 62.3 us -> 65.2 us  [xor_send(): return lax.ppermute(value, axis, [(i, i ^ step) for i in range(size)])]
  transfers between devices with their start and end apart: 49 -> 49, of which waited for: 24 -> 23; matrix products, arithmetic and copies ran while one was open for 0% -> 0% of each run, Pallas kernels for 14% -> 11%
where the time goes in v5:
time: 172 us; the launch traced here: 171 us
  waiting for transfers between devices  79.5 us (46%)
  starting transfers between devices  65.2 us (38%)
  Pallas kernels  22.9 us (13%)
  local copies, waits for them, and re-layouts  2.36 us (1%)
    ppermute x49, waiting for transfers between devices, xor_send(): return lax.ppermute(value, axis, [(i, i ^ step) for i in range(size)])  79.5 us
    ppermute x49, starting transfers between devices, xor_send(): return lax.ppermute(value, axis, [(i, i ^ step) for i in range(size)])  65.2 us
    pallas_call x23, Pallas kernels, local_call(): pl.pallas_call(kernel, out_shape=list(outs), in_specs=[SMEM] * smem + [VM...  13.1 us
    pallas_call x2, Pallas kernels, self_attend(): pl.pallas_call(functools.partial(self_kernel, cache_len, places, first_ca...  5.54 us
    pallas_call x1, Pallas kernels, make_band(): pl.pallas_call(functools.partial(band_kernel, heads_dev, cache_len, width...  4.22 us
  transfers between devices with their start and end apart: 49, of which 23 were waited for; matrix products, arithmetic and copies ran while one was open for 0% of the time, Pallas kernels for 11%

profile of v5, /device:TPU:0, one launch (start us, length us, event | category | flops | bytes accessed | tf_op | source)
XLA Modules:
  0.0 171.0 jit_solution(17903930584872228803)
XLA Ops:
  4.2 2.6 %collective-permute-start.2 = (bf16[512,256]{1,0:T(8,128)(2,1)S(1)}, bf16[512,256]{1,0:T(8,128)(2,1)S(1)}, u32[]{:S(2)}, u32[]{:S(2)}) collective-permute-start(bf16[512,256]{1,0:T(8,128)(2,1)S(1)} %get-tuple-element.88), channel_id=1, source_target_pairs={{0,8},{8,0},{16,24},{24,16},{1,9},{9,1},{17,25},{25,17},{2,10},{10... | collective-permute-start | bytes 786440 | tf_op jit(solution)/shard_map/ppermute | solution.py:21
  10.7 3.0 %collective-permute-done.1.refs_1_ = bf16[256,256]{1,0:T(8,128)(2,1)S(1)} collective-permute-done((bf16[256,256]{1,0:T(8,128)(2,1)S(1)}, bf16[256,256]{1,0:T(8,128)(2,1)S(1)}, u32[]{:S(2)}, u32[]{:S(2)}) %collective-permute-start.1) | collective-permute-done | bytes 131104 | tf_op jit(solution)/shard_map/ppermute | solution.py:21
  13.7 2.8 %collective-permute-start.7 = (bf16[512,256]{1,0:T(8,128)(2,1)S(1)}, bf16[512,256]{1,0:T(8,128)(2,1)S(1)}, u32[]{:S(2)}, u32[]{:S(2)}) collective-permute-start(bf16[512,256]{1,0:T(8,128)(2,1)S(1)} %shard_map.189.refs_0_), channel_id=1, source_target_pairs={{0,4},{1,5},{2,6},{3,7},{4,0},{5,1},{6,2},{7,3},{8,12},{9,13},{10,... | collective-permute-start | bytes 786440 | tf_op jit(solution)/shard_map/ppermute | solution.py:21
  16.7 4.1 %collective-permute-done.3.refs_2_ = bf16[512,256]{1,0:T(8,128)(2,1)S(1)} collective-permute-done((bf16[512,256]{1,0:T(8,128)(2,1)S(1)}, bf16[512,256]{1,0:T(8,128)(2,1)S(1)}, u32[]{:S(2)}, u32[]{:S(2)}) %collective-permute-start.3) | collective-permute-done | bytes 262176 | tf_op jit(solution)/shard_map/ppermute | solution.py:21
  22.1 5.4 %collective-permute-done.7.refs_1_ = bf16[512,256]{1,0:T(8,128)(2,1)S(1)} collective-permute-done((bf16[512,256]{1,0:T(8,128)(2,1)S(1)}, bf16[512,256]{1,0:T(8,128)(2,1)S(1)}, u32[]{:S(2)}, u32[]{:S(2)}) %collective-permute-start.7) | collective-permute-done | bytes 262176 | tf_op jit(solution)/shard_map/ppermute | solution.py:21
  30.4 3.5 %collective-permute-start.11 = (bf16[512,256]{1,0:T(8,128)(2,1)S(1)}, bf16[512,256]{1,0:T(8,128)(2,1)S(1)}, u32[]{:S(2)}, u32[]{:S(2)}) collective-permute-start(bf16[512,256]{1,0:T(8,128)(2,1)S(1)} %get-tuple-element.105), channel_id=1, source_target_pairs={{0,6},{1,7},{2,4},{3,5},{4,2},{5,3},{6,0},{7,1},{8,14},{9,15},{10,... | collective-permute-start | bytes 786440 | tf_op jit(solution)/shard_map/ppermute | solution.py:21
  37.4 4.2 %shard_map.194.refs_4_ = f32[2,128,5376]{2,1,0:T(8,128)S(1)} custom-call(s32[4]{0:T(128)S(1)} %copy-done.12, s32[4]{0:T(128)S(1)} %copy-done.13, f32[16,32]{1,0:T(8,128)S(1)} %bitcast.11, s32[1,4608]{1,0:T(1,128)S(1)} %broadcast_in_dim.6.bucket_ref), custom_call_target="tpu_custom_call" | custom-call | flops 11010048 | bytes 5505024 | tf_op jit(solution)/shard_map/pallas_call | solution.py:310
  41.7 9.6 %collective-permute-done.10.refs_7_.refs_2_ = bf16[512,256]{1,0:T(8,128)(2,1)S(1)} collective-permute-done((bf16[512,256]{1,0:T(8,128)(2,1)S(1)}, bf16[512,256]{1,0:T(8,128)(2,1)S(1)}, u32[]{:S(2)}, u32[]{:S(2)}) %collective-permute-start.10) | collective-permute-done | bytes 262176 | tf_op jit(solution)/shard_map/ppermute | solution.py:21
  54.6 2.7 %collective-permute-start.12 = (bf16[512,256]{1,0:T(8,128)(2,1)S(1)}, bf16[512,256]{1,0:T(8,128)(2,1)S(1)}, u32[]{:S(2)}, u32[]{:S(2)}) collective-permute-start(bf16[512,256]{1,0:T(8,128)(2,1)S(1)} %get-tuple-element.110), channel_id=1, source_target_pairs={{0,4},{1,5},{2,6},{3,7},{4,0},{5,1},{6,2},{7,3},{8,12},{9,13},{10,... | collective-permute-start | bytes 786440 | tf_op jit(solution)/shard_map/ppermute | solution.py:21
  57.3 2.6 %collective-permute-start.13 = (bf16[512,256]{1,0:T(8,128)(2,1)S(1)}, bf16[512,256]{1,0:T(8,128)(2,1)S(1)}, u32[]{:S(2)}, u32[]{:S(2)}) collective-permute-start(bf16[512,256]{1,0:T(8,128)(2,1)S(1)} %get-tuple-element.111), channel_id=1, source_target_pairs={{0,6},{1,7},{2,4},{3,5},{4,2},{5,3},{6,0},{7,1},{8,14},{9,15},{10,... | collective-permute-start | bytes 786440 | tf_op jit(solution)/shard_map/ppermute | solution.py:21
  61.6 4.5 %shard_map.196 = (f32[2,128,512]{2,1,0:T(8,128)S(1)}, f32[2,1,512]{2,1,0:T(1,128)S(1)}, f32[2,1,512]{2,1,0:T(1,128)S(1)}) custom-call(s32[4]{0:T(128)S(1)} %copy-done.12, s32[4]{0:T(128)S(1)} %copy-done.13, s32[4]{0:T(128)S(1)} %copy-done.14, bf16[2,128,512]{2,1,0:T(8,128)(2,1)S(1)} %get-tuple-element.101.refs_3_, f32[2,128,5376]{2,1,0:T(8,128)S(1)} %shard_map.194.refs_4_, ...), custom_call_target="tpu_custom_call" | custom-call | flops 1610612736 | bytes 7077888 | tf_op jit(solution)/shard_map/pallas_call | solution.py:429
  66.1 9.5 %collective-permute-done.12.refs_5_.refs_6_ = bf16[512,256]{1,0:T(8,128)(2,1)S(1)} collective-permute-done((bf16[512,256]{1,0:T(8,128)(2,1)S(1)}, bf16[512,256]{1,0:T(8,128)(2,1)S(1)}, u32[]{:S(2)}, u32[]{:S(2)}) %collective-permute-start.12) | collective-permute-done | bytes 262176 | tf_op jit(solution)/shard_map/ppermute | solution.py:21
  81.2 7.4 %collective-permute-start.19 = (bf16[64,1024]{1,0:T(8,128)(2,1)S(1)}, bf16[64,1024]{1,0:T(8,128)(2,1)S(1)}, u32[]{:S(2)}, u32[]{:S(2)}) collective-permute-start(bf16[64,1024]{1,0:T(8,128)(2,1)S(1)} %get-tuple-element.122), channel_id=1, source_target_pairs={{0,4},{1,5},{2,6},{3,7},{4,0},{5,1},{6,2},{7,3},{8,12},{9,13},{10,... | collective-permute-start | bytes 393224 | tf_op jit(solution)/shard_map/ppermute | solution.py:21
  89.7 8.9 %collective-permute-done.19.refs_3_ = bf16[64,1024]{1,0:T(8,128)(2,1)S(1)} collective-permute-done((bf16[64,1024]{1,0:T(8,128)(2,1)S(1)}, bf16[64,1024]{1,0:T(8,128)(2,1)S(1)}, u32[]{:S(2)}, u32[]{:S(2)}) %collective-permute-start.19) | collective-permute-done | bytes 131104 | tf_op jit(solution)/shard_map/ppermute | solution.py:21
  100.4 4.0 %collective-permute-start.36 = (bf16[1216,256]{1,0:T(8,128)(2,1)S(1)}, bf16[1216,256]{1,0:T(8,128)(2,1)S(1)}, u32[]{:S(2)}, u32[]{:S(2)}) collective-permute-start(bf16[1216,256]{1,0:T(8,128)(2,1)S(1)} %get-tuple-element.150.refs_2_), channel_id=1, source_target_pairs={{0,8},{8,0},{16,24},{24,16},{1,9},{9,1},{17,25},{25,17},{2,10},{10... | collective-permute-start | bytes 1867784 | tf_op jit(solution)/shard_map/ppermute | solution.py:21
  105.4 3.0 %collective-permute-start.26 = (bf16[64,256]{1,0:T(8,128)(2,1)S(1)}, bf16[64,256]{1,0:T(8,128)(2,1)S(1)}, u32[]{:S(2)}, u32[]{:S(2)}) collective-permute-start(bf16[64,256]{1,0:T(8,128)(2,1)S(1)} %get-tuple-element.133), channel_id=1, source_target_pairs={{0,4},{1,5},{2,6},{3,7},{4,0},{5,1},{6,2},{7,3},{8,12},{9,13},{10,... | collective-permute-start | bytes 98312 | tf_op jit(solution)/shard_map/ppermute | solution.py:21
  111.2 3.0 %collective-permute-done.27.refs_2_ = bf16[64,256]{1,0:T(8,128)(2,1)S(1)} collective-permute-done((bf16[64,256]{1,0:T(8,128)(2,1)S(1)}, bf16[64,256]{1,0:T(8,128)(2,1)S(1)}, u32[]{:S(2)}, u32[]{:S(2)}) %collective-permute-start.27) | collective-permute-done | bytes 32800 | tf_op jit(solution)/shard_map/ppermute | solution.py:21
  121.5 3.3 %collective-permute-done.31.refs_5_ = bf16[64,256]{1,0:T(8,128)(2,1)S(1)} collective-permute-done((bf16[64,256]{1,0:T(8,128)(2,1)S(1)}, bf16[64,256]{1,0:T(8,128)(2,1)S(1)}, u32[]{:S(2)}, u32[]{:S(2)}) %collective-permute-start.31) | collective-permute-done | bytes 32800 | tf_op jit(solution)/shard_map/ppermute | solution.py:21
  128.1 2.5 %collective-permute-start.32 = (bf16[64,1024]{1,0:T(8,128)(2,1)S(1)}, bf16[64,1024]{1,0:T(8,128)(2,1)S(1)}, u32[]{:S(2)}, u32[]{:S(2)}) collective-permute-start(bf16[64,1024]{1,0:T(8,128)(2,1)S(1)} %get-tuple-element.145.refs_0_), channel_id=1, source_target_pairs={{0,2},{1,3},{2,0},{3,1},{4,6},{5,7},{6,4},{7,5},{8,10},{9,11},{10,... | collective-permute-start | bytes 393224 | tf_op jit(solution)/shard_map/ppermute | solution.py:21
  130.7 3.9 %collective-permute-done.34.refs_3_ = bf16[64,1024]{1,0:T(8,128)(2,1)S(1)} collective-permute-done((bf16[64,1024]{1,0:T(8,128)(2,1)S(1)}, bf16[64,1024]{1,0:T(8,128)(2,1)S(1)}, u32[]{:S(2)}, u32[]{:S(2)}) %collective-permute-start.34) | collective-permute-done | bytes 131104 | tf_op jit(solution)/shard_map/ppermute | solution.py:21
  134.6 4.6 %collective-permute-done.33.refs_2_ = bf16[64,1024]{1,0:T(8,128)(2,1)S(1)} collective-permute-done((bf16[64,1024]{1,0:T(8,128)(2,1)S(1)}, bf16[64,1024]{1,0:T(8,128)(2,1)S(1)}, u32[]{:S(2)}, u32[]{:S(2)}) %collective-permute-start.33) | collective-permute-done | bytes 131104 | tf_op jit(solution)/shard_map/ppermute | solution.py:21
  145.8 6.3 %collective-permute-done.39.refs_2_ = bf16[64,1024]{1,0:T(8,128)(2,1)S(1)} collective-permute-done((bf16[64,1024]{1,0:T(8,128)(2,1)S(1)}, bf16[64,1024]{1,0:T(8,128)(2,1)S(1)}, u32[]{:S(2)}, u32[]{:S(2)}) %collective-permute-start.39) | collective-permute-done | bytes 131104 | tf_op jit(solution)/shard_map/ppermute | solution.py:21
  158.1 3.5 %collective-permute-done.44.refs_3_ = bf16[64,1024]{1,0:T(8,128)(2,1)S(1)} collective-permute-done((bf16[64,1024]{1,0:T(8,128)(2,1)S(1)}, bf16[64,1024]{1,0:T(8,128)(2,1)S(1)}, u32[]{:S(2)}, u32[]{:S(2)}) %collective-permute-start.44) | collective-permute-done | bytes 131104 | tf_op jit(solution)/shard_map/ppermute | solution.py:21
  161.6 6.8 %collective-permute-done.43.refs_2_ = bf16[64,1024]{1,0:T(8,128)(2,1)S(1)} collective-permute-done((bf16[64,1024]{1,0:T(8,128)(2,1)S(1)}, bf16[64,1024]{1,0:T(8,128)(2,1)S(1)}, u32[]{:S(2)}, u32[]{:S(2)}) %collective-permute-start.43) | collective-permute-done | bytes 131104 | tf_op jit(solution)/shard_map/ppermute | solution.py:21
  (140 shorter events, 58.1 us)
Async XLA Ops:
  3.6 12.9 %collective-permute-start = (bf16[2048,256]{1,0:T(8,128)(2,1)S(1)}, bf16[2048,256]{1,0:T(8,128)(2,1)S(1)}, u32[]{:S(2)}, u32[]{:S(2)}) collective-permute-start(bf16[2048,256]{1,0:T(8,128)(2,1)S(1)} %get-tuple-element.83), channel_id=1, source_target_pairs={{0,1},{1,0},{2,3},{3,2},{4,5},{5,4},{6,7},{7,6},{8,9},{9,8},{10,11... | collective-permute-start | bytes 3145736 | tf_op jit(solution)/shard_map/ppermute | solution.py:21
  4.2 12.5 %collective-permute-start.2 = (bf16[512,256]{1,0:T(8,128)(2,1)S(1)}, bf16[512,256]{1,0:T(8,128)(2,1)S(1)}, u32[]{:S(2)}, u32[]{:S(2)}) collective-permute-start(bf16[512,256]{1,0:T(8,128)(2,1)S(1)} %get-tuple-element.88), channel_id=1, source_target_pairs={{0,8},{8,0},{16,24},{24,16},{1,9},{9,1},{17,25},{25,17},{2,10},{10... | collective-permute-start | bytes 786440 | tf_op jit(solution)/shard_map/ppermute | solution.py:21
  6.7 14.0 %collective-permute-start.3 = (bf16[512,256]{1,0:T(8,128)(2,1)S(1)}, bf16[512,256]{1,0:T(8,128)(2,1)S(1)}, u32[]{:S(2)}, u32[]{:S(2)}) collective-permute-start(bf16[512,256]{1,0:T(8,128)(2,1)S(1)} %get-tuple-element.89), channel_id=1, source_target_pairs={{0,16},{8,24},{16,0},{24,8},{1,17},{9,25},{17,1},{25,9},{2,18},{10... | collective-permute-start | bytes 786440 | tf_op jit(solution)/shard_map/ppermute | solution.py:21
  8.2 12.5 %collective-permute-start.4 = (bf16[512,256]{1,0:T(8,128)(2,1)S(1)}, bf16[512,256]{1,0:T(8,128)(2,1)S(1)}, u32[]{:S(2)}, u32[]{:S(2)}) collective-permute-start(bf16[512,256]{1,0:T(8,128)(2,1)S(1)} %get-tuple-element.90), channel_id=1, source_target_pairs={{0,24},{8,16},{16,8},{24,0},{1,25},{9,17},{17,9},{25,1},{2,26},{10... | collective-permute-start | bytes 786440 | tf_op jit(solution)/shard_map/ppermute | solution.py:21
  13.7 13.8 %collective-permute-start.7 = (bf16[512,256]{1,0:T(8,128)(2,1)S(1)}, bf16[512,256]{1,0:T(8,128)(2,1)S(1)}, u32[]{:S(2)}, u32[]{:S(2)}) collective-permute-start(bf16[512,256]{1,0:T(8,128)(2,1)S(1)} %shard_map.189.refs_0_), channel_id=1, source_target_pairs={{0,4},{1,5},{2,6},{3,7},{4,0},{5,1},{6,2},{7,3},{8,12},{9,13},{10,... | collective-permute-start | bytes 786440 | tf_op jit(solution)/shard_map/ppermute | solution.py:21
  20.8 14.9 %collective-permute-start.5 = (bf16[1024,256]{1,0:T(8,128)(2,1)S(1)}, bf16[1024,256]{1,0:T(8,128)(2,1)S(1)}, u32[]{:S(2)}, u32[]{:S(2)}) collective-permute-start(bf16[1024,256]{1,0:T(8,128)(2,1)S(1)} %get-tuple-element.92), channel_id=1, source_target_pairs={{0,8},{8,0},{16,24},{24,16},{1,9},{9,1},{17,25},{25,17},{2,10},{10... | collective-permute-start | bytes 1572872 | tf_op jit(solution)/shard_map/ppermute | solution.py:21
  27.5 24.2 %collective-permute-start.6 = (bf16[1024,256]{1,0:T(8,128)(2,1)S(1)}, bf16[1024,256]{1,0:T(8,128)(2,1)S(1)}, u32[]{:S(2)}, u32[]{:S(2)}) collective-permute-start(bf16[1024,256]{1,0:T(8,128)(2,1)S(1)} %get-tuple-element.94), channel_id=1, source_target_pairs={{0,16},{8,24},{16,0},{24,8},{1,17},{9,25},{17,1},{25,9},{2,18},{10... | collective-permute-start | bytes 1572872 | tf_op jit(solution)/shard_map/ppermute | solution.py:21
  29.0 22.8 %collective-permute-start.8 = (bf16[1024,256]{1,0:T(8,128)(2,1)S(1)}, bf16[1024,256]{1,0:T(8,128)(2,1)S(1)}, u32[]{:S(2)}, u32[]{:S(2)}) collective-permute-start(bf16[1024,256]{1,0:T(8,128)(2,1)S(1)} %get-tuple-element.96), channel_id=1, source_target_pairs={{0,24},{8,16},{16,8},{24,0},{1,25},{9,17},{17,9},{25,1},{2,26},{10... | collective-permute-start | bytes 1572872 | tf_op jit(solution)/shard_map/ppermute | solution.py:21
  30.4 20.9 %collective-permute-start.10 = (bf16[512,256]{1,0:T(8,128)(2,1)S(1)}, bf16[512,256]{1,0:T(8,128)(2,1)S(1)}, u32[]{:S(2)}, u32[]{:S(2)}) collective-permute-start(bf16[512,256]{1,0:T(8,128)(2,1)S(1)} %get-tuple-element.104), channel_id=1, source_target_pairs={{0,4},{1,5},{2,6},{3,7},{4,0},{5,1},{6,2},{7,3},{8,12},{9,13},{10,... | collective-permute-start | bytes 786440 | tf_op jit(solution)/shard_map/ppermute | solution.py:21
  30.4 20.9 %collective-permute-start.11 = (bf16[512,256]{1,0:T(8,128)(2,1)S(1)}, bf16[512,256]{1,0:T(8,128)(2,1)S(1)}, u32[]{:S(2)}, u32[]{:S(2)}) collective-permute-start(bf16[512,256]{1,0:T(8,128)(2,1)S(1)} %get-tuple-element.105), channel_id=1, source_target_pairs={{0,6},{1,7},{2,4},{3,5},{4,2},{5,3},{6,0},{7,1},{8,14},{9,15},{10,... | collective-permute-start | bytes 786440 | tf_op jit(solution)/shard_map/ppermute | solution.py:21
  35.7 15.5 %collective-permute-start.9 = (bf16[512,256]{1,0:T(8,128)(2,1)S(1)}, bf16[512,256]{1,0:T(8,128)(2,1)S(1)}, u32[]{:S(2)}, u32[]{:S(2)}) collective-permute-start(bf16[512,256]{1,0:T(8,128)(2,1)S(1)} %get-tuple-element.103), channel_id=1, source_target_pairs={{0,2},{1,3},{2,0},{3,1},{4,6},{5,7},{6,4},{7,5},{8,10},{9,11},{10,... | collective-permute-start | bytes 786440 | tf_op jit(solution)/shard_map/ppermute | solution.py:21
  51.8 24.0 %collective-permute-start.15 = (bf16[1280,256]{1,0:T(8,128)(2,1)S(1)}, bf16[1280,256]{1,0:T(8,128)(2,1)S(1)}, u32[]{:S(2)}, u32[]{:S(2)}) collective-permute-start(bf16[1280,256]{1,0:T(8,128)(2,1)S(1)} %get-tuple-element.114.refs_0_), channel_id=1, source_target_pairs={{0,8},{8,0},{16,24},{24,16},{1,9},{9,1},{17,25},{25,17},{2,10},{10... | collective-permute-start | bytes 1966088 | tf_op jit(solution)/shard_map/ppermute | solution.py:21
  53.1 22.7 %collective-permute-start.16 = (bf16[1120,256]{1,0:T(8,128)(2,1)S(1)}, bf16[1120,256]{1,0:T(8,128)(2,1)S(1)}, u32[]{:S(2)}, u32[]{:S(2)}) collective-permute-start(bf16[1120,256]{1,0:T(8,128)(2,1)S(1)} %get-tuple-element.116.refs_2_), channel_id=1, source_target_pairs={{0,16},{8,24},{16,0},{24,8},{1,17},{9,25},{17,1},{25,9},{2,18},{10... | collective-permute-start | bytes 1720328 | tf_op jit(solution)/shard_map/ppermute | solution.py:21
  54.6 21.1 %collective-permute-start.12 = (bf16[512,256]{1,0:T(8,128)(2,1)S(1)}, bf16[512,256]{1,0:T(8,128)(2,1)S(1)}, u32[]{:S(2)}, u32[]{:S(2)}) collective-permute-start(bf16[512,256]{1,0:T(8,128)(2,1)S(1)} %get-tuple-element.110), channel_id=1, source_target_pairs={{0,4},{1,5},{2,6},{3,7},{4,0},{5,1},{6,2},{7,3},{8,12},{9,13},{10,... | collective-permute-start | bytes 786440 | tf_op jit(solution)/shard_map/ppermute | solution.py:21
  57.3 18.4 %collective-permute-start.13 = (bf16[512,256]{1,0:T(8,128)(2,1)S(1)}, bf16[512,256]{1,0:T(8,128)(2,1)S(1)}, u32[]{:S(2)}, u32[]{:S(2)}) collective-permute-start(bf16[512,256]{1,0:T(8,128)(2,1)S(1)} %get-tuple-element.111), channel_id=1, source_target_pairs={{0,6},{1,7},{2,4},{3,5},{4,2},{5,3},{6,0},{7,1},{8,14},{9,15},{10,... | collective-permute-start | bytes 786440 | tf_op jit(solution)/shard_map/ppermute | solution.py:21
  60.0 15.9 %collective-permute-start.14 = (bf16[512,256]{1,0:T(8,128)(2,1)S(1)}, bf16[512,256]{1,0:T(8,128)(2,1)S(1)}, u32[]{:S(2)}, u32[]{:S(2)}) collective-permute-start(bf16[512,256]{1,0:T(8,128)(2,1)S(1)} %get-tuple-element.112), channel_id=1, source_target_pairs={{0,2},{1,3},{2,0},{3,1},{4,6},{5,7},{6,4},{7,5},{8,10},{9,11},{10,... | collective-permute-start | bytes 786440 | tf_op jit(solution)/shard_map/ppermute | solution.py:21
  76.0 23.6 %collective-permute-start.22 = (bf16[1536,256]{1,0:T(8,128)(2,1)S(1)}, bf16[1536,256]{1,0:T(8,128)(2,1)S(1)}, u32[]{:S(2)}, u32[]{:S(2)}) collective-permute-start(bf16[1536,256]{1,0:T(8,128)(2,1)S(1)} %get-tuple-element.125.refs_0_), channel_id=1, source_target_pairs={{0,16},{8,24},{16,0},{24,8},{1,17},{9,25},{17,1},{25,9},{2,18},{10... | collective-permute-start | bytes 2359304 | tf_op jit(solution)/shard_map/ppermute | solution.py:21
  76.9 22.7 %collective-permute-start.23 = (bf16[1024,256]{1,0:T(8,128)(2,1)S(1)}, bf16[1024,256]{1,0:T(8,128)(2,1)S(1)}, u32[]{:S(2)}, u32[]{:S(2)}) collective-permute-start(bf16[1024,256]{1,0:T(8,128)(2,1)S(1)} %get-tuple-element.126.refs_2_), channel_id=1, source_target_pairs={{0,8},{8,0},{16,24},{24,16},{1,9},{9,1},{17,25},{25,17},{2,10},{10... | collective-permute-start | bytes 1572872 | tf_op jit(solution)/shard_map/ppermute | solution.py:21
  81.2 17.4 %collective-permute-start.19 = (bf16[64,1024]{1,0:T(8,128)(2,1)S(1)}, bf16[64,1024]{1,0:T(8,128)(2,1)S(1)}, u32[]{:S(2)}, u32[]{:S(2)}) collective-permute-start(bf16[64,1024]{1,0:T(8,128)(2,1)S(1)} %get-tuple-element.122), channel_id=1, source_target_pairs={{0,4},{1,5},{2,6},{3,7},{4,0},{5,1},{6,2},{7,3},{8,12},{9,13},{10,... | collective-permute-start | bytes 393224 | tf_op jit(solution)/shard_map/ppermute | solution.py:21
  100.4 25.1 %collective-permute-start.36 = (bf16[1216,256]{1,0:T(8,128)(2,1)S(1)}, bf16[1216,256]{1,0:T(8,128)(2,1)S(1)}, u32[]{:S(2)}, u32[]{:S(2)}) collective-permute-start(bf16[1216,256]{1,0:T(8,128)(2,1)S(1)} %get-tuple-element.150.refs_2_), channel_id=1, source_target_pairs={{0,8},{8,0},{16,24},{24,16},{1,9},{9,1},{17,25},{25,17},{2,10},{10... | collective-permute-start | bytes 1867784 | tf_op jit(solution)/shard_map/ppermute | solution.py:21
  104.4 21.1 %collective-permute-start.35 = (bf16[1024,256]{1,0:T(8,128)(2,1)S(1)}, bf16[1024,256]{1,0:T(8,128)(2,1)S(1)}, u32[]{:S(2)}, u32[]{:S(2)}) collective-permute-start(bf16[1024,256]{1,0:T(8,128)(2,1)S(1)} %get-tuple-element.148.refs_0_), channel_id=1, source_target_pairs={{0,16},{8,24},{16,0},{24,8},{1,17},{9,25},{17,1},{25,9},{2,18},{10... | collective-permute-start | bytes 1572872 | tf_op jit(solution)/shard_map/ppermute | solution.py:21
  125.7 13.5 %collective-permute-start.38 = (bf16[2432,256]{1,0:T(8,128)(2,1)S(1)}, bf16[2432,256]{1,0:T(8,128)(2,1)S(1)}, u32[]{:S(2)}, u32[]{:S(2)}) collective-permute-start(bf16[2432,256]{1,0:T(8,128)(2,1)S(1)} %get-tuple-element.152.refs_6_), channel_id=1, source_target_pairs={{0,1},{1,0},{2,3},{3,2},{4,5},{5,4},{6,7},{7,6},{8,9},{9,8},{10,11... | collective-permute-start | bytes 3735560 | tf_op jit(solution)/shard_map/ppermute | solution.py:21
  125.8 13.4 %collective-permute-start.37 = (bf16[2048,256]{1,0:T(8,128)(2,1)S(1)}, bf16[2048,256]{1,0:T(8,128)(2,1)S(1)}, u32[]{:S(2)}, u32[]{:S(2)}) collective-permute-start(bf16[2048,256]{1,0:T(8,128)(2,1)S(1)} %get-tuple-element.151.refs_4_), channel_id=1, source_target_pairs={{0,1},{1,0},{2,3},{3,2},{4,5},{5,4},{6,7},{7,6},{8,9},{9,8},{10,11... | collective-permute-start | bytes 3145736 | tf_op jit(solution)/shard_map/ppermute | solution.py:21
  155.6 12.7 %collective-permute-start.43 = (bf16[64,1024]{1,0:T(8,128)(2,1)S(1)}, bf16[64,1024]{1,0:T(8,128)(2,1)S(1)}, u32[]{:S(2)}, u32[]{:S(2)}) collective-permute-start(bf16[64,1024]{1,0:T(8,128)(2,1)S(1)} %shard_map.208.refs_0_), channel_id=1, source_target_pairs={{0,4},{1,5},{2,6},{3,7},{4,0},{5,1},{6,2},{7,3},{8,12},{9,13},{10,... | collective-permute-start | bytes 393224 | tf_op jit(solution)/shard_map/ppermute | solution.py:21
  (44 other events, 369.3 us)

commit v6 on v5

--- a/solution.py
+++ b/solution.py
@@ -352,7 +352,8 @@
         for t in range(0, size, TILE):
             bias = band_ref[0, :, pl.ds(pl.multiple_of(begin - t, TILE), rows)]
             scores = score_ref[t : t + TILE, :] + bias
-            scores = jnp.where(admit(t), scores, NEG_FILL)
+            if admit is not None:
+                scores = jnp.where(admit(t), scores, NEG_FILL)
             score_ref[t : t + TILE, :] = scores
             top = jnp.maximum(top, jnp.max(scores, axis=0, keepdims=True))
         weights = jnp.exp(score_ref[:size, :] - top)
@@ -384,13 +385,20 @@
     for block, place_of in zip(blocks, places):
         first = (blk ^ place_of) * block.shape[0]
 
-        @pl.when(first < old_len)
-        def _(block=block, first=first):
+        begin = cache_len - TILE - first
+        whole = first + block.shape[0] <= old_len
+
+        @pl.when(whole)
+        def _(block=block, begin=begin):
+            attend(block[...], begin, None)
+
+        @pl.when((first < old_len) & jnp.logical_not(whole))
+        def _(block=block, begin=begin, first=first):
             def admit(t):
                 keys = first + t + lax.broadcasted_iota(jnp.int32, (TILE, rows), 0)
                 return keys < old_len
 
-            attend(block[...], cache_len - TILE - first, admit)
+            attend(block[...], begin, admit)
 
     if last_call:
         total_ref[0, :HD, :] = total_ref[0, HD:, :] / norm_ref[0]

time: 172 us -> 173 us (level)
  no operation moved by 1% of the time
where the time goes in v6:
time: 173 us; the launch traced here: 172 us
  waiting for transfers between devices  78.8 us (46%)
  starting transfers between devices  66.5 us (38%)
  Pallas kernels  23.2 us (13%)
  local copies, waits for them, and re-layouts  2.36 us (1%)
    ppermute x49, waiting for transfers between devices, xor_send(): return lax.ppermute(value, axis, [(i, i ^ step) for i in range(size)])  78.8 us
    ppermute x49, starting transfers between devices, xor_send(): return lax.ppermute(value, axis, [(i, i ^ step) for i in range(size)])  66.5 us
    pallas_call x23, Pallas kernels, local_call(): pl.pallas_call(kernel, out_shape=list(outs), in_specs=[SMEM] * smem + [VM...  13.3 us
    pallas_call x2, Pallas kernels, self_attend(): pl.pallas_call(functools.partial(self_kernel, cache_len, places, first_ca...  5.65 us
    pallas_call x1, Pallas kernels, make_band(): pl.pallas_call(functools.partial(band_kernel, heads_dev, cache_len, width...  4.22 us
  transfers between devices with their start and end apart: 49, of which 23 were waited for; matrix products, arithmetic and copies ran while one was open for 0% of the time, Pallas kernels for 11%

profile of v6, /device:TPU:0, one launch (start us, length us, event | category | flops | bytes accessed | tf_op | source)
XLA Modules:
  0.0 171.9 jit_solution(17636643843466820759)
XLA Ops:
  4.2 2.6 %collective-permute-start.2 = (bf16[512,256]{1,0:T(8,128)(2,1)S(1)}, bf16[512,256]{1,0:T(8,128)(2,1)S(1)}, u32[]{:S(2)}, u32[]{:S(2)}) collective-permute-start(bf16[512,256]{1,0:T(8,128)(2,1)S(1)} %get-tuple-element.88), channel_id=1, source_target_pairs={{0,8},{8,0},{16,24},{24,16},{1,9},{9,1},{17,25},{25,17},{2,10},{10... | collective-permute-start | bytes 786440 | tf_op jit(solution)/shard_map/ppermute | solution.py:21
  10.7 3.0 %collective-permute-done.1.refs_1_ = bf16[256,256]{1,0:T(8,128)(2,1)S(1)} collective-permute-done((bf16[256,256]{1,0:T(8,128)(2,1)S(1)}, bf16[256,256]{1,0:T(8,128)(2,1)S(1)}, u32[]{:S(2)}, u32[]{:S(2)}) %collective-permute-start.1) | collective-permute-done | bytes 131104 | tf_op jit(solution)/shard_map/ppermute | solution.py:21
  13.7 2.8 %collective-permute-start.7 = (bf16[512,256]{1,0:T(8,128)(2,1)S(1)}, bf16[512,256]{1,0:T(8,128)(2,1)S(1)}, u32[]{:S(2)}, u32[]{:S(2)}) collective-permute-start(bf16[512,256]{1,0:T(8,128)(2,1)S(1)} %shard_map.189.refs_0_), channel_id=1, source_target_pairs={{0,4},{1,5},{2,6},{3,7},{4,0},{5,1},{6,2},{7,3},{8,12},{9,13},{10,... | collective-permute-start | bytes 786440 | tf_op jit(solution)/shard_map/ppermute | solution.py:21
  16.7 4.1 %collective-permute-done.3.refs_2_ = bf16[512,256]{1,0:T(8,128)(2,1)S(1)} collective-permute-done((bf16[512,256]{1,0:T(8,128)(2,1)S(1)}, bf16[512,256]{1,0:T(8,128)(2,1)S(1)}, u32[]{:S(2)}, u32[]{:S(2)}) %collective-permute-start.3) | collective-permute-done | bytes 262176 | tf_op jit(solution)/shard_map/ppermute | solution.py:21
  22.1 5.4 %collective-permute-done.7.refs_1_ = bf16[512,256]{1,0:T(8,128)(2,1)S(1)} collective-permute-done((bf16[512,256]{1,0:T(8,128)(2,1)S(1)}, bf16[512,256]{1,0:T(8,128)(2,1)S(1)}, u32[]{:S(2)}, u32[]{:S(2)}) %collective-permute-start.7) | collective-permute-done | bytes 262176 | tf_op jit(solution)/shard_map/ppermute | solution.py:21
  30.4 3.5 %collective-permute-start.11 = (bf16[512,256]{1,0:T(8,128)(2,1)S(1)}, bf16[512,256]{1,0:T(8,128)(2,1)S(1)}, u32[]{:S(2)}, u32[]{:S(2)}) collective-permute-start(bf16[512,256]{1,0:T(8,128)(2,1)S(1)} %get-tuple-element.105), channel_id=1, source_target_pairs={{0,6},{1,7},{2,4},{3,5},{4,2},{5,3},{6,0},{7,1},{8,14},{9,15},{10,... | collective-permute-start | bytes 786440 | tf_op jit(solution)/shard_map/ppermute | solution.py:21
  37.4 4.2 %shard_map.194.refs_4_ = f32[2,128,5376]{2,1,0:T(8,128)S(1)} custom-call(s32[4]{0:T(128)S(1)} %copy-done.12, s32[4]{0:T(128)S(1)} %copy-done.13, f32[16,32]{1,0:T(8,128)S(1)} %bitcast.11, s32[1,4608]{1,0:T(1,128)S(1)} %broadcast_in_dim.6.bucket_ref), custom_call_target="tpu_custom_call" | custom-call | flops 11010048 | bytes 5505024 | tf_op jit(solution)/shard_map/pallas_call | solution.py:310
  41.7 9.6 %collective-permute-done.10.refs_7_.refs_2_ = bf16[512,256]{1,0:T(8,128)(2,1)S(1)} collective-permute-done((bf16[512,256]{1,0:T(8,128)(2,1)S(1)}, bf16[512,256]{1,0:T(8,128)(2,1)S(1)}, u32[]{:S(2)}, u32[]{:S(2)}) %collective-permute-start.10) | collective-permute-done | bytes 262176 | tf_op jit(solution)/shard_map/ppermute | solution.py:21
  54.8 2.7 %collective-permute-start.12 = (bf16[512,256]{1,0:T(8,128)(2,1)S(1)}, bf16[512,256]{1,0:T(8,128)(2,1)S(1)}, u32[]{:S(2)}, u32[]{:S(2)}) collective-permute-start(bf16[512,256]{1,0:T(8,128)(2,1)S(1)} %get-tuple-element.110), channel_id=1, source_target_pairs={{0,4},{1,5},{2,6},{3,7},{4,0},{5,1},{6,2},{7,3},{8,12},{9,13},{10,... | collective-permute-start | bytes 786440 | tf_op jit(solution)/shard_map/ppermute | solution.py:21
  57.5 2.6 %collective-permute-start.13 = (bf16[512,256]{1,0:T(8,128)(2,1)S(1)}, bf16[512,256]{1,0:T(8,128)(2,1)S(1)}, u32[]{:S(2)}, u32[]{:S(2)}) collective-permute-start(bf16[512,256]{1,0:T(8,128)(2,1)S(1)} %get-tuple-element.111), channel_id=1, source_target_pairs={{0,6},{1,7},{2,4},{3,5},{4,2},{5,3},{6,0},{7,1},{8,14},{9,15},{10,... | collective-permute-start | bytes 786440 | tf_op jit(solution)/shard_map/ppermute | solution.py:21
  61.8 4.6 %shard_map.196 = (f32[2,128,512]{2,1,0:T(8,128)S(1)}, f32[2,1,512]{2,1,0:T(1,128)S(1)}, f32[2,1,512]{2,1,0:T(1,128)S(1)}) custom-call(s32[4]{0:T(128)S(1)} %copy-done.12, s32[4]{0:T(128)S(1)} %copy-done.13, s32[4]{0:T(128)S(1)} %copy-done.14, bf16[2,128,512]{2,1,0:T(8,128)(2,1)S(1)} %get-tuple-element.101.refs_3_, f32[2,128,5376]{2,1,0:T(8,128)S(1)} %shard_map.194.refs_4_, ...), custom_call_target="tpu_custom_call" | custom-call | flops 1610612736 | bytes 7077888 | tf_op jit(solution)/shard_map/pallas_call | solution.py:437
  66.3 9.5 %collective-permute-done.12.refs_5_.refs_6_ = bf16[512,256]{1,0:T(8,128)(2,1)S(1)} collective-permute-done((bf16[512,256]{1,0:T(8,128)(2,1)S(1)}, bf16[512,256]{1,0:T(8,128)(2,1)S(1)}, u32[]{:S(2)}, u32[]{:S(2)}) %collective-permute-start.12) | collective-permute-done | bytes 262176 | tf_op jit(solution)/shard_map/ppermute | solution.py:21
  81.4 7.4 %collective-permute-start.19 = (bf16[64,1024]{1,0:T(8,128)(2,1)S(1)}, bf16[64,1024]{1,0:T(8,128)(2,1)S(1)}, u32[]{:S(2)}, u32[]{:S(2)}) collective-permute-start(bf16[64,1024]{1,0:T(8,128)(2,1)S(1)} %get-tuple-element.122), channel_id=1, source_target_pairs={{0,4},{1,5},{2,6},{3,7},{4,0},{5,1},{6,2},{7,3},{8,12},{9,13},{10,... | collective-permute-start | bytes 393224 | tf_op jit(solution)/shard_map/ppermute | solution.py:21
  89.9 8.9 %collective-permute-done.19.refs_3_ = bf16[64,1024]{1,0:T(8,128)(2,1)S(1)} collective-permute-done((bf16[64,1024]{1,0:T(8,128)(2,1)S(1)}, bf16[64,1024]{1,0:T(8,128)(2,1)S(1)}, u32[]{:S(2)}, u32[]{:S(2)}) %collective-permute-start.19) | collective-permute-done | bytes 131104 | tf_op jit(solution)/shard_map/ppermute | solution.py:21
  100.6 2.8 %collective-permute-start.36 = (bf16[1216,256]{1,0:T(8,128)(2,1)S(1)}, bf16[1216,256]{1,0:T(8,128)(2,1)S(1)}, u32[]{:S(2)}, u32[]{:S(2)}) collective-permute-start(bf16[1216,256]{1,0:T(8,128)(2,1)S(1)} %get-tuple-element.150.refs_2_), channel_id=1, source_target_pairs={{0,8},{8,0},{16,24},{24,16},{1,9},{9,1},{17,25},{25,17},{2,10},{10... | collective-permute-start | bytes 1867784 | tf_op jit(solution)/shard_map/ppermute | solution.py:21
  103.4 2.6 %collective-permute-start.35 = (bf16[1024,256]{1,0:T(8,128)(2,1)S(1)}, bf16[1024,256]{1,0:T(8,128)(2,1)S(1)}, u32[]{:S(2)}, u32[]{:S(2)}) collective-permute-start(bf16[1024,256]{1,0:T(8,128)(2,1)S(1)} %get-tuple-element.148.refs_0_), channel_id=1, source_target_pairs={{0,16},{8,24},{16,0},{24,8},{1,17},{9,25},{17,1},{25,9},{2,18},{10... | collective-permute-start | bytes 1572872 | tf_op jit(solution)/shard_map/ppermute | solution.py:21
  108.5 2.6 %collective-permute-start.27 = (bf16[64,256]{1,0:T(8,128)(2,1)S(1)}, bf16[64,256]{1,0:T(8,128)(2,1)S(1)}, u32[]{:S(2)}, u32[]{:S(2)}) collective-permute-start(bf16[64,256]{1,0:T(8,128)(2,1)S(1)} %get-tuple-element.134), channel_id=1, source_target_pairs={{0,6},{1,7},{2,4},{3,5},{4,2},{5,3},{6,0},{7,1},{8,14},{9,15},{10,... | collective-permute-start | bytes 98312 | tf_op jit(solution)/shard_map/ppermute | solution.py:21
  115.1 2.4 %shard_map.204 = (bf16[64,256]{1,0:T(8,128)(2,1)S(1)}, bf16[64,256]{1,0:T(8,128)(2,1)S(1)}, bf16[64,256]{1,0:T(8,128)(2,1)S(1)}, bf16[64,256]{1,0:T(8,128)(2,1)S(1)}) custom-call(s32[4]{0:T(128)S(1)} %copy-done.12, s32[4]{0:T(128)S(1)} %copy-done.15, bf16[64,256]{1,0:T(8,128)(2,1)S(1)} %get-tuple-element.132.refs_0_, ...), custom_call_target="tpu_custom_call" | custom-call | flops 268435456 | bytes 786464 | tf_op jit(solution)/shard_map/pallas_call | solution.py:52
  123.0 2.7 %collective-permute-done.31.refs_5_ = bf16[64,256]{1,0:T(8,128)(2,1)S(1)} collective-permute-done((bf16[64,256]{1,0:T(8,128)(2,1)S(1)}, bf16[64,256]{1,0:T(8,128)(2,1)S(1)}, u32[]{:S(2)}, u32[]{:S(2)}) %collective-permute-start.31) | collective-permute-done | bytes 32800 | tf_op jit(solution)/shard_map/ppermute | solution.py:21
  131.4 3.9 %collective-permute-done.34.refs_3_ = bf16[64,1024]{1,0:T(8,128)(2,1)S(1)} collective-permute-done((bf16[64,1024]{1,0:T(8,128)(2,1)S(1)}, bf16[64,1024]{1,0:T(8,128)(2,1)S(1)}, u32[]{:S(2)}, u32[]{:S(2)}) %collective-permute-start.34) | collective-permute-done | bytes 131104 | tf_op jit(solution)/shard_map/ppermute | solution.py:21
  135.3 4.6 %collective-permute-done.33.refs_2_ = bf16[64,1024]{1,0:T(8,128)(2,1)S(1)} collective-permute-done((bf16[64,1024]{1,0:T(8,128)(2,1)S(1)}, bf16[64,1024]{1,0:T(8,128)(2,1)S(1)}, u32[]{:S(2)}, u32[]{:S(2)}) %collective-permute-start.33) | collective-permute-done | bytes 131104 | tf_op jit(solution)/shard_map/ppermute | solution.py:21
  146.6 6.5 %collective-permute-done.39.refs_2_ = bf16[64,1024]{1,0:T(8,128)(2,1)S(1)} collective-permute-done((bf16[64,1024]{1,0:T(8,128)(2,1)S(1)}, bf16[64,1024]{1,0:T(8,128)(2,1)S(1)}, u32[]{:S(2)}, u32[]{:S(2)}) %collective-permute-start.39) | collective-permute-done | bytes 131104 | tf_op jit(solution)/shard_map/ppermute | solution.py:21
  158.9 3.7 %collective-permute-done.44.refs_3_ = bf16[64,1024]{1,0:T(8,128)(2,1)S(1)} collective-permute-done((bf16[64,1024]{1,0:T(8,128)(2,1)S(1)}, bf16[64,1024]{1,0:T(8,128)(2,1)S(1)}, u32[]{:S(2)}, u32[]{:S(2)}) %collective-permute-start.44) | collective-permute-done | bytes 131104 | tf_op jit(solution)/shard_map/ppermute | solution.py:21
  162.6 6.7 %collective-permute-done.43.refs_2_ = bf16[64,1024]{1,0:T(8,128)(2,1)S(1)} collective-permute-done((bf16[64,1024]{1,0:T(8,128)(2,1)S(1)}, bf16[64,1024]{1,0:T(8,128)(2,1)S(1)}, u32[]{:S(2)}, u32[]{:S(2)}) %collective-permute-start.43) | collective-permute-done | bytes 131104 | tf_op jit(solution)/shard_map/ppermute | solution.py:21
  (140 shorter events, 61.6 us)
Async XLA Ops:
  3.6 12.9 %collective-permute-start = (bf16[2048,256]{1,0:T(8,128)(2,1)S(1)}, bf16[2048,256]{1,0:T(8,128)(2,1)S(1)}, u32[]{:S(2)}, u32[]{:S(2)}) collective-permute-start(bf16[2048,256]{1,0:T(8,128)(2,1)S(1)} %get-tuple-element.83), channel_id=1, source_target_pairs={{0,1},{1,0},{2,3},{3,2},{4,5},{5,4},{6,7},{7,6},{8,9},{9,8},{10,11... | collective-permute-start | bytes 3145736 | tf_op jit(solution)/shard_map/ppermute | solution.py:21
  4.2 12.5 %collective-permute-start.2 = (bf16[512,256]{1,0:T(8,128)(2,1)S(1)}, bf16[512,256]{1,0:T(8,128)(2,1)S(1)}, u32[]{:S(2)}, u32[]{:S(2)}) collective-permute-start(bf16[512,256]{1,0:T(8,128)(2,1)S(1)} %get-tuple-element.88), channel_id=1, source_target_pairs={{0,8},{8,0},{16,24},{24,16},{1,9},{9,1},{17,25},{25,17},{2,10},{10... | collective-permute-start | bytes 786440 | tf_op jit(solution)/shard_map/ppermute | solution.py:21
  6.7 14.0 %collective-permute-start.3 = (bf16[512,256]{1,0:T(8,128)(2,1)S(1)}, bf16[512,256]{1,0:T(8,128)(2,1)S(1)}, u32[]{:S(2)}, u32[]{:S(2)}) collective-permute-start(bf16[512,256]{1,0:T(8,128)(2,1)S(1)} %get-tuple-element.89), channel_id=1, source_target_pairs={{0,16},{8,24},{16,0},{24,8},{1,17},{9,25},{17,1},{25,9},{2,18},{10... | collective-permute-start | bytes 786440 | tf_op jit(solution)/shard_map/ppermute | solution.py:21
  8.2 12.5 %collective-permute-start.4 = (bf16[512,256]{1,0:T(8,128)(2,1)S(1)}, bf16[512,256]{1,0:T(8,128)(2,1)S(1)}, u32[]{:S(2)}, u32[]{:S(2)}) collective-permute-start(bf16[512,256]{1,0:T(8,128)(2,1)S(1)} %get-tuple-element.90), channel_id=1, source_target_pairs={{0,24},{8,16},{16,8},{24,0},{1,25},{9,17},{17,9},{25,1},{2,26},{10... | collective-permute-start | bytes 786440 | tf_op jit(solution)/shard_map/ppermute | solution.py:21
  13.7 13.8 %collective-permute-start.7 = (bf16[512,256]{1,0:T(8,128)(2,1)S(1)}, bf16[512,256]{1,0:T(8,128)(2,1)S(1)}, u32[]{:S(2)}, u32[]{:S(2)}) collective-permute-start(bf16[512,256]{1,0:T(8,128)(2,1)S(1)} %shard_map.189.refs_0_), channel_id=1, source_target_pairs={{0,4},{1,5},{2,6},{3,7},{4,0},{5,1},{6,2},{7,3},{8,12},{9,13},{10,... | collective-permute-start | bytes 786440 | tf_op jit(solution)/shard_map/ppermute | solution.py:21
  20.8 14.9 %collective-permute-start.5 = (bf16[1024,256]{1,0:T(8,128)(2,1)S(1)}, bf16[1024,256]{1,0:T(8,128)(2,1)S(1)}, u32[]{:S(2)}, u32[]{:S(2)}) collective-permute-start(bf16[1024,256]{1,0:T(8,128)(2,1)S(1)} %get-tuple-element.92), channel_id=1, source_target_pairs={{0,8},{8,0},{16,24},{24,16},{1,9},{9,1},{17,25},{25,17},{2,10},{10... | collective-permute-start | bytes 1572872 | tf_op jit(solution)/shard_map/ppermute | solution.py:21
  27.5 24.2 %collective-permute-start.6 = (bf16[1024,256]{1,0:T(8,128)(2,1)S(1)}, bf16[1024,256]{1,0:T(8,128)(2,1)S(1)}, u32[]{:S(2)}, u32[]{:S(2)}) collective-permute-start(bf16[1024,256]{1,0:T(8,128)(2,1)S(1)} %get-tuple-element.94), channel_id=1, source_target_pairs={{0,16},{8,24},{16,0},{24,8},{1,17},{9,25},{17,1},{25,9},{2,18},{10... | collective-permute-start | bytes 1572872 | tf_op jit(solution)/shard_map/ppermute | solution.py:21
  29.0 22.8 %collective-permute-start.8 = (bf16[1024,256]{1,0:T(8,128)(2,1)S(1)}, bf16[1024,256]{1,0:T(8,128)(2,1)S(1)}, u32[]{:S(2)}, u32[]{:S(2)}) collective-permute-start(bf16[1024,256]{1,0:T(8,128)(2,1)S(1)} %get-tuple-element.96), channel_id=1, source_target_pairs={{0,24},{8,16},{16,8},{24,0},{1,25},{9,17},{17,9},{25,1},{2,26},{10... | collective-permute-start | bytes 1572872 | tf_op jit(solution)/shard_map/ppermute | solution.py:21
  30.4 20.9 %collective-permute-start.10 = (bf16[512,256]{1,0:T(8,128)(2,1)S(1)}, bf16[512,256]{1,0:T(8,128)(2,1)S(1)}, u32[]{:S(2)}, u32[]{:S(2)}) collective-permute-start(bf16[512,256]{1,0:T(8,128)(2,1)S(1)} %get-tuple-element.104), channel_id=1, source_target_pairs={{0,4},{1,5},{2,6},{3,7},{4,0},{5,1},{6,2},{7,3},{8,12},{9,13},{10,... | collective-permute-start | bytes 786440 | tf_op jit(solution)/shard_map/ppermute | solution.py:21
  30.4 20.9 %collective-permute-start.11 = (bf16[512,256]{1,0:T(8,128)(2,1)S(1)}, bf16[512,256]{1,0:T(8,128)(2,1)S(1)}, u32[]{:S(2)}, u32[]{:S(2)}) collective-permute-start(bf16[512,256]{1,0:T(8,128)(2,1)S(1)} %get-tuple-element.105), channel_id=1, source_target_pairs={{0,6},{1,7},{2,4},{3,5},{4,2},{5,3},{6,0},{7,1},{8,14},{9,15},{10,... | collective-permute-start | bytes 786440 | tf_op jit(solution)/shard_map/ppermute | solution.py:21
  35.7 15.5 %collective-permute-start.9 = (bf16[512,256]{1,0:T(8,128)(2,1)S(1)}, bf16[512,256]{1,0:T(8,128)(2,1)S(1)}, u32[]{:S(2)}, u32[]{:S(2)}) collective-permute-start(bf16[512,256]{1,0:T(8,128)(2,1)S(1)} %get-tuple-element.103), channel_id=1, source_target_pairs={{0,2},{1,3},{2,0},{3,1},{4,6},{5,7},{6,4},{7,5},{8,10},{9,11},{10,... | collective-permute-start | bytes 786440 | tf_op jit(solution)/shard_map/ppermute | solution.py:21
  52.0 24.0 %collective-permute-start.15 = (bf16[1280,256]{1,0:T(8,128)(2,1)S(1)}, bf16[1280,256]{1,0:T(8,128)(2,1)S(1)}, u32[]{:S(2)}, u32[]{:S(2)}) collective-permute-start(bf16[1280,256]{1,0:T(8,128)(2,1)S(1)} %get-tuple-element.114.refs_0_), channel_id=1, source_target_pairs={{0,8},{8,0},{16,24},{24,16},{1,9},{9,1},{17,25},{25,17},{2,10},{10... | collective-permute-start | bytes 1966088 | tf_op jit(solution)/shard_map/ppermute | solution.py:21
  53.3 22.7 %collective-permute-start.16 = (bf16[1120,256]{1,0:T(8,128)(2,1)S(1)}, bf16[1120,256]{1,0:T(8,128)(2,1)S(1)}, u32[]{:S(2)}, u32[]{:S(2)}) collective-permute-start(bf16[1120,256]{1,0:T(8,128)(2,1)S(1)} %get-tuple-element.116.refs_2_), channel_id=1, source_target_pairs={{0,16},{8,24},{16,0},{24,8},{1,17},{9,25},{17,1},{25,9},{2,18},{10... | collective-permute-start | bytes 1720328 | tf_op jit(solution)/shard_map/ppermute | solution.py:21
  54.8 21.1 %collective-permute-start.12 = (bf16[512,256]{1,0:T(8,128)(2,1)S(1)}, bf16[512,256]{1,0:T(8,128)(2,1)S(1)}, u32[]{:S(2)}, u32[]{:S(2)}) collective-permute-start(bf16[512,256]{1,0:T(8,128)(2,1)S(1)} %get-tuple-element.110), channel_id=1, source_target_pairs={{0,4},{1,5},{2,6},{3,7},{4,0},{5,1},{6,2},{7,3},{8,12},{9,13},{10,... | collective-permute-start | bytes 786440 | tf_op jit(solution)/shard_map/ppermute | solution.py:21
  57.5 18.4 %collective-permute-start.13 = (bf16[512,256]{1,0:T(8,128)(2,1)S(1)}, bf16[512,256]{1,0:T(8,128)(2,1)S(1)}, u32[]{:S(2)}, u32[]{:S(2)}) collective-permute-start(bf16[512,256]{1,0:T(8,128)(2,1)S(1)} %get-tuple-element.111), channel_id=1, source_target_pairs={{0,6},{1,7},{2,4},{3,5},{4,2},{5,3},{6,0},{7,1},{8,14},{9,15},{10,... | collective-permute-start | bytes 786440 | tf_op jit(solution)/shard_map/ppermute | solution.py:21
  60.1 15.9 %collective-permute-start.14 = (bf16[512,256]{1,0:T(8,128)(2,1)S(1)}, bf16[512,256]{1,0:T(8,128)(2,1)S(1)}, u32[]{:S(2)}, u32[]{:S(2)}) collective-permute-start(bf16[512,256]{1,0:T(8,128)(2,1)S(1)} %get-tuple-element.112), channel_id=1, source_target_pairs={{0,2},{1,3},{2,0},{3,1},{4,6},{5,7},{6,4},{7,5},{8,10},{9,11},{10,... | collective-permute-start | bytes 786440 | tf_op jit(solution)/shard_map/ppermute | solution.py:21
  76.2 23.6 %collective-permute-start.22 = (bf16[1536,256]{1,0:T(8,128)(2,1)S(1)}, bf16[1536,256]{1,0:T(8,128)(2,1)S(1)}, u32[]{:S(2)}, u32[]{:S(2)}) collective-permute-start(bf16[1536,256]{1,0:T(8,128)(2,1)S(1)} %get-tuple-element.125.refs_0_), channel_id=1, source_target_pairs={{0,16},{8,24},{16,0},{24,8},{1,17},{9,25},{17,1},{25,9},{2,18},{10... | collective-permute-start | bytes 2359304 | tf_op jit(solution)/shard_map/ppermute | solution.py:21
  77.1 22.8 %collective-permute-start.23 = (bf16[1024,256]{1,0:T(8,128)(2,1)S(1)}, bf16[1024,256]{1,0:T(8,128)(2,1)S(1)}, u32[]{:S(2)}, u32[]{:S(2)}) collective-permute-start(bf16[1024,256]{1,0:T(8,128)(2,1)S(1)} %get-tuple-element.126.refs_2_), channel_id=1, source_target_pairs={{0,8},{8,0},{16,24},{24,16},{1,9},{9,1},{17,25},{25,17},{2,10},{10... | collective-permute-start | bytes 1572872 | tf_op jit(solution)/shard_map/ppermute | solution.py:21
  81.4 17.4 %collective-permute-start.19 = (bf16[64,1024]{1,0:T(8,128)(2,1)S(1)}, bf16[64,1024]{1,0:T(8,128)(2,1)S(1)}, u32[]{:S(2)}, u32[]{:S(2)}) collective-permute-start(bf16[64,1024]{1,0:T(8,128)(2,1)S(1)} %get-tuple-element.122), channel_id=1, source_target_pairs={{0,4},{1,5},{2,6},{3,7},{4,0},{5,1},{6,2},{7,3},{8,12},{9,13},{10,... | collective-permute-start | bytes 393224 | tf_op jit(solution)/shard_map/ppermute | solution.py:21
  100.6 25.6 %collective-permute-start.36 = (bf16[1216,256]{1,0:T(8,128)(2,1)S(1)}, bf16[1216,256]{1,0:T(8,128)(2,1)S(1)}, u32[]{:S(2)}, u32[]{:S(2)}) collective-permute-start(bf16[1216,256]{1,0:T(8,128)(2,1)S(1)} %get-tuple-element.150.refs_2_), channel_id=1, source_target_pairs={{0,8},{8,0},{16,24},{24,16},{1,9},{9,1},{17,25},{25,17},{2,10},{10... | collective-permute-start | bytes 1867784 | tf_op jit(solution)/shard_map/ppermute | solution.py:21
  103.4 22.8 %collective-permute-start.35 = (bf16[1024,256]{1,0:T(8,128)(2,1)S(1)}, bf16[1024,256]{1,0:T(8,128)(2,1)S(1)}, u32[]{:S(2)}, u32[]{:S(2)}) collective-permute-start(bf16[1024,256]{1,0:T(8,128)(2,1)S(1)} %get-tuple-element.148.refs_0_), channel_id=1, source_target_pairs={{0,16},{8,24},{16,0},{24,8},{1,17},{9,25},{17,1},{25,9},{2,18},{10... | collective-permute-start | bytes 1572872 | tf_op jit(solution)/shard_map/ppermute | solution.py:21
  126.4 13.5 %collective-permute-start.38 = (bf16[2432,256]{1,0:T(8,128)(2,1)S(1)}, bf16[2432,256]{1,0:T(8,128)(2,1)S(1)}, u32[]{:S(2)}, u32[]{:S(2)}) collective-permute-start(bf16[2432,256]{1,0:T(8,128)(2,1)S(1)} %get-tuple-element.152.refs_6_), channel_id=1, source_target_pairs={{0,1},{1,0},{2,3},{3,2},{4,5},{5,4},{6,7},{7,6},{8,9},{9,8},{10,11... | collective-permute-start | bytes 3735560 | tf_op jit(solution)/shard_map/ppermute | solution.py:21
  126.5 13.4 %collective-permute-start.37 = (bf16[2048,256]{1,0:T(8,128)(2,1)S(1)}, bf16[2048,256]{1,0:T(8,128)(2,1)S(1)}, u32[]{:S(2)}, u32[]{:S(2)}) collective-permute-start(bf16[2048,256]{1,0:T(8,128)(2,1)S(1)} %get-tuple-element.151.refs_4_), channel_id=1, source_target_pairs={{0,1},{1,0},{2,3},{3,2},{4,5},{5,4},{6,7},{7,6},{8,9},{9,8},{10,11... | collective-permute-start | bytes 3145736 | tf_op jit(solution)/shard_map/ppermute | solution.py:21
  156.4 12.9 %collective-permute-start.43 = (bf16[64,1024]{1,0:T(8,128)(2,1)S(1)}, bf16[64,1024]{1,0:T(8,128)(2,1)S(1)}, u32[]{:S(2)}, u32[]{:S(2)}) collective-permute-start(bf16[64,1024]{1,0:T(8,128)(2,1)S(1)} %shard_map.208.refs_0_), channel_id=1, source_target_pairs={{0,4},{1,5},{2,6},{3,7},{4,0},{5,1},{6,2},{7,3},{8,12},{9,13},{10,... | collective-permute-start | bytes 393224 | tf_op jit(solution)/shard_map/ppermute | solution.py:21
  (44 other events, 371.3 us)
